TPU v7x, 32 devices: a whole 2x2x4 slice. The times are simulated.
32 devices in a mesh: dp: 16 (over z, y, x), rep: 2 (over core).
Axes of the slice: x: 2, y: 2, z: 4, core: 2. Of those that a mesh axis runs over, the one named last changes fastest.
Arguments:
- language_in: bfloat16 [64, 128, 768], P(('dp', 'rep')), may hold values from -6 to 6
- vision_in: bfloat16 [64, 128, 768], P(('dp', 'rep')), may hold values from -6 to 6
- language_count: int32 [64], P(('dp', 'rep')), may hold values from 5 to 128, as said below
- vision_count: int32 [64], P(('dp', 'rep')), may hold values from 5 to 128, as said below
- cross_qkv: bfloat16 [2, 3, 768, 768], P(None, None, 'dp'), may hold values from -0.21875 to 0.21875
- cross_proj: bfloat16 [2, 768, 768], P(None, 'dp'), may hold values from -1.25 to 1.25
- cross_bias: bfloat16 [2, 3, 768], P(None, None, 'dp'), may hold values from -4 to 4
- norm_gain: bfloat16 [2, 3, 768], P(None, None, 'dp'), may hold values from 0.5 to 1.5
- norm_bias: bfloat16 [2, 3, 768], P(None, None, 'dp'), may hold values from -4 to 4
- self_qkv: bfloat16 [2, 3, 768, 768], P(None, None, 'dp'), may hold values from -0.21875 to 0.21875
- self_proj: bfloat16 [2, 768, 768], P(None, 'dp'), may hold values from -1.25 to 1.25
- self_bias: bfloat16 [2, 3, 768], P(None, None, 'dp'), may hold values from -4 to 4
- ffn_in: bfloat16 [2, 768, 3072], P(None, 'dp'), may hold values from -0.21875 to 0.21875
- ffn_in_bias: bfloat16 [2, 3072], P(None, 'dp'), may hold values from -4 to 4
- ffn_out: bfloat16 [2, 3072, 768], P(None, 'dp'), may hold values from -0.109375 to 0.109375
- ffn_out_bias: bfloat16 [2, 768], P(None, 'dp'), may hold values from -4 to 4
- gate_weight: bfloat16 [2, 768, 768], P(None, 'dp'), may hold values from -0.15625 to 0.15625
- gate_bias: bfloat16 [768], P('dp'), may hold values from -6 to 6
- cotangent: bfloat16 [64, 128, 768], P(('dp', 'rep')), may hold values from -6 to 6
Outputs:
- united: bfloat16 [64, 128, 768], P(('dp', 'rep'))
- grad_language: bfloat16 [64, 128, 768], P(('dp', 'rep'))
- grad_vision: bfloat16 [64, 128, 768], P(('dp', 'rep'))
- grad_cross_qkv: float32 [2, 3, 768, 768], P(None, None, 'dp')
- grad_cross_proj: float32 [2, 768, 768], P(None, 'dp')
- grad_cross_bias: float32 [2, 3, 768], P(None, None, 'dp')
- grad_norm_gain: float32 [2, 3, 768], P(None, None, 'dp')
- grad_norm_bias: float32 [2, 3, 768], P(None, None, 'dp')
- grad_self_qkv: float32 [2, 3, 768, 768], P(None, None, 'dp')
- grad_self_proj: float32 [2, 768, 768], P(None, 'dp')
- grad_self_bias: float32 [2, 3, 768], P(None, None, 'dp')
- grad_ffn_in: float32 [2, 768, 3072], P(None, 'dp')
- grad_ffn_in_bias: float32 [2, 3072], P(None, 'dp')
- grad_ffn_out: float32 [2, 3072, 768], P(None, 'dp')
- grad_ffn_out_bias: float32 [2, 768], P(None, 'dp')
- grad_gate_weight: float32 [2, 768, 768], P(None, 'dp')
- grad_gate_bias: float32 [768], P('dp')
Inputs may be any that keep to these rules, and one draw needn't show every extreme that they name: The real language regions of a page are its first language_count slots. The real vision regions of a page are its first vision_count slots.
All inputs are finite; a program needn't handle non-finite values.
Results may differ from a plain program's by a relative error of at most 0.024.
Values may be sent and summed in bfloat16 or wider, within the bound.
No kernel may reach another device: no remote copies, remote signals or barrier semaphores. Data moves between devices by JAX's collectives and lax.ppermute only.
A program may use at most 256 MiB of HBM per device.

v0:
```python
import functools

import jax
import jax.numpy as jnp
from jax import lax
from jax.experimental import pallas as pl
from jax.experimental.pallas import tpu as pltpu
from jax.sharding import PartitionSpec as P

HEADS = 12
HEAD = 64
norm_epsilon = 1e-05
bf16 = jnp.bfloat16
f32 = jnp.float32
AXES = ("dp", "rep")
VMEM_LIMIT = 32 << 20
GLUE_LIMIT = 20 << 20
HBM = pl.BlockSpec(memory_space=pltpu.HBM)
VMEM = pl.BlockSpec(memory_space=pltpu.VMEM)
SMEM = pl.BlockSpec(memory_space=pltpu.SMEM)


class Grid:
    def __init__(self, mesh):
        self.n = mesh.shape["dp"]
        self.r = mesh.shape["rep"]
        self.high = self.n >> 1
        self.partner = self.n >> 2
        self.groups = [0, self.partner, self.high, self.high | self.partner]
        low = []
        bit = 1
        while bit < self.partner:
            low.append(bit)
            bit *= 2
        self.orders = [low, low[::-1]]
        self.high_bit = len(low) + 1

    def across(self, values, mask):
        pairs = [
            (d * self.r + c, (d ^ mask) * self.r + c) for d in range(self.n) for c in range(self.r)
        ]
        return lax.ppermute(values, AXES, pairs)

    def swap_cores(self, values):
        pairs = [
            (d * self.r + c, d * self.r + (c ^ 1)) for d in range(self.n) for c in range(self.r)
        ]
        return lax.ppermute(values, AXES, pairs)

    def hop(self, values, step):
        pairs = []
        for d in range(self.n):
            for c in range(self.r):
                mask = self.orders[c % 2][step]
                pairs.append((d * self.r + c, (d ^ mask) * self.r + c))
        return lax.ppermute(values, AXES, pairs)

    def place(self, info):
        core, me = info[1], info[2]
        first = jnp.right_shift(me, core) & 1
        second = jnp.right_shift(me, 1 - core) & 1
        return jnp.right_shift(me, 2), first, second, 1 + core, 2 - core

    def masks(self, core):
        found = [0]
        for low, high in zip(*self.orders, strict=True):
            bit = low + core * (high - low)
            found = found + [m ^ bit for m in found]
        return found


def call(kernel, outs, ins, specs, out_specs, scratch=(), flops=0, moved=0, room=VMEM_LIMIT):
    results = pl.pallas_call(
        kernel,
        out_shape=[jax.ShapeDtypeStruct(shape, dtype) for shape, dtype in outs],
        in_specs=specs,
        out_specs=out_specs,
        scratch_shapes=list(scratch),
        compiler_params=pltpu.CompilerParams(vmem_limit_bytes=room),
        cost_estimate=pl.CostEstimate(flops=flops, bytes_accessed=moved, transcendentals=0),
    )(*ins)
    return list(results)


def pair_kernel(bit_of, info_ref, *refs):
    mine, other = refs[:2]
    bit = jnp.right_shift(info_ref[2], bit_of) & 1
    start = 0
    for out in refs[2:]:
        end = start + out.shape[-2]
        out[bit] = mine[..., start:end, :]
        out[1 - bit] = other[..., start:end, :]
        start = end


def pair(info, bit_of, mine, other, parts=None):
    shape = mine.shape
    parts = [shape[-2]] if parts is None else parts
    if shape[-2] % 16:
        bit = jnp.right_shift(info[2], bit_of) & 1
        both = jnp.where(bit == 0, jnp.stack([mine, other]), jnp.stack([other, mine]))
        starts = [sum(parts[:i]) for i in range(len(parts))]
        return [both[..., s : s + p, :] for s, p in zip(starts, parts, strict=True)]
    return call(
        functools.partial(pair_kernel, bit_of),
        [((2,) + shape[:-2] + (part, shape[-1]), bf16) for part in parts],
        [info, mine, other],
        [SMEM, VMEM, VMEM],
        [VMEM] * len(parts),
        room=GLUE_LIMIT,
    )


def group_kernel(high_bit, info_ref, *refs):
    group = jnp.right_shift(info_ref[2], high_bit - 1)
    for k, source in enumerate(refs[:4]):
        refs[4][jnp.bitwise_xor(group, k)] = source[...]


def all_meet(grid, info, mine, theirs):
    return [
        mine,
        grid.across(theirs, grid.groups[1]),
        grid.across(theirs, grid.groups[2]),
        grid.across(mine, grid.groups[3]),
    ]


def grouped(grid, info, sources):
    shape = sources[0].shape
    if shape[0] % 16:
        group = jnp.right_shift(info[2], grid.high_bit - 1)
        return jnp.take(jnp.stack(sources), jnp.arange(4) ^ group, axis=0)
    return call(
        functools.partial(group_kernel, grid.high_bit),
        [((4,) + shape, bf16)],
        [info] + sources,
        [SMEM] + [VMEM] * 4,
        [VMEM],
        room=GLUE_LIMIT,
    )[0]


def join_kernel(grid, info_ref, mine, other, out):
    bit = grid.place(info_ref)[1]
    for g in range(4):
        out[g, bit] = mine[g]
        out[g, 1 - bit] = other[g]


def join_pair(grid, info, pieces):
    shape = pieces[0].shape
    return call(
        functools.partial(join_kernel, grid),
        [((4, 2) + shape[1:], bf16)],
        [info] + pieces,
        [SMEM] + [VMEM] * 2,
        [VMEM],
        room=GLUE_LIMIT,
    )[0]


def tie(*values):
    flat, tree = jax.tree.flatten(values)
    return jax.tree.unflatten(tree, lax.optimization_barrier(flat))


def meet(grid, info, held):
    rows, width = held.shape[1:]
    received = grid.across(held, grid.groups[3])

    def place(received):
        return pair(info, grid.high_bit, held, received)[0].reshape(4, rows, width)

    return received, place


def second_hops(grid, held):
    if len(grid.orders[0]) == 2:
        return [held, grid.hop(held, 0)]
    for step in range(len(grid.orders[0])):
        held = jnp.concatenate([held, grid.hop(held, step)], 0)
    return [held]


def third_hops(grid, info, pieces):
    if len(pieces) == 1:
        return pieces
    held = join_pair(grid, info, pieces)
    return [held, grid.hop(held, 1), grid.swap_cores(held)]


def extra_rows(grid, info, pieces, start, keep):
    held = pieces[0][:, start : start + keep]
    return jnp.take(held, jnp.argsort(slots_of(grid, info)), axis=0)


def slots_of(grid, info):
    masks = jnp.stack(grid.masks(info[1])).astype(jnp.int32)[:, None]
    groups = jnp.arange(4, dtype=jnp.int32)[None, :] * grid.partner
    return ((masks ^ (info[2] & (grid.partner - 1))) | groups).reshape(-1)


def whole(grid, info, pieces, rows, count):
    if len(pieces) == 3:
        return [pieces[0], pieces[1], pieces[2], grid.swap_cores(pieces[1])]
    held = pieces[0][:, : count * rows]
    held = jnp.take(held, jnp.argsort(slots_of(grid, info)), axis=0).reshape(grid.n, count, rows, -1).transpose(1, 0, 2, 3)
    held = held.reshape(count, grid.n * rows, -1)
    return [held, grid.swap_cores(held)]


def split_kernel(grid, extra, info_ref, keep, received, *refs):
    outs = refs[-2:]
    count, rows = keep.shape[0], keep.shape[2]
    unused, unused, second, first_step, second_step = grid.place(info_ref)
    for g in range(4):
        for a in range(2):
            for b, out in ((second, outs[0]), (1 - second, outs[1])):
                source = 4 * g + a * first_step + b * second_step
                for j in range(count):
                    total = keep[j, source].astype(f32) + received[j, source].astype(f32)
                    out[g, a, j * rows : (j + 1) * rows] = total.astype(bf16)
                if extra:
                    out[g, a, count * rows :] = refs[0][source]


def added(a, b):
    return (a.astype(f32) + b.astype(f32)).astype(bf16)


def first_returns(grid, info, keep, received, more=None):
    blocks, n, rows, width = keep.shape
    depth = blocks * rows + (0 if more is None else more.shape[1])
    extra = [] if more is None else [more]
    if len(grid.orders[0]) != 2:
        total = added(keep, received).transpose(1, 0, 2, 3).reshape(n, blocks * rows, width)
        total = jnp.concatenate([total] + extra, 1)
        held = jnp.take(total, slots_of(grid, info), axis=0)
        for step in reversed(range(len(grid.orders[0]))):
            half = held.shape[0] // 2
            held = added(held[:half], grid.hop(held[half:], step))
        return [held]
    held, sent = call(
        functools.partial(split_kernel, grid, len(extra)),
        [((4, 2, depth, width), bf16)] * 2,
        [info, keep, received] + extra,
        [SMEM, VMEM, VMEM] + [VMEM] * len(extra),
        [VMEM] * 2,
        room=GLUE_LIMIT,
    )
    return [held, grid.hop(sent, 1)]


def merge_kernel(grid, info_ref, *refs):
    near, far = refs[-2:]
    bit = grid.place(info_ref)[1]
    start = 0
    for held, received in zip(refs[:-2:2], refs[1:-2:2], strict=True):
        at = slice(start, start + held.shape[2])
        for g in range(4):
            for which, out in ((bit, near), (1 - bit, far)):
                out[g, at] = added(held[g, which], received[g, which])
        start += held.shape[2]


def second_returns(grid, info, *parts):
    if len(parts[0]) == 1:
        return [jnp.concatenate([part[0] for part in parts], 1)]
    depth = sum(part[0].shape[2] for part in parts)
    near, far = call(
        functools.partial(merge_kernel, grid),
        [((4, depth, parts[0][0].shape[3]), bf16)] * 2,
        [info] + [array for part in parts for array in part],
        [SMEM] + [VMEM] * (2 * len(parts)),
        [VMEM] * 2,
        room=GLUE_LIMIT,
    )
    return [near, grid.hop(far, 0)]


def collect_kernel(grid, info_ref, held, received, *outs):
    group = grid.place(info_ref)[0]
    for k, out in enumerate(outs):
        at = jnp.bitwise_xor(group, k)
        out[...] = added(held[at], received[at])


def third_returns(grid, info, pieces):
    if len(pieces) == 1:
        group = jnp.right_shift(info[2], grid.high_bit - 1)
        totals = [
            lax.dynamic_index_in_dim(pieces[0], group ^ g, 0, keepdims=False) for g in range(4)
        ]
    else:
        totals = call(
            functools.partial(collect_kernel, grid),
            [(pieces[0].shape[1:], bf16)] * 4,
            [info] + pieces,
            [SMEM] + [VMEM] * 2,
            [VMEM] * 4,
            room=GLUE_LIMIT,
        )
    return [totals[0]] + [grid.across(totals[g], grid.groups[g]) for g in (3, 1, 2)]


def last_kernel(near_a, near_b, far_a, far_b, out):
    out[0] = (near_a[...].astype(f32) + near_b[...].astype(f32)).astype(bf16)
    out[1] = (far_a[...].astype(f32) + far_b[...].astype(f32)).astype(bf16)


def last_swap(grid, terms):
    mine = call(
        last_kernel,
        [((2,) + terms[0].shape, bf16)],
        terms,
        [VMEM] * 4,
        [VMEM],
        room=GLUE_LIMIT,
    )[0]
    return mine, grid.swap_cores(mine)


def finish_kernel(layout, rows, info_ref, mine_ref, far_ref, *outs):
    side, core = info_ref[0], info_ref[1]

    def write(which, ref):
        for j, (out, at) in enumerate(layout[which]):
            for k in range(2):
                value = ref[k, j * rows : (j + 1) * rows].astype(f32)
                outs[out][(jnp.bitwise_xor(side, k),) + at] = value

    for which in range(2):
        pl.when(core == which)(functools.partial(write, which, mine_ref))
        pl.when(core != which)(functools.partial(write, which, far_ref))


def finish(info, done, layout, rows, shapes):
    return call(
        functools.partial(finish_kernel, layout, rows),
        [(shape, f32) for shape in shapes],
        [info] + list(done),
        [SMEM, VMEM, VMEM],
        [VMEM] * len(shapes),
        room=GLUE_LIMIT,
    )


def finish_gate_kernel(info_ref, mine_ref, far_ref, out):
    side, core = info_ref[0], info_ref[1]
    rows = out.shape[1]

    def write(own_ref, other_ref):
        for k in range(2):
            own = own_ref[k, :rows].astype(f32)
            out[jnp.bitwise_xor(side, k)] = own + other_ref[1 - k, :rows].astype(f32)

    pl.when(core == 0)(functools.partial(write, mine_ref, far_ref))
    pl.when(core != 0)(functools.partial(write, far_ref, mine_ref))


def nn(a, b):
    return lax.dot_general(a, b, (((1,), (0,)), ((), ())), preferred_element_type=f32)


def nt(a, b):
    return lax.dot_general(a, b, (((1,), (1,)), ((), ())), preferred_element_type=f32)


def tn(a, b):
    return lax.dot_general(a, b, (((0,), (0,)), ((), ())), preferred_element_type=f32)


def block_shapes(grid, count, rows, width, mixed=False):
    if rows % 16 or len(grid.orders[0]) != 2:
        return (4 * grid.n * rows, width) if mixed else (count, grid.n * rows, width)
    inner = (4, rows, width) if mixed else (rows, width)
    return ((4, 2, 2) if mixed else (count, 4, 2, 2)) + inner


def load_blocks(grid, info_ref, sources, blocks, sem, start=0, only=None, mixed=False):
    core = info_ref[1]
    middle = len(sources) // 2

    def load(which, refs):
        count = 1 if only is not None else 2 if mixed else blocks.shape[0] // 2
        first = 0 if only is not None else which * count
        if len(refs) == 1:
            for j in range(count):
                pltpu.make_async_copy(refs[0].at[start + j], blocks.at[first + j], sem).start()
            return
        rows = blocks.shape[-2]
        bit = jnp.right_shift(info_ref[2], 1 - which) & 1
        for j in range(count):
            for ref, b in ((refs[0], bit), (refs[1], 1 - bit)):
                source = ref.at[:, :, pl.ds((start + j) * rows, rows)]

                def low_first(b=b, j=j, source=source):
                    target = blocks.at[:, b, :, first + j] if mixed else blocks.at[first + j, :, b]
                    pltpu.make_async_copy(source, target, sem).start()

                def high_first(b=b, j=j, source=source):
                    target = (
                        blocks.at[:, :, b, first + j] if mixed else blocks.at[first + j, :, :, b]
                    )
                    pltpu.make_async_copy(source, target, sem).start()

                pl.when(which == 0)(low_first)
                pl.when(which != 0)(high_first)

    if len(sources) == 1:
        pltpu.make_async_copy(sources[0], blocks, sem).start()
    elif only is None:
        load(core, sources[:middle])
        load(1 - core, sources[middle:])
    else:
        pl.when(core == only)(lambda: load(only, sources[:middle]))
        pl.when(core != only)(lambda: load(only, sources[middle:]))
    return pltpu.make_async_copy(blocks, blocks, sem).wait


def matrix(values):
    return values.reshape(-1, values.shape[-1])


def load_inputs(info_ref, language, vision, both_far, src_ref, oth_ref, sem):
    half = language.shape[0]

    def copies(mine, mine_at, other, other_at):
        return [
            pltpu.make_async_copy(mine, src_ref.at[pl.ds(0, half)], sem.at[0]),
            pltpu.make_async_copy(
                both_far.at[pl.ds(mine_at, half)], src_ref.at[pl.ds(half, half)], sem.at[1]
            ),
            pltpu.make_async_copy(other, oth_ref.at[pl.ds(0, half)], sem.at[2]),
            pltpu.make_async_copy(
                both_far.at[pl.ds(other_at, half)], oth_ref.at[pl.ds(half, half)], sem.at[3]
            ),
        ]

    @pl.when(info_ref[0] == 0)
    def _():
        for copy in copies(language, 0, vision, half):
            copy.start()

    @pl.when(info_ref[0] != 0)
    def _():
        for copy in copies(vision, half, language, 0):
            copy.start()

    def wait():
        for copy in copies(language, 0, vision, half):
            copy.wait()

    return wait


def store_blocks(core, blocks, keep, send, sem):
    count = keep.shape[0]
    copies = []
    for j in range(count):
        copies.append(pltpu.make_async_copy(blocks.at[core * count + j], keep.at[j], sem.at[j]))
        copies.append(
            pltpu.make_async_copy(
                blocks.at[(1 - core) * count + j], send.at[j], sem.at[count + j]
            )
        )
    for copy in copies:
        copy.start()

    def wait():
        for copy in copies:
            copy.wait()

    return wait


def normalised(values):
    mean_row = jnp.mean(values, axis=-1, keepdims=True)
    centred = values - mean_row
    variance = jnp.mean(centred * centred, axis=-1, keepdims=True)
    scale = lax.rsqrt(variance + norm_epsilon)
    return centred * scale, scale


def norm_back(values, grads, gain):
    unit, scale = normalised(values)
    scaled = grads * gain
    first = jnp.mean(scaled, axis=-1, keepdims=True)
    second = jnp.mean(scaled * unit, axis=-1, keepdims=True)
    return (scaled - first - unit * second) * scale, grads * unit


def lane_masks():
    lanes = lax.broadcasted_iota(jnp.int32, (128, 2 * HEAD), 1)
    left = (lanes < HEAD).astype(f32).astype(bf16)
    right = (lanes >= HEAD).astype(f32).astype(bf16)
    return lanes < HEAD, left, right


def two_heads(values, left, right):
    return jnp.concatenate([values * left, values * right], 0)


def softened(queries, keys_both, barred):
    scores = []
    for pair, keys in zip(queries, keys_both, strict=True):
        both = nt(pair, keys) * HEAD ** (-0.5)
        slots = both.shape[0]
        scores += [both[:, :slots], both[:, slots:]]
    scores = [jnp.where(barred, -1000000000.0, part) for part in scores]
    peaks = [jnp.max(part, axis=-1, keepdims=True) for part in scores]
    weights = [jnp.exp(part - peak) for part, peak in zip(scores, peaks, strict=True)]
    totals = [1.0 / jnp.sum(part, axis=-1, keepdims=True) for part in weights]
    return [part * total for part, total in zip(weights, totals, strict=True)]


def joined(parts, pair):
    return jnp.concatenate([part.astype(bf16) for part in parts[2 * pair : 2 * pair + 2]], 1)


def barred_slots(slots, count):
    return lax.broadcasted_iota(jnp.int32, (slots, slots), 1) >= count


def pages_of(rows, slots, body):
    def step(page, carry):
        body(page, pl.ds(pl.multiple_of(page * slots, slots), slots))
        return carry

    lax.fori_loop(0, rows // slots, step, 0, unroll=2)


def column_sum(values):
    return jnp.sum(values.astype(f32), axis=0, keepdims=True)


def attend_kernel(grid, cross, slots, held, at_table, info_ref, counts_ref, vec_ref, *refs):
    if cross:
        inputs, refs = refs[:3], refs[3:]
    else:
        residual_ref, low_ref = refs[:2]
        refs = refs[2:]
    sources, refs = refs[:held], refs[held:]

    def row(i):
        return vec_ref[at_table[i] : at_table[i] + 1, :]

    q_ref, k_ref, v_ref, o_ref, sum_ref, norm_ref, norm_low_ref = refs[:7]
    blocks, sem = refs[7:9]
    rows = q_ref.shape[0]
    half = rows // 2
    wait_blocks = load_blocks(grid, info_ref, sources, blocks, sem)
    if cross:
        src_ref, oth_ref, in_sem = refs[9:12]
        load_inputs(info_ref, *inputs, src_ref, oth_ref, in_sem)()
    else:
        src_ref = oth_ref = low_ref
    wait_blocks()
    width = q_ref.shape[1]
    q_ref[...] = (nn(src_ref[...], matrix(blocks[0])) + row(0)).astype(bf16)
    k_ref[...] = nn(oth_ref[...], matrix(blocks[1])).astype(bf16)
    v_ref[...] = (nn(oth_ref[...], matrix(blocks[2])) + row(1)).astype(bf16)
    unused, left, right = lane_masks()
    cuts = [slice(at, at + 128) for at in range(0, width, 128)]

    def one_page(page, at):
        soft = softened(
            [q_ref[at, cut] for cut in cuts],
            [two_heads(k_ref[at, cut], left, right) for cut in cuts],
            barred_slots(slots, counts_ref[page]),
        )
        for i, cut in enumerate(cuts):
            mixed = nn(joined(soft, i), two_heads(v_ref[at, cut], left, right))
            o_ref[at, cut] = mixed.astype(bf16)

    pages_of(rows, slots, one_page)
    residual = src_ref[...].astype(f32) if cross else residual_ref[...]
    total = residual + nn(o_ref[...], matrix(blocks[3])) + row(2)
    sum_ref[...] = total
    result = normalised(total)[0] * row(3) + row(4)
    norm_ref[...] = result
    norm_low_ref[...] = result.astype(bf16)


def attend(grid, cross, slots, info, counts, vectors, at_table, inputs, weights):
    width = weights[0].shape[-1]
    rows = counts.shape[0] * slots
    blocks = block_shapes(grid, 4, grid.rows, width)
    scratch = [pltpu.VMEM(blocks, bf16), pltpu.SemaphoreType.DMA]
    if cross:
        scratch += [pltpu.VMEM((rows, width), bf16)] * 2 + [pltpu.SemaphoreType.DMA((4,))]
    return call(
        functools.partial(attend_kernel, grid, cross, slots, len(weights), at_table),
        [((rows, width), bf16)] * 4 + [((rows, width), f32)] * 2 + [((rows, width), bf16)],
        [info, counts, vectors] + list(inputs) + list(weights),
        [SMEM, SMEM, VMEM] + ([HBM] * 3 if cross else [VMEM] * 2) + [HBM] * len(weights),
        [VMEM] * 7,
        scratch,
        flops=8 * rows * width * width + 8 * rows * slots * width,
        moved=4 * width * width * 2 + rows * width * 20,
    )


def hidden_kernel(grid, held, info_ref, shift_ref, low_ref, *refs):
    sources = refs[:held]
    active_ref, slope_ref, blocks, sem = refs[held:]
    load_blocks(grid, info_ref, sources, blocks, sem)()
    width = low_ref.shape[1]
    for b in range(4):
        at = slice(b * width, (b + 1) * width)
        hidden = nn(low_ref[...], matrix(blocks[b])) + shift_ref[0:1, at]
        square = hidden * hidden
        bent = jnp.tanh(0.7978845608028654 * (hidden + 0.044715 * square * hidden))
        active_ref[:, at] = (0.5 * hidden * (1.0 + bent)).astype(bf16)
        slope = 0.5 * (1.0 + bent) + 0.5 * hidden * (1.0 - bent * bent) * (
            0.7978845608028654 * (1.0 + 3.0 * 0.044715 * square)
        )
        slope_ref[:, at] = slope.astype(bf16)


def hidden_layer(grid, info, shift, low, weights):
    rows, width = low.shape
    return call(
        functools.partial(hidden_kernel, grid, len(weights)),
        [((rows, 4 * width), bf16)] * 2,
        [info, shift, low] + list(weights),
        [SMEM, VMEM, VMEM] + [HBM] * len(weights),
        [VMEM, VMEM],
        [pltpu.VMEM(block_shapes(grid, 4, grid.rows, width), bf16), pltpu.SemaphoreType.DMA],
        flops=8 * rows * width * width,
        moved=8 * width * width + rows * width * 18,
    )


def store_wide(core, wide, keep, send, sem):
    copies = []
    for j in range(2):
        for which, target in ((core, keep), (1 - core, send)):
            copies.append(pltpu.make_async_copy(wide.at[:, 2 * which + j], target.at[j], sem))
    for copy in copies:
        copy.start()
    pltpu.make_async_copy(wide, wide, sem).wait()


def branch_kernel(grid, held, info_ref, vec_ref, active_ref, residual_ref, *refs):
    sources = refs[:held]
    sum_ref, norm_ref, far_ref, wide, sem = refs[held:]
    load_blocks(grid, info_ref, sources, wide, sem, mixed=True)()
    half = residual_ref.shape[0] // 2
    total = residual_ref[...] + nn(active_ref[...], matrix(wide[...])) + vec_ref[12:13, :]
    sum_ref[...] = total
    result = normalised(total)[0] * vec_ref[8:9, :] + vec_ref[11:12, :]
    norm_ref[...] = result[:half]
    far_ref[...] = result[half:].astype(bf16)


def branch_layer(grid, info, vectors, active, residual, weights):
    rows, width = residual.shape
    return call(
        functools.partial(branch_kernel, grid, len(weights)),
        [((rows, width), f32), ((rows // 2, width), f32), ((rows // 2, width), bf16)],
        [info, vectors, active, residual] + list(weights),
        [SMEM, VMEM, VMEM, VMEM] + [HBM] * len(weights),
        [VMEM] * 3,
        [pltpu.VMEM(block_shapes(grid, 4, grid.rows, width, True), bf16), pltpu.SemaphoreType.DMA],
        flops=8 * rows * width * width,
        moved=8 * width * width + rows * width * 20,
    )


def gate_kernel(grid, held, info_ref, shift_ref, third_ref, far_ref, cotangent_ref, *refs):
    sources = refs[:held]
    united_ref, grad_own_ref, grad_far_ref, grad_shift_ref, keep_ref, send_ref = refs[held : held + 6]
    blocks, sem, grads, mix_ref, low_ref, out_sem = refs[held + 6 :]
    load_blocks(grid, info_ref, sources, blocks, sem, 2)()
    first = info_ref[0] == 0
    low_ref[...] = third_ref[...].astype(bf16)
    logits = nn(low_ref[...], matrix(blocks[0])) + nn(far_ref[...], matrix(blocks[1])) + shift_ref[13:14, :]
    mixing = 1.0 / (1.0 + jnp.exp(-logits))
    share = jnp.where(first, mixing, 1.0 - mixing)
    mine, other = third_ref[...], far_ref[...].astype(f32)
    united_ref[...] = (share * mine + (1.0 - share) * other).astype(bf16)
    cotangent = cotangent_ref[...].astype(f32)
    gap = jnp.where(first, mine - other, other - mine)
    grad = (cotangent * gap * mixing * (1.0 - mixing)).astype(bf16)
    mix_ref[...] = grad
    grad_shift_ref[0:1, :] = column_sum(grad)
    direct = cotangent * share
    grad_own_ref[...] = direct + nt(mix_ref[...], matrix(blocks[0]))
    grad_far_ref[...] = (cotangent - direct + nt(mix_ref[...], matrix(blocks[1]))).astype(bf16)
    grads[0] = tn(low_ref[...], mix_ref[...]).astype(bf16)
    grads[1] = tn(far_ref[...], mix_ref[...]).astype(bf16)
    store_blocks(info_ref[1], grads, keep_ref, send_ref, out_sem)()


def gate_layer(grid, info, shift, third, far, cotangent, weights):
    rows, width = third.shape
    blocks = (2, width, width)
    return call(
        functools.partial(gate_kernel, grid, len(weights)),
        [
            ((rows, width), bf16),
            ((rows, width), f32),
            ((rows, width), bf16),
            ((8, width), f32),
            ((1,) + blocks[1:], bf16),
            ((1,) + blocks[1:], bf16),
        ],
        [info, shift, third, far, cotangent] + list(weights),
        [SMEM] + [VMEM] * 4 + [HBM] * len(weights),
        [VMEM] * 4 + [HBM] * 2,
        [
            pltpu.VMEM(block_shapes(grid, 2, grid.rows, width), bf16),
            pltpu.SemaphoreType.DMA,
            pltpu.VMEM(blocks, bf16),
            pltpu.VMEM((rows, width), bf16),
            pltpu.VMEM((rows, width), bf16),
            pltpu.SemaphoreType.DMA((2,)),
        ],
        flops=12 * rows * width * width,
        moved=8 * width * width + rows * width * 14,
    )


def branch_back_kernel(
    wide_out,
    info_ref,
    gain_ref,
    sum_ref,
    grad_own_ref,
    grad_far_ref,
    active_ref,
    grad_sum_ref,
    grad_low_ref,
    vec_ref,
    *refs,
):
    rows, width = sum_ref.shape
    half = rows // 2
    vec_ref[...] = jnp.zeros_like(vec_ref)
    for offset, grads_ref in ((0, grad_own_ref), (half, grad_far_ref)):
        at = slice(offset, offset + half)
        grads = grads_ref[...].astype(f32)
        back, gain_rows = norm_back(sum_ref[at, :], grads, gain_ref[8:9, :])
        low = back.astype(bf16)
        grad_sum_ref[at, :] = back
        grad_low_ref[at, :] = low
        vec_ref[0:1, :] += column_sum(gain_rows)
        vec_ref[1:2, :] += column_sum(grads)
        vec_ref[2:3, :] += column_sum(low)
    wide, sem = refs[-2:]
    for b in range(4):
        at = slice(b * width, (b + 1) * width)
        part = tn(active_ref[:, at], grad_low_ref[...]).astype(bf16)
        if wide_out:
            devices = wide.shape[0] // 4
            wide[b * devices : (b + 1) * devices] = part.reshape((devices,) + wide.shape[1:])
        else:
            wide[at, :] = part
    if wide_out:
        store_wide(info_ref[1], wide, refs[0], refs[1], sem)
    else:
        copy = pltpu.make_async_copy(wide, refs[0], sem)
        copy.start()
        copy.wait()


def branch_back(grid, info, gain, sums, grad_own, grad_far, active, piece):
    rows, width = sums.shape
    wide_out = piece % 16 == 0
    target = (2, grid.n, piece, width) if wide_out else (4 * width, width)
    outs = [(target, bf16)] * (2 if wide_out else 1)
    return call(
        functools.partial(branch_back_kernel, wide_out),
        [((rows, width), f32), ((rows, width), bf16), ((8, width), f32)] + outs,
        [info, gain, sums, grad_own, grad_far, active],
        [SMEM] + [VMEM] * 5,
        [VMEM] * 3 + [HBM] * len(outs),
        [
            pltpu.VMEM((grid.n, 4, piece, width) if wide_out else (4 * width, width), bf16),
            pltpu.SemaphoreType.DMA,
        ],
        flops=8 * rows * width * width,
        moved=8 * width * width + rows * width * 24,
    )


def hidden_back_kernel(grid, held, info_ref, grad_low_ref, slope_ref, low_ref, *refs):
    core = info_ref[1]
    grad_hidden_ref, vec_ref, keep_ref, send_ref, wide, sem, grads, out_sem = refs[held:]
    load_blocks(grid, info_ref, refs[:held], wide, sem, mixed=True)()
    whole_wide = matrix(wide[...])
    width = low_ref.shape[1]
    for b in range(4):
        at = slice(b * width, (b + 1) * width)
        low = (nt(grad_low_ref[...], whole_wide[at, :]) * slope_ref[:, at].astype(f32)).astype(bf16)
        grad_hidden_ref[:, at] = low
        vec_ref[0:1, at] = column_sum(low)
        grads[b] = tn(low_ref[...], low).astype(bf16)
    store_blocks(core, grads, keep_ref, send_ref, out_sem)()


def hidden_back(grid, info, grad_low, slope, low, weights):
    rows, width = low.shape
    blocks = (4, width, width)
    return call(
        functools.partial(hidden_back_kernel, grid, len(weights)),
        [((rows, 4 * width), bf16), ((8, 4 * width), f32)] + [((2,) + blocks[1:], bf16)] * 2,
        [info, grad_low, slope, low] + list(weights),
        [SMEM] + [VMEM] * 3 + [HBM] * len(weights),
        [VMEM] * 2 + [HBM] * 2,
        [
            pltpu.VMEM(block_shapes(grid, 4, grid.rows, width, True), bf16),
            pltpu.SemaphoreType.DMA,
            pltpu.VMEM(blocks, bf16),
            pltpu.SemaphoreType.DMA((4,)),
        ],
        flops=16 * rows * width * width,
        moved=16 * width * width + rows * width * 30,
    )


def second_back_kernel(
    grid, held, info_ref, gain_ref, sum_ref, grad_ref, grad_hidden_ref, *refs
):
    grad_sum_ref, vec_ref, blocks, sem = refs[held:]
    load_blocks(grid, info_ref, refs[:held], blocks, sem)()
    width = sum_ref.shape[1]
    total = grad_ref[...]
    for b in range(4):
        total += nt(grad_hidden_ref[:, b * width : (b + 1) * width], matrix(blocks[b]))
    grad_sum_ref[...] = norm_back_into(vec_ref, sum_ref[...], total, gain_ref[7:8, :])


def norm_back_into(vec_ref, sums, grads, gain):
    back, gain_rows = norm_back(sums, grads, gain)
    vec_ref[0:1, :] = column_sum(gain_rows)
    vec_ref[1:2, :] = column_sum(grads)
    return back


def second_back(grid, info, gain, sums, grads, grad_hidden, weights):
    rows, width = sums.shape
    return call(
        functools.partial(second_back_kernel, grid, len(weights)),
        [((rows, width), f32), ((8, width), f32)],
        [info, gain, sums, grads, grad_hidden] + list(weights),
        [SMEM] + [VMEM] * 4 + [HBM] * len(weights),
        [VMEM] * 2,
        [pltpu.VMEM(block_shapes(grid, 4, grid.rows, width), bf16), pltpu.SemaphoreType.DMA],
        flops=8 * rows * width * width,
        moved=8 * width * width + rows * width * 20,
    )


def scores_back_kernel(
    grid, cross, slots, held, info_ref, counts_ref, grad_ref, q_ref, k_ref, v_ref, o_ref, *refs
):
    count = 3 if cross else 1
    inputs, sources, refs = refs[:count], refs[count : count + held], refs[count + held :]
    dq_ref, dk_ref, dv_ref, vec_ref, keep_ref, send_ref = refs[:6]
    weight, sem, low_grad, grad_o, grads, out_sem = refs[6:12]
    wait_block = load_blocks(grid, info_ref, sources, weight, sem, 1, 1)
    if cross:
        src_ref, oth_ref, in_sem = refs[12:]
        wait_inputs = load_inputs(info_ref, *inputs, src_ref, oth_ref, in_sem)
    else:
        src_ref = oth_ref = inputs[0]
    rows, width = q_ref.shape
    low = grad_ref[...].astype(bf16)
    low_grad[...] = low
    vec_ref[2:3, :] = column_sum(low)
    grads[3] = tn(o_ref[...], low_grad[...]).astype(bf16)
    wait_block()
    grad_o[...] = nt(low_grad[...], matrix(weight[0])).astype(bf16)
    left_lanes, left, right = lane_masks()
    cuts = [slice(at, at + 128) for at in range(0, width, 128)]

    def one_page(page, at):
        keys = [two_heads(k_ref[at, cut], left, right) for cut in cuts]
        soft = softened(
            [q_ref[at, cut] for cut in cuts], keys, barred_slots(slots, counts_ref[page])
        )
        grad_soft = []
        for cut in cuts:
            both = nt(grad_o[at, cut], two_heads(v_ref[at, cut], left, right))
            grad_soft += [both[:, :slots], both[:, slots:]]
        weighted = [a * b for a, b in zip(soft, grad_soft, strict=True)]
        sums = [jnp.sum(part, axis=-1, keepdims=True) for part in weighted]
        grad_scores = [w - p * t for w, p, t in zip(weighted, soft, sums, strict=True)]
        for i, cut in enumerate(cuts):
            dv = tn(joined(soft, i), grad_o[at, cut])
            dv_ref[at, cut] = jnp.where(left_lanes, dv[:slots], dv[slots:]).astype(bf16)
        for i, cut in enumerate(cuts):
            pair = joined(grad_scores, i)
            dq_ref[at, cut] = (nn(pair, keys[i]) * HEAD ** (-0.5)).astype(bf16)
            dk = tn(pair, q_ref[at, cut]) * HEAD ** (-0.5)
            dk_ref[at, cut] = jnp.where(left_lanes, dk[:slots], dk[slots:]).astype(bf16)

    pages_of(rows, slots, one_page)
    vec_ref[0:1, :] = column_sum(dq_ref[...])
    vec_ref[1:2, :] = column_sum(dv_ref[...])
    if cross:
        wait_inputs()
    grads[0] = tn(src_ref[...], dq_ref[...]).astype(bf16)
    grads[1] = tn(oth_ref[...], dk_ref[...]).astype(bf16)
    grads[2] = tn(oth_ref[...], dv_ref[...]).astype(bf16)
    store_blocks(info_ref[1], grads, keep_ref, send_ref, out_sem)()


def scores_back(grid, cross, slots, info, counts, grad, saved, inputs, weights):
    rows, width = grad.shape
    full = pltpu.VMEM((rows, width), bf16)
    blocks = (4, width, width)
    scratch = [
        pltpu.VMEM(block_shapes(grid, 1, grid.rows, width), bf16),
        pltpu.SemaphoreType.DMA,
        full,
        full,
        pltpu.VMEM(blocks, bf16),
        pltpu.SemaphoreType.DMA((4,)),
    ]
    if cross:
        scratch += [full, full, pltpu.SemaphoreType.DMA((4,))]
    return call(
        functools.partial(scores_back_kernel, grid, cross, slots, len(weights)),
        [((rows, width), bf16)] * 3 + [((8, width), f32)] + [((2,) + blocks[1:], bf16)] * 2,
        [info, counts, grad] + list(saved) + list(inputs) + list(weights),
        [SMEM, SMEM] + [VMEM] * 5 + ([HBM] * 3 if cross else [VMEM]) + [HBM] * len(weights),
        [VMEM] * 4 + [HBM] * 2,
        scratch,
        flops=10 * rows * width * width + 24 * rows * slots * width,
        moved=12 * width * width + rows * width * 20,
    )


def project_back_kernel(grid, cross, held, info_ref, gain_ref, grad_ref, *refs):
    dq_ref, dk_ref, dv_ref = refs[:3]
    refs = refs[3:]
    if cross:
        sources = refs[:held]
        mine_ref, other_ref, far_ref, blocks, sem = refs[held:]
    else:
        sum_ref, sources = refs[0], refs[1 : 1 + held]
        out_ref, vec_ref, blocks, sem = refs[1 + held :]
    load_blocks(grid, info_ref, sources, blocks, sem)()
    half = grad_ref.shape[0] // 2
    mine = grad_ref[...] + nt(dq_ref[...], matrix(blocks[0]))
    other = nt(dk_ref[...], matrix(blocks[1])) + nt(dv_ref[...], matrix(blocks[2]))
    if cross:
        mine_ref[...] = mine[:half]
        other_ref[...] = other[:half]
        far_ref[:half] = other[half:].astype(bf16)
        far_ref[half:] = mine[half:].astype(bf16)
    else:
        vec_ref[...] = jnp.zeros_like(vec_ref)
        out_ref[...] = norm_back_into(vec_ref, sum_ref[...], mine + other, gain_ref[6:7, :])


def project_back(grid, cross, info, gain, grad, parts, sums, weights):
    rows, width = grad.shape
    half = (rows // 2, width)
    if cross:
        outs = [(half, f32), (half, f32), ((rows, width), bf16)]
    else:
        outs = [((rows, width), f32), ((8, width), f32)]
    return call(
        functools.partial(project_back_kernel, grid, cross, len(weights)),
        outs,
        [info, gain, grad] + list(parts) + list(sums) + list(weights),
        [SMEM] + [VMEM] * (5 + len(sums)) + [HBM] * len(weights),
        [VMEM] * len(outs),
        [pltpu.VMEM(block_shapes(grid, 4, grid.rows, width), bf16), pltpu.SemaphoreType.DMA],
        flops=6 * rows * width * width,
        moved=8 * width * width + rows * width * 18,
    )


SPOTS = (
    [(i, 0, 1) for i in range(3)]
    + [(i, 128, 1) for i in range(3)]
    + [(i, 256, 1) for i in range(3)]
    + [(i, 384, 1) for i in range(3)]
    + [(4, 0, 1), (4, 128, 1), (3, 0, 4)]
)
EXTRA = 16


def lay_vectors(cross_bias, self_bias, gains, shifts, out_bias, gate_bias, in_bias, width):
    def at(values, row, lane):
        depth, length = values.shape[1:]
        return jnp.pad(
            values, ((0, 0), (row, EXTRA - row - depth), (lane, width - lane - length))
        )

    gate = jnp.broadcast_to(gate_bias[None, None], (2, 1) + gate_bias.shape)
    return (
        at(cross_bias, 0, 0)
        + at(self_bias, 0, 128)
        + at(gains, 0, 256)
        + at(shifts, 0, 384)
        + at(out_bias[:, None], 4, 0)
        + at(gate, 4, 128)
        + at(in_bias[:, None], 3, 0)
    )


def unlay_kernel(grid, start, info_ref, mine_ref, other_ref, table_ref, wide_ref, held, found, sem):
    copies = []
    for k, ref in enumerate((mine_ref, other_ref)):
        source = ref.at[:, :, pl.ds(start, EXTRA)]
        copies.append(pltpu.make_async_copy(source, held.at[k], sem.at[k]))
    for copy in copies:
        copy.start()
    for copy in copies:
        copy.wait()
    unused, unused, second, first_step, second_step = grid.place(info_ref)
    for g in range(4):
        for a in range(2):
            for k, b in ((0, second), (1, 1 - second)):
                place = 4 * g + a * first_step + b * second_step
                found[place] = held[k, g, a].astype(f32)
    rows = grid.rows
    for p in range(grid.n):
        for i, (row, lane, unused) in enumerate(SPOTS[:-1]):
            table_ref[i : i + 1, p * rows : (p + 1) * rows] = found[p, row : row + 1, lane : lane + rows]
        row, lane, length = SPOTS[-1]
        wide_ref[0:1, p * length * rows : (p + 1) * length * rows] = found[
            p, row : row + 1, lane : lane + length * rows
        ]


def unlay_vectors(grid, info, pieces, start):
    width = pieces[0].shape[-1]
    rows = grid.rows
    if len(pieces) == 1:
        found = extra_rows(grid, info, pieces, start, EXTRA).astype(f32)
        parts = [
            found[:, row, lane : lane + length * rows].reshape(-1) for row, lane, length in SPOTS
        ]
        table = jnp.pad(jnp.stack(parts[:-1]), ((0, 2), (0, 0)))
        return table, jnp.pad(parts[-1][None], ((0, 7), (0, 0)))
    return call(
        functools.partial(unlay_kernel, grid, start),
        [((16, width), f32), ((8, 4 * width), f32)],
        [info] + pieces[:2],
        [SMEM, HBM, HBM],
        [VMEM, VMEM],
        [
            pltpu.VMEM((2, 4, 2, EXTRA, width), bf16),
            pltpu.VMEM((grid.n, EXTRA, width), f32),
            pltpu.SemaphoreType.DMA((2,)),
        ],
        room=GLUE_LIMIT,
    )


def relay_kernel(grid, where, *refs):
    out, held = refs[-2:]
    rows = grid.rows
    held[...] = jnp.zeros_like(held)
    for p in range(grid.n):
        for (table, i), (row, lane, length) in zip(where, SPOTS, strict=True):
            size = length * rows
            held[p, row : row + 1, lane : lane + size] = refs[table][i : i + 1, p * size : (p + 1) * size]
    out[...] = held[...].astype(bf16)


def relay_vectors(grid, tables, where):
    width = tables[0].shape[1]
    rows = grid.rows
    if rows % 16:
        out = jnp.zeros((grid.n, EXTRA, width), f32)
        for (table, i), (row, lane, length) in zip(where, SPOTS, strict=True):
            part = tables[table][i].reshape(grid.n, length * rows)
            out = out.at[:, row, lane : lane + length * rows].set(part)
        return out.astype(bf16)
    return call(
        functools.partial(relay_kernel, grid, where),
        [((grid.n, EXTRA, width), bf16)],
        tables,
        [VMEM] * len(tables),
        [VMEM],
        [pltpu.VMEM((grid.n, EXTRA, width), f32)],
        room=GLUE_LIMIT,
    )[0]


def on_device(
    grid,
    language_in,
    vision_in,
    language_count,
    vision_count,
    cross_qkv,
    cross_proj,
    cross_bias,
    norm_gain,
    norm_bias,
    self_qkv,
    self_proj,
    self_bias,
    ffn_in,
    ffn_in_bias,
    ffn_out,
    ffn_out_bias,
    gate_weight,
    gate_bias,
    cotangent,
):
    n = grid.n
    grid.rows = cross_proj.shape[1]
    me = lax.axis_index("dp")
    core = lax.axis_index("rep")
    side = ((me // grid.high) ^ (me // grid.partner)) & 1
    first = side == 0
    info = jnp.stack([side, core, me]).astype(jnp.int32)
    rows, width = cross_proj.shape[1:]
    dim = n * rows
    pages, slots = language_in.shape[:2]
    wide_ok = rows % 16 == 0

    def own(pair):
        return lax.dynamic_index_in_dim(pair, side, 0, keepdims=False)

    def other(pair):
        return lax.dynamic_index_in_dim(pair, 1 - side, 0, keepdims=False)

    vectors = lay_vectors(
        cross_bias, self_bias, norm_gain, norm_bias, ffn_out_bias, gate_bias, ffn_in_bias, width
    )
    groups = [
        [cross_qkv[:, 0], cross_qkv[:, 1], vectors, cross_qkv[:, 2], cross_proj, vectors],
        [self_qkv[:, 0], self_qkv[:, 1], self_qkv[:, 2], self_proj],
        [ffn_in[:, :, i * width : (i + 1) * width] for i in range(4)],
        [ffn_out[:, i * rows : (i + 1) * rows] for i in range(2)]
        + [gate_weight]
        + [ffn_out[:, i * rows : (i + 1) * rows] for i in range(2, 4)]
        + [gate_weight[::-1]],
    ]

    def shards(blocks):
        half = len(blocks) // 2
        parts = [jnp.concatenate(blocks[:half], 1), jnp.concatenate(blocks[half:], 1)]
        mine = lax.dynamic_index_in_dim(jnp.stack(parts), core, 0, keepdims=False)
        return own(mine), other(mine)

    sent = [shards(blocks) for blocks in groups]
    later = [jnp.concatenate([part[k] for part in sent[2:]], 0) for k in range(2)]
    parts = [part[0].shape[0] for part in sent[2:]]
    language = language_in.reshape(pages * slots, width)
    vision = vision_in.reshape(pages * slots, width)
    counts_mine = jnp.stack([language_count, vision_count])
    counts_wide = jnp.pad(counts_mine.astype(bf16), ((0, 14), (0, width - pages)))
    seen = jnp.concatenate([language, vision, counts_wide], 0)

    t1 = all_meet(grid, info, *sent[0])
    u0 = grid.across(sent[1][1], grid.partner)
    t1, u0, later = tie(t1, u0, later)
    t2 = second_hops(grid, grouped(grid, info, t1))
    u1, place_u = meet(grid, info, pair(info, grid.high_bit - 1, sent[1][0], u0)[0])
    later_far = grid.across(later[1], grid.partner)
    t2, u1, later_far, seen = tie(t2, u1, later_far, seen)
    t3 = third_hops(grid, info, t2)
    u2 = second_hops(grid, place_u(u1))
    w0, x0 = pair(info, grid.high_bit - 1, later[0], later_far, parts)
    w1, place_w = meet(grid, info, w0)
    seen_far = grid.across(seen, grid.partner)
    t3, u2, w1, seen_far, x0 = tie(t3, u2, w1, seen_far, x0)
    cross_w = whole(grid, info, t3, rows, 2)
    table, ffn_in_shift = unlay_vectors(grid, info, t3, 2 * rows)
    counts_far = seen_far[2 * pages * slots :, :pages][:2].astype(jnp.int32)
    counts = jnp.concatenate([own(counts_mine), own(counts_far)])
    other_counts = jnp.concatenate([other(counts_mine), other(counts_far)])
    inputs = [language, vision, seen_far]
    u3 = third_hops(grid, info, u2)
    w2 = second_hops(grid, place_w(w1))
    x1, place_x = meet(grid, info, x0)
    cq, ck, cv, co, first_sum, first_norm, first_low = attend(
        grid, True, slots, info, other_counts, table, (0, 1, 2, 6, 9), inputs, cross_w
    )
    first_norm, first_low, u3, w2, x1 = tie(first_norm, first_low, u3, w2, x1)
    self_w = whole(grid, info, u3, rows, 2)
    w3 = third_hops(grid, info, w2)
    x2 = second_hops(grid, place_x(x1))
    sq, sk, sv, so, second_sum, second_norm, second_low = attend(
        grid,
        False,
        slots,
        info,
        counts,
        table,
        (3, 4, 5, 7, 10),
        [first_norm, first_low],
        self_w,
    )
    second_norm, second_low, w3, x2 = tie(second_norm, second_low, w3, x2)
    in_w = whole(grid, info, w3, rows, 2)
    x3 = third_hops(grid, info, x2)
    active, slope = hidden_layer(grid, info, ffn_in_shift, second_low, in_w)
    active, second_norm, x3 = tie(active, second_norm, x3)
    gate_w = out_w = whole(grid, info, x3, rows, 3)
    if len(out_w) == 2:
        both = jnp.where(core == 0, jnp.stack(out_w), jnp.stack(out_w[::-1]))[:, :2]
        both = both.reshape(4, n, rows, width).transpose(1, 0, 2, 3)
        out_w = [both.reshape(4 * dim, width)]
    third_sum, third_own, third_send = branch_layer(
        grid, info, table, active, second_norm, out_w
    )
    third_far = grid.across(third_send, grid.partner)
    cotangent_rows = cotangent.reshape(pages * slots, width)
    united, grad_third_own, grad_third_send, grad_gate_shift, gate_keep, gate_send = gate_layer(
        grid, info, table, third_own, third_far, cotangent_rows, gate_w
    )

    def by_piece(values):
        return values.reshape(values.shape[0], n, rows, width)

    gate_keep, gate_send = by_piece(gate_keep), by_piece(gate_send)
    gate_got = grid.swap_cores(gate_send)
    grad_third_far = grid.across(grad_third_send, grid.partner)
    gate = first_returns(grid, info, gate_keep, gate_got)
    gate[0], grad_third_far = tie(gate[0], grad_third_far)
    grad_third_sum, grad_branch_low, vec_third, *out_grads = branch_back(
        grid, info, table, third_sum, grad_third_own, grad_third_far, active, rows
    )
    if len(out_grads) == 1:
        by_core = out_grads[0].reshape(n, 2, 2, rows, width).transpose(1, 2, 0, 3, 4)
        out_grads = [
            lax.dynamic_index_in_dim(by_core, c, 0, keepdims=False) for c in (core, 1 - core)
        ]
    out_keep, out_send = out_grads
    gate, grad_branch_low, out_keep, out_send = tie(gate, grad_branch_low, out_keep, out_send)
    out_got = grid.swap_cores(out_send)
    grad_hidden, vec_hidden, in_keep, in_send = hidden_back(
        grid, info, grad_branch_low, slope, second_low, out_w
    )
    out_got, grad_hidden, in_keep, in_send = tie(out_got, grad_hidden, in_keep, in_send)
    in_keep, in_send = by_piece(in_keep), by_piece(in_send)
    in_got = grid.swap_cores(in_send)
    outs = first_returns(grid, info, out_keep, out_got)
    grad_second_sum, vec_second = second_back(
        grid, info, table, second_sum, grad_third_sum, grad_hidden, in_w
    )
    outs, in_got, grad_second_sum = tie(outs, in_got, grad_second_sum)
    ins = first_returns(grid, info, in_keep, in_got)
    outs = second_returns(grid, info, gate, outs)
    *self_parts, vec_self, self_keep, self_send = scores_back(
        grid, False, slots, info, counts, grad_second_sum, [sq, sk, sv, so], [first_low], self_w
    )
    outs, ins, self_parts, self_keep, self_send = tie(outs, ins, self_parts, self_keep, self_send)
    self_keep, self_send = by_piece(self_keep), by_piece(self_send)
    self_got = grid.swap_cores(self_send)
    ins = second_returns(grid, info, ins)
    outs = third_returns(grid, info, outs)
    grad_first_sum, vec_first = project_back(
        grid, False, info, table, grad_second_sum, self_parts, [first_sum], self_w
    )
    ins, self_got, grad_first_sum = tie(ins, self_got, grad_first_sum)
    selfs = first_returns(grid, info, self_keep, self_got)
    ins = third_returns(grid, info, ins)
    *cross_parts, vec_cross, cross_keep, cross_send = scores_back(
        grid, True, slots, info, other_counts, grad_first_sum, [cq, ck, cv, co], inputs, cross_w
    )
    selfs, outs, cross_parts, cross_keep, cross_send = tie(
        selfs, outs, cross_parts, cross_keep, cross_send
    )
    cross_keep, cross_send = by_piece(cross_keep), by_piece(cross_send)
    cross_got = grid.swap_cores(cross_send)
    selfs = second_returns(grid, info, selfs)
    tables = [vec_cross, vec_self, vec_first, vec_second, vec_third, grad_gate_shift, vec_hidden]
    where = [(0, 0), (0, 1), (0, 2), (1, 0), (1, 1), (1, 2)]
    where += [(2, 0), (3, 0), (4, 0), (2, 1), (3, 1), (4, 1), (4, 2), (5, 0), (6, 0)]
    grad_vec = relay_vectors(grid, tables, where)
    grad_mine, grad_theirs, outgoing = project_back(
        grid, True, info, table, grad_first_sum, cross_parts, [], cross_w
    )
    cross_got, outgoing, selfs, ins, outs, grad_vec = tie(
        cross_got, outgoing, selfs, ins, outs, grad_vec
    )
    crosses = first_returns(grid, info, cross_keep, cross_got, grad_vec)
    incoming = grid.across(outgoing, grid.partner)
    selfs = third_returns(grid, info, selfs)
    crosses, selfs = tie(crosses, selfs)
    crosses = second_returns(grid, info, crosses)
    crosses[0], outs, ins = tie(crosses[0], outs, ins)
    out_done = last_swap(grid, outs)
    in_done = last_swap(grid, ins)

    def sides(near, far):
        return jnp.where(first, jnp.stack([near, far]), jnp.stack([far, near]))

    def finished(done, count, start=0):
        mine, far = [part[:, start * rows : (start + count) * rows] for part in done]
        mine, far = [part.reshape(2, count, rows, width) for part in (mine, far)]
        both = jnp.where(core == 0, jnp.concatenate([mine, far], 1), jnp.concatenate([far, mine], 1))
        return both.astype(f32)

    def by_side(both):
        return jnp.where(first, both, both[::-1])

    def attention_grads(done):
        if rows % 16:
            both = by_side(finished(done, 2))
            return [both[:, 0:3], both[:, 3]]
        layout = (((0, (0,)), (0, (1,))), ((0, (2,)), (1, ())))
        return finish(info, done, layout, rows, [(2, 3, rows, width), (2, rows, width)])

    if rows % 16:
        in_all = by_side(finished(in_done, 2)).transpose(0, 2, 1, 3).reshape(2, rows, 4 * width)
        gate_all = finished(out_done, 1)
        gate_both = sides(gate_all[0, 0] + gate_all[1, 1], gate_all[0, 1] + gate_all[1, 0])
        out_all = by_side(finished(out_done, 2, 1)).reshape(2, 4 * rows, width)
    else:
        every = slice(None)
        cuts = [(0, (every, slice(i * width, (i + 1) * width))) for i in range(4)]
        in_all = finish(info, in_done, (cuts[:2], cuts[2:]), rows, [(2, rows, 4 * width)])[0]
        gate_both = call(
            finish_gate_kernel,
            [((2, rows, width), f32)],
            [info] + list(out_done),
            [SMEM, VMEM, VMEM],
            [VMEM],
            room=GLUE_LIMIT,
        )[0]
        places = [(1, ())] + [(0, (slice(i * rows, (i + 1) * rows),)) for i in range(4)]
        layout = ((places[0], places[1], places[2]), (places[0], places[3], places[4]))
        shapes = [(2, 4 * rows, width), (2, rows, width)]
        out_all = finish(info, out_done, layout, rows, shapes)[0]
    crosses, in_all, out_all, gate_both = tie(crosses, in_all, out_all, gate_both)
    crosses = third_returns(grid, info, crosses)
    selfs, crosses[0], incoming = tie(selfs, crosses[0], incoming)
    self_done = last_swap(grid, selfs)
    page_shape = language_in.shape
    got = incoming.astype(f32)
    grad_mine = grad_mine + got[: pages * slots]
    grad_theirs = grad_theirs + got[pages * slots :]
    grad_language = jnp.where(first, grad_mine, grad_theirs).astype(bf16).reshape(page_shape)
    grad_vision = jnp.where(first, grad_theirs, grad_mine).astype(bf16).reshape(page_shape)

    self_qkv_grad, self_proj_grad = attention_grads(self_done)
    crosses, self_qkv_grad, self_proj_grad, grad_language, grad_vision = tie(
        crosses, self_qkv_grad, self_proj_grad, grad_language, grad_vision
    )
    cross_done = last_swap(grid, crosses)
    cross_qkv_grad, cross_proj_grad = attention_grads(cross_done)
    vec_sum = (cross_done[0].astype(f32) + cross_done[1].astype(f32))[:, 2 * rows :]
    vec_both = by_side(vec_sum)
    gate_vec = vec_sum[0, 4, 128 : 128 + rows] + vec_sum[1, 4, 128 : 128 + rows]
    return (
        united.reshape(page_shape),
        grad_language,
        grad_vision,
        cross_qkv_grad,
        cross_proj_grad,
        vec_both[:, 0:3, :rows],
        vec_both[:, 0:3, 256 : 256 + rows],
        vec_both[:, 0:3, 384 : 384 + rows],
        self_qkv_grad,
        self_proj_grad,
        vec_both[:, 0:3, 128 : 128 + rows],
        in_all,
        vec_both[:, 3, : 4 * rows],
        out_all,
        vec_both[:, 4, :rows],
        gate_both,
        gate_vec,
    )


def solution(mesh):
    whole = P(("dp", "rep"), None, None)
    weights = (
        P(None, None, "dp", None),
        P(None, "dp", None),
        P(None, None, "dp"),
        P(None, None, "dp"),
        P(None, None, "dp"),
        P(None, None, "dp", None),
        P(None, "dp", None),
        P(None, None, "dp"),
        P(None, "dp", None),
        P(None, "dp"),
        P(None, "dp", None),
        P(None, "dp"),
        P(None, "dp", None),
        P("dp"),
    )
    return jax.shard_map(
        functools.partial(on_device, Grid(mesh)),
        mesh=mesh,
        in_specs=(whole, whole, P(("dp", "rep")), P(("dp", "rep"))) + weights + (whole,),
        out_specs=(whole, whole, whole) + weights,
        check_vma=False,
    )
```

profile of v0, /device:TPU:0, one launch (start us, length us, event | category | flops | bytes accessed | tf_op | source)
XLA Modules:
  0.0 359.2 jit_solution(17626940636124552703)
XLA Ops:
  4.5 4.1 %collective-permute-start.1 = (bf16[112,768]{1,0:T(8,128)(2,1)S(1)}, bf16[112,768]{1,0:T(8,128)(2,1)S(1)}, u32[]{:S(2)}, u32[]{:S(2)}) collective-permute-start(bf16[112,768]{1,0:T(8,128)(2,1)S(1)} %get-tuple-element.482), channel_id=1, source_target_pairs={{0,16},{1,17},{2,18},{3,19},{4,20},{5,21},{6,22},{7,23},{8,24},{9,... | collective-permute-start | bytes 516104 | tf_op jit(solution)/shard_map/ppermute | solution.py:42
  12.2 11.6 %collective-permute-done.3.refs_1_ = bf16[96,768]{1,0:T(8,128)(2,1)S(1)} collective-permute-done((bf16[96,768]{1,0:T(8,128)(2,1)S(1)}, bf16[96,768]{1,0:T(8,128)(2,1)S(1)}, u32[]{:S(2)}, u32[]{:S(2)}) %collective-permute-start.3) | collective-permute-done | bytes 147488 | tf_op jit(solution)/shard_map/ppermute | solution.py:42
  28.1 2.9 collective-permute-start.5
  31.1 13.8 %collective-permute-done.5.refs_1_ = bf16[2,96,768]{2,1,0:T(8,128)(2,1)S(1)} collective-permute-done((bf16[2,96,768]{2,1,0:T(8,128)(2,1)S(1)}, bf16[2,96,768]{2,1,0:T(8,128)(2,1)S(1)}, u32[]{:S(2)}, u32[]{:S(2)}) %collective-permute-start.5) | collective-permute-done | bytes 294944 | tf_op jit(solution)/shard_map/ppermute | solution.py:42
  49.5 22.2 %collective-permute-done.10.refs_1_ = bf16[2,96,768]{2,1,0:T(8,128)(2,1)S(1)} collective-permute-done((bf16[2,96,768]{2,1,0:T(8,128)(2,1)S(1)}, bf16[2,96,768]{2,1,0:T(8,128)(2,1)S(1)}, u32[]{:S(2)}, u32[]{:S(2)}) %collective-permute-start.10) | collective-permute-done | bytes 294944 | tf_op jit(solution)/shard_map/ppermute | solution.py:42
  77.6 2.2 collective-permute-start.16
  79.9 7.8 %shard_map.320 = (bf16[512,768]{1,0:T(8,128)(2,1)S(1)}, bf16[512,768]{1,0:T(8,128)(2,1)S(1)}, bf16[512,768]{1,0:T(8,128)(2,1)S(1)}, bf16[512,768]{1,0:T(8,128)(2...) custom-call(s32[3]{0:T(128)S(1)} %pad_add_fusion.2.info_ref, ...), custom_call_target="tpu_custom_call" | custom-call | flops 2818572288 | bytes 12582912 | tf_op jit(solution)/shard_map/pallas_call | solution.py:73
  92.4 4.7 %collective-permute-done.13.refs_3_.refs_2_.refs_5_ = bf16[4,2,96,768]{3,2,1,0:T(8,128)(2,1)S(1)} collective-permute-done((bf16[4,2,96,768]{3,2,1,0:T(8,128)(2,1)S(1)}, bf16[4,2,96,768]{3,2,1,0:T(8,128)(2,1)S(1)}, u32[]{:S(2)}, u32[]{:S(2)}) %collective-permute-start.13) | collective-permute-done | bytes 1179680 | tf_op jit(solution)/shard_map/ppermute | solution.py:56
  100.5 7.3 %shard_map.323 = (bf16[512,768]{1,0:T(8,128)(2,1)S(1)}, bf16[512,768]{1,0:T(8,128)(2,1)S(1)}, bf16[512,768]{1,0:T(8,128)(2,1)S(1)}, bf16[512,768]{1,0:T(8,128)(2...) custom-call(s32[3]{0:T(128)S(1)} %pad_add_fusion.2.info_ref, ...), custom_call_target="tpu_custom_call" | custom-call | flops 2818572288 | bytes 12582912 | tf_op jit(solution)/shard_map/pallas_call | solution.py:73
  111.5 11.0 %collective-permute-done.20.other = bf16[4,144,768]{2,1,0:T(8,128)(2,1)S(1)} collective-permute-done((bf16[4,144,768]{2,1,0:T(8,128)(2,1)S(1)}, bf16[4,144,768]{2,1,0:T(8,128)(2,1)S(1)}, u32[]{:S(2)}, u32[]{:S(2)}) %collective-permute-start.20) | collective-permute-done | bytes 884768 | tf_op jit(solution)/shard_map/ppermute | solution.py:56
  125.9 4.3 %collective-permute-done.21.refs_3_ = bf16[4,2,96,768]{3,2,1,0:T(8,128)(2,1)S(1)} collective-permute-done((bf16[4,2,96,768]{3,2,1,0:T(8,128)(2,1)S(1)}, bf16[4,2,96,768]{3,2,1,0:T(8,128)(2,1)S(1)}, u32[]{:S(2)}, u32[]{:S(2)}) %collective-permute-start.21) | collective-permute-done | bytes 1179680 | tf_op jit(solution)/shard_map/ppermute | solution.py:48
  130.1 6.7 %shard_map.326 = (bf16[512,3072]{1,0:T(8,128)(2,1)S(1)}, bf16[512,3072]{1,0:T(8,128)(2,1)S(1)}) custom-call(s32[3]{0:T(128)S(1)} %pad_add_fusion.2.info_ref, f32[8,3072]{1,0:T(8,128)S(1)} %get-tuple-element.256.shift_ref, bf16[512,768]{1,0:T(8,128)(2,1)S(1)} %get-tuple-element.275.low_ref, bf16[4,2,96,768]{3,2,1,0:T(8,128)(2,1)S(1)} %shard_map.324.refs_0_, ...), custom_call_target="tpu_custom_call" | custom-call | flops 2415919104 | bytes 11796480 | tf_op jit(solution)/shard_map/pallas_call | solution.py:73
  137.9 1.7 copy-done.52
  140.5 6.9 %collective-permute-done.22.refs_1_ = bf16[4,2,144,768]{3,2,1,0:T(8,128)(2,1)S(1)} collective-permute-done((bf16[4,2,144,768]{3,2,1,0:T(8,128)(2,1)S(1)}, bf16[4,2,144,768]{3,2,1,0:T(8,128)(2,1)S(1)}, u32[]{:S(2)}, u32[]{:S(2)}) %collective-permute-start.22) | collective-permute-done | bytes 1769504 | tf_op jit(solution)/shard_map/ppermute | solution.py:56
  147.4 3.7 %collective-permute-done.24.refs_3_ = bf16[4,2,144,768]{3,2,1,0:T(8,128)(2,1)S(1)} collective-permute-done((bf16[4,2,144,768]{3,2,1,0:T(8,128)(2,1)S(1)}, bf16[4,2,144,768]{3,2,1,0:T(8,128)(2,1)S(1)}, u32[]{:S(2)}, u32[]{:S(2)}) %collective-permute-start.24) | collective-permute-done | bytes 1769504 | tf_op jit(solution)/shard_map/ppermute | solution.py:48
  151.0 4.4 %shard_map.328 = (f32[512,768]{1,0:T(8,128)S(1)}, f32[256,768]{1,0:T(8,128)S(1)}, bf16[256,768]{1,0:T(8,128)(2,1)S(1)}) custom-call(s32[3]{0:T(128)S(1)} %pad_add_fusion.2.info_ref, f32[16,768]{1,0:T(8,128)S(1)} %get-tuple-element.255.vec_ref.shift_ref.gain_ref, bf16[512,3072]{1,0:T(8,128)(2,1)S(1)} %get-tuple-element.283.active_ref, ...), custom_call_target="tpu_custom_call" | custom-call | flops 2415919104 | bytes 12582912 | tf_op jit(solution)/shard_map/pallas_call | solution.py:73
  156.8 9.9 %collective-permute-done.25.far_ref = bf16[256,768]{1,0:T(8,128)(2,1)S(1)} collective-permute-done((bf16[256,768]{1,0:T(8,128)(2,1)S(1)}, bf16[256,768]{1,0:T(8,128)(2,1)S(1)}, u32[]{:S(2)}, u32[]{:S(2)}) %collective-permute-start.25) | collective-permute-done | bytes 393248 | tf_op jit(solution)/shard_map/ppermute | solution.py:42
  166.7 4.5 %shard_map.329 = (bf16[256,768]{1,0:T(8,128)(2,1)}, f32[256,768]{1,0:T(8,128)S(1)}, bf16[256,768]{1,0:T(8,128)(2,1)S(1)}, f32[8,768]{1,0:T(8,128)S(1)}, bf16[1,7...) custom-call(s32[3]{0:T(128)S(1)} %pad_add_fusion.2.info_ref, ...), custom_call_target="tpu_custom_call" | custom-call | flops 1811939328 | bytes 7471104 | tf_op jit(solution)/shard_map/pallas_call | solution.py:73
  176.9 6.0 %collective-permute-done.27.grad_far_ref = bf16[256,768]{1,0:T(8,128)(2,1)S(1)} collective-permute-done((bf16[256,768]{1,0:T(8,128)(2,1)S(1)}, bf16[256,768]{1,0:T(8,128)(2,1)S(1)}, u32[]{:S(2)}, u32[]{:S(2)}) %collective-permute-start.27) | collective-permute-done | bytes 393248 | tf_op jit(solution)/shard_map/ppermute | solution.py:42
  182.9 6.0 %shard_map.331 = (f32[512,768]{1,0:T(8,128)S(1)}, bf16[512,768]{1,0:T(8,128)(2,1)S(1)}, f32[8,768]{1,0:T(8,128)S(1)}, bf16[2,16,48,768]{3,2,1,0:T(8,128)(2,1)S(1)}, bf16[2,16,48,768]{3,2,1,0:T(8,128)(2,1)}) custom-call(s32[3]{0:T(128)S(1)} %pad_add_fusion.2.info_ref, f32[16,768]{1,0:T(8,128)S(1)} %get-tuple-element.255.vec_ref.shift_ref.gain_ref, ...), custom_call_target="tpu_custom_call" | custom-call | flops 2415919104 | bytes 14155776 | tf_op jit(solution)/shard_map/pallas_call | solution.py:73
  191.5 1.9 copy-done.53
  194.5 7.4 %shard_map.332 = (bf16[512,3072]{1,0:T(8,128)(2,1)S(1)}, f32[8,3072]{1,0:T(8,128)S(1)}, bf16[2,768,768]{2,1,0:T(8,128)(2,1)S(1)}, bf16[2,768,768]{2,1,0:T(8,128)(2,1)S(1)}) custom-call(s32[3]{0:T(128)S(1)} %pad_add_fusion.2.info_ref, bf16[512,768]{1,0:T(8,128)(2,1)S(1)} %get-tuple-element.307.grad_low_ref, bf16[512,3072]{1,0:T(8,128)(2,1)S(1)} %copy-done.53, ...), custom_call_target="tpu_custom_call" | custom-call | flops 4831838208 | bytes 21233664 | tf_op jit(solution)/shard_map/pallas_call | solution.py:73
  206.7 1.9 copy-done.1
  211.1 4.3 %shard_map.334 = (f32[512,768]{1,0:T(8,128)S(1)}, f32[8,768]{1,0:T(8,128)S(1)}) custom-call(s32[3]{0:T(128)S(1)} %pad_add_fusion.2.info_ref, f32[16,768]{1,0:T(8,128)S(1)} %get-tuple-element.255.vec_ref.shift_ref.gain_ref, f32[512,768]{1,0:T(8,128)S(1)} %copy-done.5, f32[512,768]{1,0:T(8,128)S(1)} %copy-done.7, bf16[512,3072]{1,0:T(8,128)(2,1)S(1)} %copy-done.1, ...), custom_call_target="tpu_custom_call" | custom-call | flops 2415919104 | bytes 12582912 | tf_op jit(solution)/shard_map/pallas_call | solution.py:73
  215.4 5.8 %collective-permute-done.30.refs_3_ = bf16[4,2,96,768]{3,2,1,0:T(8,128)(2,1)S(1)} collective-permute-done((bf16[4,2,96,768]{3,2,1,0:T(8,128)(2,1)S(1)}, bf16[4,2,96,768]{3,2,1,0:T(8,128)(2,1)S(1)}, u32[]{:S(2)}, u32[]{:S(2)}) %collective-permute-start.30) | collective-permute-done | bytes 1179680 | tf_op jit(solution)/shard_map/ppermute | solution.py:56
  226.0 11.2 %shard_map.337 = (bf16[512,768]{1,0:T(8,128)(2,1)S(1)}, bf16[512,768]{1,0:T(8,128)(2,1)S(1)}, bf16[512,768]{1,0:T(8,128)(2,1)S(1)}, f32[8,768]{1,0:T(8,128)S(1)}...) custom-call(s32[3]{0:T(128)S(1)} %pad_add_fusion.2.info_ref, s32[4]{0:T(128)S(1)} %pad_add_fusion.3.counts_ref, ...), custom_call_target="tpu_custom_call" | custom-call | flops 4227858432 | bytes 14942208 | tf_op jit(solution)/shard_map/pallas_call | solution.py:73
  237.2 9.6 %collective-permute-done.32.received = bf16[4,144,768]{2,1,0:T(8,128)(2,1)S(1)} collective-permute-done((bf16[4,144,768]{2,1,0:T(8,128)(2,1)S(1)}, bf16[4,144,768]{2,1,0:T(8,128)(2,1)S(1)}, u32[]{:S(2)}, u32[]{:S(2)}) %collective-permute-start.32) | collective-permute-done | bytes 884768 | tf_op jit(solution)/shard_map/ppermute | solution.py:56
  250.8 3.7 %shard_map.339 = (f32[512,768]{1,0:T(8,128)S(1)}, f32[8,768]{1,0:T(8,128)S(1)}) custom-call(s32[3]{0:T(128)S(1)} %pad_add_fusion.2.info_ref, f32[16,768]{1,0:T(8,128)S(1)} %get-tuple-element.255.vec_ref.shift_ref.gain_ref, f32[512,768]{1,0:T(8,128)S(1)} %get-tuple-element.328.grad_ref, bf16[512,768]{1,0:T(8,128)(2,1)S(1)} %get-tuple-element.344.refs_0_, ...), custom_call_target="tpu_custom_call" | custom-call | flops 1811939328 | bytes 11796480 | tf_op jit(solution)/shard_map/pallas_call | solution.py:73
  254.5 5.2 %collective-permute-done.34.received = bf16[4,96,768]{2,1,0:T(8,128)(2,1)S(1)} collective-permute-done((bf16[4,96,768]{2,1,0:T(8,128)(2,1)S(1)}, bf16[4,96,768]{2,1,0:T(8,128)(2,1)S(1)}, u32[]{:S(2)}, u32[]{:S(2)}) %collective-permute-start.34) | collective-permute-done | bytes 589856 | tf_op jit(solution)/shard_map/ppermute | solution.py:56
  262.8 2.0 collective-permute-start.37
  264.9 2.4 collective-permute-start.39
  267.3 12.2 %shard_map.342 = (bf16[512,768]{1,0:T(8,128)(2,1)S(1)}, bf16[512,768]{1,0:T(8,128)(2,1)S(1)}, bf16[512,768]{1,0:T(8,128)(2,1)S(1)}, f32[8,768]{1,0:T(8,128)S(1)}...) custom-call(s32[3]{0:T(128)S(1)} %pad_add_fusion.2.info_ref, s32[4]{0:T(128)S(1)} %pad_add_fusion.4.counts_ref, ...), custom_call_target="tpu_custom_call" | custom-call | flops 4227858432 | bytes 14942208 | tf_op jit(solution)/shard_map/pallas_call | solution.py:73
  279.5 5.3 %collective-permute-done.39.far_b = bf16[144,768]{1,0:T(8,128)(2,1)S(1)} collective-permute-done((bf16[144,768]{1,0:T(8,128)(2,1)S(1)}, bf16[144,768]{1,0:T(8,128)(2,1)S(1)}, u32[]{:S(2)}, u32[]{:S(2)}) %collective-permute-start.39) | collective-permute-done | bytes 221216 | tf_op jit(solution)/shard_map/ppermute | solution.py:42
  288.4 3.2 collective-permute-start.44
  292.0 4.0 %shard_map.343 = (f32[256,768]{1,0:T(8,128)S(1)}, f32[256,768]{1,0:T(8,128)S(1)}, bf16[512,768]{1,0:T(8,128)(2,1)}) custom-call(s32[3]{0:T(128)S(1)} %pad_add_fusion.2.info_ref, f32[16,768]{1,0:T(8,128)S(1)} %get-tuple-element.255.vec_ref.shift_ref.gain_ref, f32[512,768]{1,0:T(8,128)S(1)} %get-tuple-element.358.grad_ref, ...), custom_call_target="tpu_custom_call" | custom-call | flops 1811939328 | bytes 11796480 | tf_op jit(solution)/shard_map/pallas_call | solution.py:73
  296.0 5.3 %collective-permute-done.43.far_a = bf16[96,768]{1,0:T(8,128)(2,1)S(1)} collective-permute-done((bf16[96,768]{1,0:T(8,128)(2,1)S(1)}, bf16[96,768]{1,0:T(8,128)(2,1)S(1)}, u32[]{:S(2)}, u32[]{:S(2)}) %collective-permute-start.43) | collective-permute-done | bytes 147488 | tf_op jit(solution)/shard_map/ppermute | solution.py:42
  303.7 2.7 collective-permute-start.46
  306.4 1.8 collective-permute-start.48
  308.8 3.6 collective-permute-done.46.near_b
  312.3 2.8 collective-permute-done.47.far_a
  315.2 4.2 %collective-permute-done.48.far_b = bf16[96,768]{1,0:T(8,128)(2,1)S(1)} collective-permute-done((bf16[96,768]{1,0:T(8,128)(2,1)S(1)}, bf16[96,768]{1,0:T(8,128)(2,1)S(1)}, u32[]{:S(2)}, u32[]{:S(2)}) %collective-permute-start.48) | collective-permute-done | bytes 147488 | tf_op jit(solution)/shard_map/ppermute | solution.py:42
  320.8 1.7 shard_map.349
  328.5 1.8 shard_map.353
  330.2 3.3 collective-permute-done.49.received
  334.3 2.5 collective-permute-start.53
  336.8 2.0 collective-permute-start.55
  343.5 3.3 collective-permute-done.54.far_a
  346.9 4.3 %collective-permute-done.55.far_b = bf16[112,768]{1,0:T(8,128)(2,1)S(1)} collective-permute-done((bf16[112,768]{1,0:T(8,128)(2,1)S(1)}, bf16[112,768]{1,0:T(8,128)(2,1)S(1)}, u32[]{:S(2)}, u32[]{:S(2)}) %collective-permute-start.55) | collective-permute-done | bytes 172064 | tf_op jit(solution)/shard_map/ppermute | solution.py:42
  (316 shorter events, 96.1 us)
Async XLA Ops:
  4.5 19.3 %collective-permute-start.1 = (bf16[112,768]{1,0:T(8,128)(2,1)S(1)}, bf16[112,768]{1,0:T(8,128)(2,1)S(1)}, u32[]{:S(2)}, u32[]{:S(2)}) collective-permute-start(bf16[112,768]{1,0:T(8,128)(2,1)S(1)} %get-tuple-element.482), channel_id=1, source_target_pairs={{0,16},{1,17},{2,18},{3,19},{4,20},{5,21},{6,22},{7,23},{8,24},{9,... | collective-permute-start | bytes 516104 | tf_op jit(solution)/shard_map/ppermute | solution.py:42
  8.6 15.2 %collective-permute-start = (bf16[112,768]{1,0:T(8,128)(2,1)S(1)}, bf16[112,768]{1,0:T(8,128)(2,1)S(1)}, u32[]{:S(2)}, u32[]{:S(2)}) collective-permute-start(bf16[112,768]{1,0:T(8,128)(2,1)S(1)} %get-tuple-element.482), channel_id=1, source_target_pairs={{0,8},{1,9},{2,10},{3,11},{4,12},{5,13},{6,14},{7,15},{8,0},{9,1},... | collective-permute-start | bytes 516104 | tf_op jit(solution)/shard_map/ppermute | solution.py:42
  10.2 13.6 %collective-permute-start.2 = (bf16[112,768]{1,0:T(8,128)(2,1)S(1)}, bf16[112,768]{1,0:T(8,128)(2,1)S(1)}, u32[]{:S(2)}, u32[]{:S(2)}) collective-permute-start(bf16[112,768]{1,0:T(8,128)(2,1)S(1)} %get-tuple-element.239.refs_0_), channel_id=1, source_target_pairs={{0,24},{1,25},{2,26},{3,27},{4,28},{5,29},{6,30},{7,31},{8,16},{9,... | collective-permute-start | bytes 516104 | tf_op jit(solution)/shard_map/ppermute | solution.py:42
  10.4 13.4 %collective-permute-start.3 = (bf16[96,768]{1,0:T(8,128)(2,1)S(1)}, bf16[96,768]{1,0:T(8,128)(2,1)S(1)}, u32[]{:S(2)}, u32[]{:S(2)}) collective-permute-start(bf16[96,768]{1,0:T(8,128)(2,1)S(1)} %get-tuple-element.485), channel_id=1, source_target_pairs={{0,8},{1,9},{2,10},{3,11},{4,12},{5,13},{6,14},{7,15},{8,0},{9,1},... | collective-permute-start | bytes 442376 | tf_op jit(solution)/shard_map/ppermute | solution.py:42
  24.4 20.5 %collective-permute-start.4 = (bf16[4,112,768]{2,1,0:T(8,128)(2,1)S(1)}, bf16[4,112,768]{2,1,0:T(8,128)(2,1)S(1)}, u32[]{:S(2)}, u32[]{:S(2)}) collective-permute-start(bf16[4,112,768]{2,1,0:T(8,128)(2,1)S(1)} %shard_map.314.mine), channel_id=1, source_target_pairs={{0,2},{1,5},{2,0},{3,7},{4,6},{5,1},{6,4},{7,3},{8,10},{9,13},{10,... | collective-permute-start | bytes 2064392 | tf_op jit(solution)/shard_map/ppermute | solution.py:56
  26.0 18.9 %collective-permute-start.6 = (bf16[240,768]{1,0:T(8,128)(2,1)S(1)}, bf16[240,768]{1,0:T(8,128)(2,1)S(1)}, u32[]{:S(2)}, u32[]{:S(2)}) collective-permute-start(bf16[240,768]{1,0:T(8,128)(2,1)S(1)} %pad_maximum_fusion.3), channel_id=1, source_target_pairs={{0,8},{1,9},{2,10},{3,11},{4,12},{5,13},{6,14},{7,15},{8,0},{9,1},... | collective-permute-start | bytes 1105928 | tf_op jit(solution)/shard_map/ppermute | solution.py:42
  28.1 16.8 %collective-permute-start.5 = (bf16[2,96,768]{2,1,0:T(8,128)(2,1)S(1)}, bf16[2,96,768]{2,1,0:T(8,128)(2,1)S(1)}, u32[]{:S(2)}, u32[]{:S(2)}) collective-permute-start(bf16[2,96,768]{2,1,0:T(8,128)(2,1)S(1)} %shard_map.315.refs_0_), channel_id=1, source_target_pairs={{0,24},{1,25},{2,26},{3,27},{4,28},{5,29},{6,30},{7,31},{8,16},{9,... | collective-permute-start | bytes 884744 | tf_op jit(solution)/shard_map/ppermute | solution.py:42
  45.6 27.7 %collective-permute-start.8 = (bf16[4,2,112,768]{3,2,1,0:T(8,128)(2,1)S(1)}, bf16[4,2,112,768]{3,2,1,0:T(8,128)(2,1)S(1)}, u32[]{:S(2)}, u32[]{:S(2)}) collective-permute-start(bf16[4,2,112,768]{3,2,1,0:T(8,128)(2,1)S(1)} %shard_map.316.mine_ref.refs_3_), channel_id=1, source_target_pairs={{0,1},{1,0},{2,3},{3,2},{4,5},{5,4},{6,7},{7,6},{8,9},{9,8},{10,11... | collective-permute-start | bytes 4128776 | tf_op jit(solution)/shard_map/ppermute | solution.py:48
  45.6 27.7 %collective-permute-start.7 = (bf16[4,2,112,768]{3,2,1,0:T(8,128)(2,1)S(1)}, bf16[4,2,112,768]{3,2,1,0:T(8,128)(2,1)S(1)}, u32[]{:S(2)}, u32[]{:S(2)}) collective-permute-start(bf16[4,2,112,768]{3,2,1,0:T(8,128)(2,1)S(1)} %shard_map.316.mine_ref.refs_3_), channel_id=1, source_target_pairs={{0,4},{1,3},{2,6},{3,1},{4,0},{5,7},{6,2},{7,5},{8,12},{9,11},{10,... | collective-permute-start | bytes 4128776 | tf_op jit(solution)/shard_map/ppermute | solution.py:56
  46.2 27.1 %collective-permute-start.11 = (bf16[528,768]{1,0:T(8,128)(2,1)S(1)}, bf16[528,768]{1,0:T(8,128)(2,1)S(1)}, u32[]{:S(2)}, u32[]{:S(2)}) collective-permute-start(bf16[528,768]{1,0:T(8,128)(2,1)S(1)} %fusion.1), channel_id=1, source_target_pairs={{0,8},{1,9},{2,10},{3,11},{4,12},{5,13},{6,14},{7,15},{8,0},{9,1},... | collective-permute-start | bytes 2433032 | tf_op jit(solution)/shard_map/ppermute | solution.py:42
  46.8 24.9 %collective-permute-start.9 = (bf16[4,96,768]{2,1,0:T(8,128)(2,1)S(1)}, bf16[4,96,768]{2,1,0:T(8,128)(2,1)S(1)}, u32[]{:S(2)}, u32[]{:S(2)}) collective-permute-start(bf16[4,96,768]{2,1,0:T(8,128)(2,1)S(1)} %bitcast.99), channel_id=1, source_target_pairs={{0,2},{1,5},{2,0},{3,7},{4,6},{5,1},{6,4},{7,3},{8,10},{9,13},{10,... | collective-permute-start | bytes 1769480 | tf_op jit(solution)/shard_map/ppermute | solution.py:56
  49.0 22.7 %collective-permute-start.10 = (bf16[2,96,768]{2,1,0:T(8,128)(2,1)S(1)}, bf16[2,96,768]{2,1,0:T(8,128)(2,1)S(1)}, u32[]{:S(2)}, u32[]{:S(2)}) collective-permute-start(bf16[2,96,768]{2,1,0:T(8,128)(2,1)S(1)} %get-tuple-element.250.refs_0_), channel_id=1, source_target_pairs={{0,24},{1,25},{2,26},{3,27},{4,28},{5,29},{6,30},{7,31},{8,16},{9,... | collective-permute-start | bytes 884744 | tf_op jit(solution)/shard_map/ppermute | solution.py:42
  74.1 18.2 %collective-permute-start.14 = (bf16[4,2,96,768]{3,2,1,0:T(8,128)(2,1)S(1)}, bf16[4,2,96,768]{3,2,1,0:T(8,128)(2,1)S(1)}, u32[]{:S(2)}, u32[]{:S(2)}) collective-permute-start(bf16[4,2,96,768]{3,2,1,0:T(8,128)(2,1)S(1)} %shard_map.321.refs_2_.refs_1_.refs_4_), channel_id=1, source_target_pairs={{0,1},{1,0},{2,3},{3,2},{4,5},{5,4},{6,7},{7,6},{8,9},{9,8},{10,11... | collective-permute-start | bytes 3538952 | tf_op jit(solution)/shard_map/ppermute | solution.py:48
  74.6 22.5 %collective-permute-start.13 = (bf16[4,2,96,768]{3,2,1,0:T(8,128)(2,1)S(1)}, bf16[4,2,96,768]{3,2,1,0:T(8,128)(2,1)S(1)}, u32[]{:S(2)}, u32[]{:S(2)}) collective-permute-start(bf16[4,2,96,768]{3,2,1,0:T(8,128)(2,1)S(1)} %shard_map.321.refs_2_.refs_1_.refs_4_), channel_id=1, source_target_pairs={{0,4},{1,3},{2,6},{3,1},{4,0},{5,7},{6,2},{7,5},{8,12},{9,11},{10,... | collective-permute-start | bytes 3538952 | tf_op jit(solution)/shard_map/ppermute | solution.py:56
  76.0 16.3 %collective-permute-start.15 = (bf16[4,96,768]{2,1,0:T(8,128)(2,1)S(1)}, bf16[4,96,768]{2,1,0:T(8,128)(2,1)S(1)}, u32[]{:S(2)}, u32[]{:S(2)}) collective-permute-start(bf16[4,96,768]{2,1,0:T(8,128)(2,1)S(1)} %bitcast.97), channel_id=1, source_target_pairs={{0,2},{1,5},{2,0},{3,7},{4,6},{5,1},{6,4},{7,3},{8,10},{9,13},{10,... | collective-permute-start | bytes 1769480 | tf_op jit(solution)/shard_map/ppermute | solution.py:56
  77.6 13.6 %collective-permute-start.16 = (bf16[2,144,768]{2,1,0:T(8,128)(2,1)S(1)}, bf16[2,144,768]{2,1,0:T(8,128)(2,1)S(1)}, u32[]{:S(2)}, u32[]{:S(2)}) collective-permute-start(bf16[2,144,768]{2,1,0:T(8,128)(2,1)S(1)} %get-tuple-element.264.refs_0_), channel_id=1, source_target_pairs={{0,24},{1,25},{2,26},{3,27},{4,28},{5,29},{6,30},{7,31},{8,16},{9,... | collective-permute-start | bytes 1327112 | tf_op jit(solution)/shard_map/ppermute | solution.py:42
  97.7 24.7 %collective-permute-start.19 = (bf16[4,2,96,768]{3,2,1,0:T(8,128)(2,1)S(1)}, bf16[4,2,96,768]{3,2,1,0:T(8,128)(2,1)S(1)}, u32[]{:S(2)}, u32[]{:S(2)}) collective-permute-start(bf16[4,2,96,768]{3,2,1,0:T(8,128)(2,1)S(1)} %shard_map.324.refs_0_), channel_id=1, source_target_pairs={{0,1},{1,0},{2,3},{3,2},{4,5},{5,4},{6,7},{7,6},{8,9},{9,8},{10,11... | collective-permute-start | bytes 3538952 | tf_op jit(solution)/shard_map/ppermute | solution.py:48
  98.3 25.7 %collective-permute-start.18 = (bf16[4,2,96,768]{3,2,1,0:T(8,128)(2,1)S(1)}, bf16[4,2,96,768]{3,2,1,0:T(8,128)(2,1)S(1)}, u32[]{:S(2)}, u32[]{:S(2)}) collective-permute-start(bf16[4,2,96,768]{3,2,1,0:T(8,128)(2,1)S(1)} %shard_map.324.refs_0_), channel_id=1, source_target_pairs={{0,4},{1,3},{2,6},{3,1},{4,0},{5,7},{6,2},{7,5},{8,12},{9,11},{10,... | collective-permute-start | bytes 3538952 | tf_op jit(solution)/shard_map/ppermute | solution.py:56
  99.8 22.7 %collective-permute-start.20 = (bf16[4,144,768]{2,1,0:T(8,128)(2,1)S(1)}, bf16[4,144,768]{2,1,0:T(8,128)(2,1)S(1)}, u32[]{:S(2)}, u32[]{:S(2)}) collective-permute-start(bf16[4,144,768]{2,1,0:T(8,128)(2,1)S(1)} %bitcast.95), channel_id=1, source_target_pairs={{0,2},{1,5},{2,0},{3,7},{4,6},{5,1},{6,4},{7,3},{8,10},{9,13},{10,... | collective-permute-start | bytes 2654216 | tf_op jit(solution)/shard_map/ppermute | solution.py:56
  124.7 15.8 %collective-permute-start.23 = (bf16[4,2,144,768]{3,2,1,0:T(8,128)(2,1)S(1)}, bf16[4,2,144,768]{3,2,1,0:T(8,128)(2,1)S(1)}, u32[]{:S(2)}, u32[]{:S(2)}) collective-permute-start(bf16[4,2,144,768]{3,2,1,0:T(8,128)(2,1)S(1)} %shard_map.327.refs_0_), channel_id=1, source_target_pairs={{0,1},{1,0},{2,3},{3,2},{4,5},{5,4},{6,7},{7,6},{8,9},{9,8},{10,11... | collective-permute-start | bytes 5308424 | tf_op jit(solution)/shard_map/ppermute | solution.py:48
  124.8 22.6 %collective-permute-start.22 = (bf16[4,2,144,768]{3,2,1,0:T(8,128)(2,1)S(1)}, bf16[4,2,144,768]{3,2,1,0:T(8,128)(2,1)S(1)}, u32[]{:S(2)}, u32[]{:S(2)}) collective-permute-start(bf16[4,2,144,768]{3,2,1,0:T(8,128)(2,1)S(1)} %shard_map.327.refs_0_), channel_id=1, source_target_pairs={{0,4},{1,3},{2,6},{3,1},{4,0},{5,7},{6,2},{7,5},{8,12},{9,11},{10,... | collective-permute-start | bytes 5308424 | tf_op jit(solution)/shard_map/ppermute | solution.py:56
  155.5 11.2 %collective-permute-start.25 = (bf16[256,768]{1,0:T(8,128)(2,1)S(1)}, bf16[256,768]{1,0:T(8,128)(2,1)S(1)}, u32[]{:S(2)}, u32[]{:S(2)}) collective-permute-start(bf16[256,768]{1,0:T(8,128)(2,1)S(1)} %get-tuple-element.289), channel_id=1, source_target_pairs={{0,8},{1,9},{2,10},{3,11},{4,12},{5,13},{6,14},{7,15},{8,0},{9,1},... | collective-permute-start | bytes 1179656 | tf_op jit(solution)/shard_map/ppermute | solution.py:42
  171.3 11.5 %collective-permute-start.27 = (bf16[256,768]{1,0:T(8,128)(2,1)S(1)}, bf16[256,768]{1,0:T(8,128)(2,1)S(1)}, u32[]{:S(2)}, u32[]{:S(2)}) collective-permute-start(bf16[256,768]{1,0:T(8,128)(2,1)S(1)} %get-tuple-element.294), channel_id=1, source_target_pairs={{0,8},{1,9},{2,10},{3,11},{4,12},{5,13},{6,14},{7,15},{8,0},{9,1},... | collective-permute-start | bytes 1179656 | tf_op jit(solution)/shard_map/ppermute | solution.py:42
  175.8 14.8 %collective-permute-start.28 = (bf16[4,2,48,768]{3,2,1,0:T(8,128)(2,1)S(1)}, bf16[4,2,48,768]{3,2,1,0:T(8,128)(2,1)S(1)}, u32[]{:S(2)}, u32[]{:S(2)}) collective-permute-start(bf16[4,2,48,768]{3,2,1,0:T(8,128)(2,1)S(1)} %get-tuple-element.296), channel_id=1, source_target_pairs={{0,4},{1,3},{2,6},{3,1},{4,0},{5,7},{6,2},{7,5},{8,12},{9,11},{10,... | collective-permute-start | bytes 1769480 | tf_op jit(solution)/shard_map/ppermute | solution.py:56
  191.5 11.8 %collective-permute-start.29 = (bf16[2,16,48,768]{3,2,1,0:T(8,128)(2,1)}, bf16[2,16,48,768]{3,2,1,0:T(8,128)(2,1)S(1)}, u32[]{:S(2)}, u32[]{:S(2)}) collective-permute-start(bf16[2,16,48,768]{3,2,1,0:T(8,128)(2,1)} %get-tuple-element.306), channel_id=1, source_target_pairs={{0,1},{1,0},{2,3},{3,2},{4,5},{5,4},{6,7},{7,6},{8,9},{9,8},{10,11... | collective-permute-start | bytes 7077896 | tf_op jit(solution)/shard_map/ppermute | solution.py:48
  203.3 17.9 %collective-permute-start.31 = (bf16[2,16,48,768]{3,2,1,0:T(8,128)(2,1)}, bf16[2,16,48,768]{3,2,1,0:T(8,128)(2,1)S(1)}, u32[]{:S(2)}, u32[]{:S(2)}) collective-permute-start(bf16[2,16,48,768]{3,2,1,0:T(8,128)(2,1)} %bitcast.114), channel_id=1, source_target_pairs={{0,1},{1,0},{2,3},{3,2},{4,5},{5,4},{6,7},{7,6},{8,9},{9,8},{10,11... | collective-permute-start | bytes 7077896 | tf_op jit(solution)/shard_map/ppermute | solution.py:48
  205.0 16.3 %collective-permute-start.30 = (bf16[4,2,96,768]{3,2,1,0:T(8,128)(2,1)S(1)}, bf16[4,2,96,768]{3,2,1,0:T(8,128)(2,1)S(1)}, u32[]{:S(2)}, u32[]{:S(2)}) collective-permute-start(bf16[4,2,96,768]{3,2,1,0:T(8,128)(2,1)S(1)} %get-tuple-element.314), channel_id=1, source_target_pairs={{0,4},{1,3},{2,6},{3,1},{4,0},{5,7},{6,2},{7,5},{8,12},{9,11},{10,... | collective-permute-start | bytes 3538952 | tf_op jit(solution)/shard_map/ppermute | solution.py:56
  222.4 25.7 %collective-permute-start.33 = (bf16[4,2,96,768]{3,2,1,0:T(8,128)(2,1)S(1)}, bf16[4,2,96,768]{3,2,1,0:T(8,128)(2,1)S(1)}, u32[]{:S(2)}, u32[]{:S(2)}) collective-permute-start(bf16[4,2,96,768]{3,2,1,0:T(8,128)(2,1)S(1)} %get-tuple-element.327), channel_id=1, source_target_pairs={{0,4},{1,3},{2,6},{3,1},{4,0},{5,7},{6,2},{7,5},{8,12},{9,11},{10,... | collective-permute-start | bytes 3538952 | tf_op jit(solution)/shard_map/ppermute | solution.py:56
  224.5 22.3 %collective-permute-start.32 = (bf16[4,144,768]{2,1,0:T(8,128)(2,1)S(1)}, bf16[4,144,768]{2,1,0:T(8,128)(2,1)S(1)}, u32[]{:S(2)}, u32[]{:S(2)}) collective-permute-start(bf16[4,144,768]{2,1,0:T(8,128)(2,1)S(1)} %get-tuple-element.323), channel_id=1, source_target_pairs={{0,2},{1,5},{2,0},{3,7},{4,6},{5,1},{6,4},{7,3},{8,10},{9,13},{10,... | collective-permute-start | bytes 2654216 | tf_op jit(solution)/shard_map/ppermute | solution.py:56
  248.2 11.5 %collective-permute-start.35 = (bf16[2,16,48,768]{3,2,1,0:T(8,128)(2,1)S(1)}, bf16[2,16,48,768]{3,2,1,0:T(8,128)(2,1)S(1)}, u32[]{:S(2)}, u32[]{:S(2)}) collective-permute-start(bf16[2,16,48,768]{3,2,1,0:T(8,128)(2,1)S(1)} %bitcast.113), channel_id=1, source_target_pairs={{0,1},{1,0},{2,3},{3,2},{4,5},{5,4},{6,7},{7,6},{8,9},{9,8},{10,11... | collective-permute-start | bytes 7077896 | tf_op jit(solution)/shard_map/ppermute | solution.py:48
  249.8 9.9 %collective-permute-start.34 = (bf16[4,96,768]{2,1,0:T(8,128)(2,1)S(1)}, bf16[4,96,768]{2,1,0:T(8,128)(2,1)S(1)}, u32[]{:S(2)}, u32[]{:S(2)}) collective-permute-start(bf16[4,96,768]{2,1,0:T(8,128)(2,1)S(1)} %get-tuple-element.342), channel_id=1, source_target_pairs={{0,2},{1,5},{2,0},{3,7},{4,6},{5,1},{6,4},{7,3},{8,10},{9,13},{10,... | collective-permute-start | bytes 1769480 | tf_op jit(solution)/shard_map/ppermute | solution.py:56
  260.9 23.9 %collective-permute-start.36 = (bf16[4,2,96,768]{3,2,1,0:T(8,128)(2,1)S(1)}, bf16[4,2,96,768]{3,2,1,0:T(8,128)(2,1)S(1)}, u32[]{:S(2)}, u32[]{:S(2)}) collective-permute-start(bf16[4,2,96,768]{3,2,1,0:T(8,128)(2,1)S(1)} %get-tuple-element.351), channel_id=1, source_target_pairs={{0,4},{1,3},{2,6},{3,1},{4,0},{5,7},{6,2},{7,5},{8,12},{9,11},{10,... | collective-permute-start | bytes 3538952 | tf_op jit(solution)/shard_map/ppermute | solution.py:56
  262.8 16.7 %collective-permute-start.37 = (bf16[144,768]{1,0:T(8,128)(2,1)S(1)}, bf16[144,768]{1,0:T(8,128)(2,1)S(1)}, u32[]{:S(2)}, u32[]{:S(2)}) collective-permute-start(bf16[144,768]{1,0:T(8,128)(2,1)S(1)} %get-tuple-element.355), channel_id=1, source_target_pairs={{0,24},{1,25},{2,26},{3,27},{4,28},{5,29},{6,30},{7,31},{8,16},{9,... | collective-permute-start | bytes 663560 | tf_op jit(solution)/shard_map/ppermute | solution.py:42
  264.8 14.8 %collective-permute-start.38 = (bf16[144,768]{1,0:T(8,128)(2,1)S(1)}, bf16[144,768]{1,0:T(8,128)(2,1)S(1)}, u32[]{:S(2)}, u32[]{:S(2)}) collective-permute-start(bf16[144,768]{1,0:T(8,128)(2,1)S(1)} %get-tuple-element.356), channel_id=1, source_target_pairs={{0,8},{1,9},{2,10},{3,11},{4,12},{5,13},{6,14},{7,15},{8,0},{9,1},... | collective-permute-start | bytes 663560 | tf_op jit(solution)/shard_map/ppermute | solution.py:42
  264.9 19.9 %collective-permute-start.39 = (bf16[144,768]{1,0:T(8,128)(2,1)S(1)}, bf16[144,768]{1,0:T(8,128)(2,1)S(1)}, u32[]{:S(2)}, u32[]{:S(2)}) collective-permute-start(bf16[144,768]{1,0:T(8,128)(2,1)S(1)} %get-tuple-element.357), channel_id=1, source_target_pairs={{0,16},{1,17},{2,18},{3,19},{4,20},{5,21},{6,22},{7,23},{8,24},{9,... | collective-permute-start | bytes 663560 | tf_op jit(solution)/shard_map/ppermute | solution.py:42
  284.8 16.4 %collective-permute-start.40 = (bf16[2,16,48,768]{3,2,1,0:T(8,128)(2,1)S(1)}, bf16[2,16,48,768]{3,2,1,0:T(8,128)(2,1)S(1)}, u32[]{:S(2)}, u32[]{:S(2)}) collective-permute-start(bf16[2,16,48,768]{3,2,1,0:T(8,128)(2,1)S(1)} %bitcast.112), channel_id=1, source_target_pairs={{0,1},{1,0},{2,3},{3,2},{4,5},{5,4},{6,7},{7,6},{8,9},{9,8},{10,11... | collective-permute-start | bytes 7077896 | tf_op jit(solution)/shard_map/ppermute | solution.py:48
  285.7 15.5 %collective-permute-start.41 = (bf16[4,96,768]{2,1,0:T(8,128)(2,1)S(1)}, bf16[4,96,768]{2,1,0:T(8,128)(2,1)S(1)}, u32[]{:S(2)}, u32[]{:S(2)}) collective-permute-start(bf16[4,96,768]{2,1,0:T(8,128)(2,1)S(1)} %get-tuple-element.377), channel_id=1, source_target_pairs={{0,2},{1,5},{2,0},{3,7},{4,6},{5,1},{6,4},{7,3},{8,10},{9,13},{10,... | collective-permute-start | bytes 1769480 | tf_op jit(solution)/shard_map/ppermute | solution.py:56
  287.2 8.8 %collective-permute-start.42 = (bf16[96,768]{1,0:T(8,128)(2,1)S(1)}, bf16[96,768]{1,0:T(8,128)(2,1)S(1)}, u32[]{:S(2)}, u32[]{:S(2)}) collective-permute-start(bf16[96,768]{1,0:T(8,128)(2,1)S(1)} %get-tuple-element.381), channel_id=1, source_target_pairs={{0,24},{1,25},{2,26},{3,27},{4,28},{5,29},{6,30},{7,31},{8,16},{9,... | collective-permute-start | bytes 442376 | tf_op jit(solution)/shard_map/ppermute | solution.py:42
  288.4 12.9 %collective-permute-start.43 = (bf16[96,768]{1,0:T(8,128)(2,1)S(1)}, bf16[96,768]{1,0:T(8,128)(2,1)S(1)}, u32[]{:S(2)}, u32[]{:S(2)}) collective-permute-start(bf16[96,768]{1,0:T(8,128)(2,1)S(1)} %get-tuple-element.382), channel_id=1, source_target_pairs={{0,8},{1,9},{2,10},{3,11},{4,12},{5,13},{6,14},{7,15},{8,0},{9,1},... | collective-permute-start | bytes 442376 | tf_op jit(solution)/shard_map/ppermute | solution.py:42
  288.4 12.9 %collective-permute-start.44 = (bf16[96,768]{1,0:T(8,128)(2,1)S(1)}, bf16[96,768]{1,0:T(8,128)(2,1)S(1)}, u32[]{:S(2)}, u32[]{:S(2)}) collective-permute-start(bf16[96,768]{1,0:T(8,128)(2,1)S(1)} %get-tuple-element.383), channel_id=1, source_target_pairs={{0,16},{1,17},{2,18},{3,19},{4,20},{5,21},{6,22},{7,23},{8,24},{9,... | collective-permute-start | bytes 442376 | tf_op jit(solution)/shard_map/ppermute | solution.py:42
  302.4 18.4 %collective-permute-start.45 = (bf16[4,2,112,768]{3,2,1,0:T(8,128)(2,1)S(1)}, bf16[4,2,112,768]{3,2,1,0:T(8,128)(2,1)S(1)}, u32[]{:S(2)}, u32[]{:S(2)}) collective-permute-start(bf16[4,2,112,768]{3,2,1,0:T(8,128)(2,1)S(1)} %get-tuple-element.398), channel_id=1, source_target_pairs={{0,4},{1,3},{2,6},{3,1},{4,0},{5,7},{6,2},{7,5},{8,12},{9,11},{10,... | collective-permute-start | bytes 4128776 | tf_op jit(solution)/shard_map/ppermute | solution.py:56
  306.4 8.8 %collective-permute-start.47 = (bf16[96,768]{1,0:T(8,128)(2,1)S(1)}, bf16[96,768]{1,0:T(8,128)(2,1)S(1)}, u32[]{:S(2)}, u32[]{:S(2)}) collective-permute-start(bf16[96,768]{1,0:T(8,128)(2,1)S(1)} %get-tuple-element.403), channel_id=1, source_target_pairs={{0,8},{1,9},{2,10},{3,11},{4,12},{5,13},{6,14},{7,15},{8,0},{9,1},... | collective-permute-start | bytes 442376 | tf_op jit(solution)/shard_map/ppermute | solution.py:42
  306.4 13.0 %collective-permute-start.48 = (bf16[96,768]{1,0:T(8,128)(2,1)S(1)}, bf16[96,768]{1,0:T(8,128)(2,1)S(1)}, u32[]{:S(2)}, u32[]{:S(2)}) collective-permute-start(bf16[96,768]{1,0:T(8,128)(2,1)S(1)} %get-tuple-element.404), channel_id=1, source_target_pairs={{0,16},{1,17},{2,18},{3,19},{4,20},{5,21},{6,22},{7,23},{8,24},{9,... | collective-permute-start | bytes 442376 | tf_op jit(solution)/shard_map/ppermute | solution.py:42
  308.1 26.2 %collective-permute-start.52 = (bf16[512,768]{1,0:T(8,128)(2,1)}, bf16[512,768]{1,0:T(8,128)(2,1)}, u32[]{:S(2)}, u32[]{:S(2)}) collective-permute-start(bf16[512,768]{1,0:T(8,128)(2,1)} %get-tuple-element.434), channel_id=1, source_target_pairs={{0,8},{1,9},{2,10},{3,11},{4,12},{5,13},{6,14},{7,15},{8,0},{9,1},... | collective-permute-start | bytes 2359304 | tf_op jit(solution)/shard_map/ppermute | solution.py:42
  322.4 11.1 %collective-permute-start.49 = (bf16[4,112,768]{2,1,0:T(8,128)(2,1)}, bf16[4,112,768]{2,1,0:T(8,128)(2,1)S(1)}, u32[]{:S(2)}, u32[]{:S(2)}) collective-permute-start(bf16[4,112,768]{2,1,0:T(8,128)(2,1)} %get-tuple-element.421), channel_id=1, source_target_pairs={{0,2},{1,5},{2,0},{3,7},{4,6},{5,1},{6,4},{7,3},{8,10},{9,13},{10,... | collective-permute-start | bytes 2064392 | tf_op jit(solution)/shard_map/ppermute | solution.py:56
  334.3 9.2 %collective-permute-start.53 = (bf16[112,768]{1,0:T(8,128)(2,1)S(1)}, bf16[112,768]{1,0:T(8,128)(2,1)S(1)}, u32[]{:S(2)}, u32[]{:S(2)}) collective-permute-start(bf16[112,768]{1,0:T(8,128)(2,1)S(1)} %get-tuple-element.436), channel_id=1, source_target_pairs={{0,24},{1,25},{2,26},{3,27},{4,28},{5,29},{6,30},{7,31},{8,16},{9,... | collective-permute-start | bytes 516104 | tf_op jit(solution)/shard_map/ppermute | solution.py:42
  336.8 10.1 %collective-permute-start.54 = (bf16[112,768]{1,0:T(8,128)(2,1)S(1)}, bf16[112,768]{1,0:T(8,128)(2,1)S(1)}, u32[]{:S(2)}, u32[]{:S(2)}) collective-permute-start(bf16[112,768]{1,0:T(8,128)(2,1)S(1)} %get-tuple-element.437), channel_id=1, source_target_pairs={{0,8},{1,9},{2,10},{3,11},{4,12},{5,13},{6,14},{7,15},{8,0},{9,1},... | collective-permute-start | bytes 516104 | tf_op jit(solution)/shard_map/ppermute | solution.py:42
  336.8 14.4 %collective-permute-start.55 = (bf16[112,768]{1,0:T(8,128)(2,1)S(1)}, bf16[112,768]{1,0:T(8,128)(2,1)S(1)}, u32[]{:S(2)}, u32[]{:S(2)}) collective-permute-start(bf16[112,768]{1,0:T(8,128)(2,1)S(1)} %get-tuple-element.438), channel_id=1, source_target_pairs={{0,16},{1,17},{2,18},{3,19},{4,20},{5,21},{6,22},{7,23},{8,24},{9,... | collective-permute-start | bytes 516104 | tf_op jit(solution)/shard_map/ppermute | solution.py:42
  (91 other events, 514.6 us)
where the time goes:
time: 366 us; the launch traced here: 359 us
  waiting for transfers between devices  159 us (43%)
  Pallas kernels  107 us (29%)
  starting transfers between devices  54.2 us (15%)
  local copies, waits for them, and re-layouts  30.2 us (8%)
  other arithmetic  5.92 us (2%)
    pallas_call x46, Pallas kernels, call(): pl.pallas_call(kernel, out_shape=[jax.ShapeDtypeStruct(shape, dtype) for...  107 us
    ppermute x24, waiting for transfers between devices, across(): return lax.ppermute(values, AXES, pairs)  94.5 us
    ppermute x17, waiting for transfers between devices, hop(): return lax.ppermute(values, AXES, pairs)  52 us
    ppermute x24, starting transfers between devices, across(): return lax.ppermute(values, AXES, pairs)  34.9 us
    unnamed x167, local copies, waits for them, and re-layouts  27.6 us
    ppermute x17, starting transfers between devices, hop(): return lax.ppermute(values, AXES, pairs)  16.3 us
    ppermute x17, waiting for transfers between devices, swap_cores(): return lax.ppermute(values, AXES, pairs)  12.7 us
  transfers between devices with their start and end apart: 58, of which 30 were waited for; matrix products, arithmetic and copies ran while one was open for 1% of the time, Pallas kernels for 25%

commit v1 on v0

--- a/solution.py
+++ b/solution.py
@@ -13,7 +13,7 @@
 bf16 = jnp.bfloat16
 f32 = jnp.float32
 AXES = ("dp", "rep")
-VMEM_LIMIT = 32 << 20
+VMEM_LIMIT = 27 << 20
 GLUE_LIMIT = 20 << 20
 HBM = pl.BlockSpec(memory_space=pltpu.HBM)
 VMEM = pl.BlockSpec(memory_space=pltpu.VMEM)
@@ -175,19 +175,32 @@
     return received, place
 
 
+def join_all_kernel(grid, info_ref, mine, first_away, second_away, both_away, out):
+    unused, first, second, unused, unused = grid.place(info_ref)
+    for g in range(4):
+        out[g, second, first] = mine[g]
+        out[g, second, 1 - first] = first_away[g]
+        out[g, 1 - second, first] = second_away[g]
+        out[g, 1 - second, 1 - first] = both_away[g]
+
+
 def second_hops(grid, held):
     if len(grid.orders[0]) == 2:
-        return [held, grid.hop(held, 0)]
+        return [held, grid.hop(held, 0), grid.hop(held, 1)]
     for step in range(len(grid.orders[0])):
         held = jnp.concatenate([held, grid.hop(held, step)], 0)
     return [held]
 
 
-def third_hops(grid, info, pieces):
+def third_hops(grid, pieces):
+    return pieces + [grid.hop(pieces[1], 1)] if len(pieces) == 3 else pieces
+
+
+def ahead(grid, info, pieces):
     if len(pieces) == 1:
-        return pieces
-    held = join_pair(grid, info, pieces)
-    return [held, grid.hop(held, 1), grid.swap_cores(held)]
+        return []
+    held = join_pair(grid, info, pieces[:2])
+    return [held, pieces[2], grid.swap_cores(held), grid.swap_cores(pieces[2])]
 
 
 def extra_rows(grid, info, pieces, start, keep):
@@ -201,9 +214,21 @@
     return ((masks ^ (info[2] & (grid.partner - 1))) | groups).reshape(-1)
 
 
-def whole(grid, info, pieces, rows, count):
-    if len(pieces) == 3:
-        return [pieces[0], pieces[1], pieces[2], grid.swap_cores(pieces[1])]
+def whole(grid, info, pieces, rows, count, early=()):
+    if early:
+        mine, away, mine_swapped, away_swapped = early
+        return [mine, away, pieces[3], mine_swapped, away_swapped, grid.swap_cores(pieces[3])]
+    if len(pieces) == 4:
+        shape = pieces[0].shape
+        held = call(
+            functools.partial(join_all_kernel, grid),
+            [((4, 2, 2) + shape[1:], bf16)],
+            [info] + pieces,
+            [SMEM] + [VMEM] * 4,
+            [VMEM],
+            room=GLUE_LIMIT,
+        )[0]
+        return [held, grid.swap_cores(held)]
     held = pieces[0][:, : count * rows]
     held = jnp.take(held, jnp.argsort(slots_of(grid, info)), axis=0).reshape(grid.n, count, rows, -1).transpose(1, 0, 2, 3)
     held = held.reshape(count, grid.n * rows, -1)
@@ -385,28 +410,43 @@
     def load(which, refs):
         count = 1 if only is not None else 2 if mixed else blocks.shape[0] // 2
         first = 0 if only is not None else which * count
-        if len(refs) == 1:
+        if len(refs[0].shape) == 3:
             for j in range(count):
                 pltpu.make_async_copy(refs[0].at[start + j], blocks.at[first + j], sem).start()
             return
         rows = blocks.shape[-2]
+        near = jnp.right_shift(info_ref[2], which) & 1
         bit = jnp.right_shift(info_ref[2], 1 - which) & 1
+
+        def copy(source, target):
+            pltpu.make_async_copy(source, target, sem).start()
+
+        def place(j, *at):
+            return blocks.at[at + (first + j,)] if mixed else blocks.at[(first + j,) + at]
+
+        every = slice(None)
         for j in range(count):
-            for ref, b in ((refs[0], bit), (refs[1], 1 - bit)):
-                source = ref.at[:, :, pl.ds((start + j) * rows, rows)]
-
-                def low_first(b=b, j=j, source=source):
-                    target = blocks.at[:, b, :, first + j] if mixed else blocks.at[first + j, :, b]
-                    pltpu.make_async_copy(source, target, sem).start()
-
-                def high_first(b=b, j=j, source=source):
-                    target = (
-                        blocks.at[:, :, b, first + j] if mixed else blocks.at[first + j, :, :, b]
-                    )
-                    pltpu.make_async_copy(source, target, sem).start()
-
-                pl.when(which == 0)(low_first)
-                pl.when(which != 0)(high_first)
+            cut = pl.ds((start + j) * rows, rows)
+
+            def low_first(j=j, cut=cut):
+                if len(refs) == 1:
+                    copy(refs[0].at[:, :, :, cut], place(j, every, every, every))
+                    return
+                copy(refs[0].at[:, :, cut], place(j, every, bit, every))
+                copy(refs[1].at[:, cut], place(j, every, 1 - bit, near))
+                copy(refs[2].at[:, cut], place(j, every, 1 - bit, 1 - near))
+
+            def high_first(j=j, cut=cut):
+                if len(refs) == 1:
+                    for b in range(2):
+                        copy(refs[0].at[:, b, :, cut], place(j, every, every, b))
+                    return
+                copy(refs[0].at[:, :, cut], place(j, every, every, bit))
+                copy(refs[1].at[:, cut], place(j, every, near, 1 - bit))
+                copy(refs[2].at[:, cut], place(j, every, 1 - near, 1 - bit))
+
+            pl.when(which == 0)(low_first)
+            pl.when(which != 0)(high_first)
 
     if len(sources) == 1:
         pltpu.make_async_copy(sources[0], blocks, sem).start()
@@ -1006,21 +1046,15 @@
     )
 
 
-def unlay_kernel(grid, start, info_ref, mine_ref, other_ref, table_ref, wide_ref, held, found, sem):
-    copies = []
-    for k, ref in enumerate((mine_ref, other_ref)):
-        source = ref.at[:, :, pl.ds(start, EXTRA)]
-        copies.append(pltpu.make_async_copy(source, held.at[k], sem.at[k]))
-    for copy in copies:
-        copy.start()
-    for copy in copies:
-        copy.wait()
-    unused, unused, second, first_step, second_step = grid.place(info_ref)
+def unlay_kernel(grid, start, info_ref, all_ref, table_ref, wide_ref, held, found, sem):
+    copy = pltpu.make_async_copy(all_ref.at[:, :, :, pl.ds(start, EXTRA)], held, sem)
+    copy.start()
+    copy.wait()
+    unused, unused, unused, first_step, second_step = grid.place(info_ref)
     for g in range(4):
-        for a in range(2):
-            for k, b in ((0, second), (1, 1 - second)):
-                place = 4 * g + a * first_step + b * second_step
-                found[place] = held[k, g, a].astype(f32)
+        for b in range(2):
+            for a in range(2):
+                found[4 * g + a * first_step + b * second_step] = held[g, b, a].astype(f32)
     rows = grid.rows
     for p in range(grid.n):
         for i, (row, lane, unused) in enumerate(SPOTS[:-1]):
@@ -1034,7 +1068,7 @@
 def unlay_vectors(grid, info, pieces, start):
     width = pieces[0].shape[-1]
     rows = grid.rows
-    if len(pieces) == 1:
+    if len(pieces[0].shape) == 3:
         found = extra_rows(grid, info, pieces, start, EXTRA).astype(f32)
         parts = [
             found[:, row, lane : lane + length * rows].reshape(-1) for row, lane, length in SPOTS
@@ -1044,13 +1078,13 @@
     return call(
         functools.partial(unlay_kernel, grid, start),
         [((16, width), f32), ((8, 4 * width), f32)],
-        [info] + pieces[:2],
-        [SMEM, HBM, HBM],
+        [info, pieces[0]],
+        [SMEM, HBM],
         [VMEM, VMEM],
         [
-            pltpu.VMEM((2, 4, 2, EXTRA, width), bf16),
+            pltpu.VMEM((4, 2, 2, EXTRA, width), bf16),
             pltpu.VMEM((grid.n, EXTRA, width), f32),
-            pltpu.SemaphoreType.DMA((2,)),
+            pltpu.SemaphoreType.DMA,
         ],
         room=GLUE_LIMIT,
     )
@@ -1162,19 +1196,19 @@
     u1, place_u = meet(grid, info, pair(info, grid.high_bit - 1, sent[1][0], u0)[0])
     later_far = grid.across(later[1], grid.partner)
     t2, u1, later_far, seen = tie(t2, u1, later_far, seen)
-    t3 = third_hops(grid, info, t2)
+    t3 = third_hops(grid, t2)
     u2 = second_hops(grid, place_u(u1))
     w0, x0 = pair(info, grid.high_bit - 1, later[0], later_far, parts)
     w1, place_w = meet(grid, info, w0)
     seen_far = grid.across(seen, grid.partner)
     t3, u2, w1, seen_far, x0 = tie(t3, u2, w1, seen_far, x0)
     cross_w = whole(grid, info, t3, rows, 2)
-    table, ffn_in_shift = unlay_vectors(grid, info, t3, 2 * rows)
+    table, ffn_in_shift = unlay_vectors(grid, info, cross_w if len(t3) == 4 else t3, 2 * rows)
     counts_far = seen_far[2 * pages * slots :, :pages][:2].astype(jnp.int32)
     counts = jnp.concatenate([own(counts_mine), own(counts_far)])
     other_counts = jnp.concatenate([other(counts_mine), other(counts_far)])
     inputs = [language, vision, seen_far]
-    u3 = third_hops(grid, info, u2)
+    u3 = third_hops(grid, u2)
     w2 = second_hops(grid, place_w(w1))
     x1, place_x = meet(grid, info, x0)
     cq, ck, cv, co, first_sum, first_norm, first_low = attend(
@@ -1182,7 +1216,7 @@
     )
     first_norm, first_low, u3, w2, x1 = tie(first_norm, first_low, u3, w2, x1)
     self_w = whole(grid, info, u3, rows, 2)
-    w3 = third_hops(grid, info, w2)
+    w3 = third_hops(grid, w2)
     x2 = second_hops(grid, place_x(x1))
     sq, sk, sv, so, second_sum, second_norm, second_low = attend(
         grid,
@@ -1197,10 +1231,11 @@
     )
     second_norm, second_low, w3, x2 = tie(second_norm, second_low, w3, x2)
     in_w = whole(grid, info, w3, rows, 2)
-    x3 = third_hops(grid, info, x2)
+    x3 = third_hops(grid, x2)
+    early = ahead(grid, info, x2)
     active, slope = hidden_layer(grid, info, ffn_in_shift, second_low, in_w)
-    active, second_norm, x3 = tie(active, second_norm, x3)
-    gate_w = out_w = whole(grid, info, x3, rows, 3)
+    active, second_norm, x3, early = tie(active, second_norm, x3, early)
+    gate_w = out_w = whole(grid, info, x3, rows, 3, early)
     if len(out_w) == 2:
         both = jnp.where(core == 0, jnp.stack(out_w), jnp.stack(out_w[::-1]))[:, :2]
         both = both.reshape(4, n, rows, width).transpose(1, 0, 2, 3)
@@ -1245,26 +1280,26 @@
     )
     outs, in_got, grad_second_sum = tie(outs, in_got, grad_second_sum)
     ins = first_returns(grid, info, in_keep, in_got)
-    outs = second_returns(grid, info, gate, outs)
+    outs = second_returns(grid, info, outs)
     *self_parts, vec_self, self_keep, self_send = scores_back(
         grid, False, slots, info, counts, grad_second_sum, [sq, sk, sv, so], [first_low], self_w
     )
     outs, ins, self_parts, self_keep, self_send = tie(outs, ins, self_parts, self_keep, self_send)
     self_keep, self_send = by_piece(self_keep), by_piece(self_send)
     self_got = grid.swap_cores(self_send)
-    ins = second_returns(grid, info, ins)
+    ins = second_returns(grid, info, gate, ins)
     outs = third_returns(grid, info, outs)
     grad_first_sum, vec_first = project_back(
         grid, False, info, table, grad_second_sum, self_parts, [first_sum], self_w
     )
-    ins, self_got, grad_first_sum = tie(ins, self_got, grad_first_sum)
+    ins, outs, self_got, grad_first_sum = tie(ins, outs, self_got, grad_first_sum)
     selfs = first_returns(grid, info, self_keep, self_got)
     ins = third_returns(grid, info, ins)
     *cross_parts, vec_cross, cross_keep, cross_send = scores_back(
         grid, True, slots, info, other_counts, grad_first_sum, [cq, ck, cv, co], inputs, cross_w
     )
-    selfs, outs, cross_parts, cross_keep, cross_send = tie(
-        selfs, outs, cross_parts, cross_keep, cross_send
+    selfs, ins, cross_parts, cross_keep, cross_send = tie(
+        selfs, ins, cross_parts, cross_keep, cross_send
     )
     cross_keep, cross_send = by_piece(cross_keep), by_piece(cross_send)
     cross_got = grid.swap_cores(cross_send)
@@ -1276,9 +1311,7 @@
     grad_mine, grad_theirs, outgoing = project_back(
         grid, True, info, table, grad_first_sum, cross_parts, [], cross_w
     )
-    cross_got, outgoing, selfs, ins, outs, grad_vec = tie(
-        cross_got, outgoing, selfs, ins, outs, grad_vec
-    )
+    cross_got, outgoing, selfs, outs, grad_vec = tie(cross_got, outgoing, selfs, outs, grad_vec)
     crosses = first_returns(grid, info, cross_keep, cross_got, grad_vec)
     incoming = grid.across(outgoing, grid.partner)
     selfs = third_returns(grid, info, selfs)
@@ -1308,26 +1341,26 @@
         return finish(info, done, layout, rows, [(2, 3, rows, width), (2, rows, width)])
 
     if rows % 16:
-        in_all = by_side(finished(in_done, 2)).transpose(0, 2, 1, 3).reshape(2, rows, 4 * width)
-        gate_all = finished(out_done, 1)
+        in_all = by_side(finished(in_done, 2, 1)).transpose(0, 2, 1, 3).reshape(2, rows, 4 * width)
+        gate_all = finished(in_done, 1)
         gate_both = sides(gate_all[0, 0] + gate_all[1, 1], gate_all[0, 1] + gate_all[1, 0])
-        out_all = by_side(finished(out_done, 2, 1)).reshape(2, 4 * rows, width)
+        out_all = by_side(finished(out_done, 2)).reshape(2, 4 * rows, width)
     else:
         every = slice(None)
         cuts = [(0, (every, slice(i * width, (i + 1) * width))) for i in range(4)]
-        in_all = finish(info, in_done, (cuts[:2], cuts[2:]), rows, [(2, rows, 4 * width)])[0]
+        layout = [[(1, ())] + cuts[:2], [(1, ())] + cuts[2:]]
+        in_all = finish(info, in_done, layout, rows, [(2, rows, 4 * width), (2, rows, width)])[0]
         gate_both = call(
             finish_gate_kernel,
             [((2, rows, width), f32)],
-            [info] + list(out_done),
+            [info] + list(in_done),
             [SMEM, VMEM, VMEM],
             [VMEM],
             room=GLUE_LIMIT,
         )[0]
-        places = [(1, ())] + [(0, (slice(i * rows, (i + 1) * rows),)) for i in range(4)]
-        layout = ((places[0], places[1], places[2]), (places[0], places[3], places[4]))
-        shapes = [(2, 4 * rows, width), (2, rows, width)]
-        out_all = finish(info, out_done, layout, rows, shapes)[0]
+        places = [(0, (slice(i * rows, (i + 1) * rows),)) for i in range(4)]
+        layout = (places[:2], places[2:])
+        out_all = finish(info, out_done, layout, rows, [(2, 4 * rows, width)])[0]
     crosses, in_all, out_all, gate_both = tie(crosses, in_all, out_all, gate_both)
     crosses = third_returns(grid, info, crosses)
     selfs, crosses[0], incoming = tie(selfs, crosses[0], incoming)

time: 366 us -> 349 us (0.954)
  local copies, waits for them, and re-layouts: 30.2 us -> 12.2 us
  starting transfers between devices: 54.2 us -> 60.1 us
  waiting for transfers between devices: 159 us -> 154 us
    unnamed x167 -> x119, local copies, waits for them, and re-layouts: 27.6 us -> 9.69 us
    ppermute x17 -> x21, starting transfers between devices: 16.3 us -> 21.3 us  [hop(): return lax.ppermute(values, AXES, pairs)]
    ppermute x17 -> x15, waiting for transfers between devices: 12.7 us -> 9.35 us  [swap_cores(): return lax.ppermute(values, AXES, pairs)]
    ppermute x17 -> x21, waiting for transfers between devices: 52 us -> 50.2 us  [hop(): return lax.ppermute(values, AXES, pairs)]
  transfers between devices with their start and end apart: 58 -> 60, of which waited for: 30 -> 32; matrix products, arithmetic and copies ran while one was open for 1% -> 1% of each run, Pallas kernels for 25% -> 27%
where the time goes in v1:
time: 349 us; the launch traced here: 342 us
  waiting for transfers between devices  154 us (44%)
  Pallas kernels  108 us (31%)
  starting transfers between devices  60.1 us (17%)
  local copies, waits for them, and re-layouts  12.2 us (3%)
  other arithmetic  5.87 us (2%)
    pallas_call x46, Pallas kernels, call(): pl.pallas_call(kernel, out_shape=[jax.ShapeDtypeStruct(shape, dtype) for...  108 us
    ppermute x24, waiting for transfers between devices, across(): return lax.ppermute(values, AXES, pairs)  94.2 us
    ppermute x21, waiting for transfers between devices, hop(): return lax.ppermute(values, AXES, pairs)  50.2 us
    ppermute x24, starting transfers between devices, across(): return lax.ppermute(values, AXES, pairs)  36.6 us
    ppermute x21, starting transfers between devices, hop(): return lax.ppermute(values, AXES, pairs)  21.3 us
    unnamed x119, local copies, waits for them, and re-layouts  9.69 us
    ppermute x15, waiting for transfers between devices, swap_cores(): return lax.ppermute(values, AXES, pairs)  9.35 us
  transfers between devices with their start and end apart: 60, of which 32 were waited for; matrix products, arithmetic and copies ran while one was open for 1% of the time, Pallas kernels for 27%

profile of v1, /device:TPU:0, one launch (start us, length us, event | category | flops | bytes accessed | tf_op | source)
XLA Modules:
  0.0 342.1 jit_solution(11955170801802099541)
XLA Ops:
  4.5 4.1 %collective-permute-start.1 = (bf16[112,768]{1,0:T(8,128)(2,1)S(1)}, bf16[112,768]{1,0:T(8,128)(2,1)S(1)}, u32[]{:S(2)}, u32[]{:S(2)}) collective-permute-start(bf16[112,768]{1,0:T(8,128)(2,1)S(1)} %get-tuple-element.500), channel_id=1, source_target_pairs={{0,16},{1,17},{2,18},{3,19},{4,20},{5,21},{6,22},{7,23},{8,24},{9,... | collective-permute-start | bytes 516104 | tf_op jit(solution)/shard_map/ppermute | solution.py:42
  12.2 11.6 %collective-permute-done.3.refs_1_ = bf16[96,768]{1,0:T(8,128)(2,1)S(1)} collective-permute-done((bf16[96,768]{1,0:T(8,128)(2,1)S(1)}, bf16[96,768]{1,0:T(8,128)(2,1)S(1)}, u32[]{:S(2)}, u32[]{:S(2)}) %collective-permute-start.3) | collective-permute-done | bytes 147488 | tf_op jit(solution)/shard_map/ppermute | solution.py:42
  29.6 2.9 collective-permute-start.6
  32.6 13.5 %collective-permute-done.6.refs_1_ = bf16[2,96,768]{2,1,0:T(8,128)(2,1)S(1)} collective-permute-done((bf16[2,96,768]{2,1,0:T(8,128)(2,1)S(1)}, bf16[2,96,768]{2,1,0:T(8,128)(2,1)S(1)}, u32[]{:S(2)}, u32[]{:S(2)}) %collective-permute-start.6) | collective-permute-done | bytes 294944 | tf_op jit(solution)/shard_map/ppermute | solution.py:42
  51.3 20.0 %collective-permute-done.11.refs_1_ = bf16[2,96,768]{2,1,0:T(8,128)(2,1)S(1)} collective-permute-done((bf16[2,96,768]{2,1,0:T(8,128)(2,1)S(1)}, bf16[2,96,768]{2,1,0:T(8,128)(2,1)S(1)}, u32[]{:S(2)}, u32[]{:S(2)}) %collective-permute-start.11) | collective-permute-done | bytes 294944 | tf_op jit(solution)/shard_map/ppermute | solution.py:42
  76.2 2.0 collective-permute-start.17
  78.3 7.8 %shard_map.320 = (bf16[512,768]{1,0:T(8,128)(2,1)S(1)}, bf16[512,768]{1,0:T(8,128)(2,1)S(1)}, bf16[512,768]{1,0:T(8,128)(2,1)S(1)}, bf16[512,768]{1,0:T(8,128)(2...) custom-call(s32[3]{0:T(128)S(1)} %pad_add_fusion.2.info_ref, ...), custom_call_target="tpu_custom_call" | custom-call | flops 2818572288 | bytes 12582912 | tf_op jit(solution)/shard_map/pallas_call | solution.py:73
  86.1 4.8 %collective-permute-done.17.refs_1_ = bf16[2,144,768]{2,1,0:T(8,128)(2,1)S(1)} collective-permute-done((bf16[2,144,768]{2,1,0:T(8,128)(2,1)S(1)}, bf16[2,144,768]{2,1,0:T(8,128)(2,1)S(1)}, u32[]{:S(2)}, u32[]{:S(2)}) %collective-permute-start.17) | collective-permute-done | bytes 442400 | tf_op jit(solution)/shard_map/ppermute | solution.py:42
  91.0 4.0 %collective-permute-done.14.both_away = bf16[4,96,768]{2,1,0:T(8,128)(2,1)S(1)} collective-permute-done((bf16[4,96,768]{2,1,0:T(8,128)(2,1)S(1)}, bf16[4,96,768]{2,1,0:T(8,128)(2,1)S(1)}, u32[]{:S(2)}, u32[]{:S(2)}) %collective-permute-start.14) | collective-permute-done | bytes 589856 | tf_op jit(solution)/shard_map/ppermute | solution.py:56
  100.3 7.2 %shard_map.323 = (bf16[512,768]{1,0:T(8,128)(2,1)S(1)}, bf16[512,768]{1,0:T(8,128)(2,1)S(1)}, bf16[512,768]{1,0:T(8,128)(2,1)S(1)}, bf16[512,768]{1,0:T(8,128)(2...) custom-call(s32[3]{0:T(128)S(1)} %pad_add_fusion.2.info_ref, ...), custom_call_target="tpu_custom_call" | custom-call | flops 2818572288 | bytes 12582912 | tf_op jit(solution)/shard_map/pallas_call | solution.py:73
  109.4 16.0 %collective-permute-done.19.both_away = bf16[4,96,768]{2,1,0:T(8,128)(2,1)S(1)} collective-permute-done((bf16[4,96,768]{2,1,0:T(8,128)(2,1)S(1)}, bf16[4,96,768]{2,1,0:T(8,128)(2,1)S(1)}, u32[]{:S(2)}, u32[]{:S(2)}) %collective-permute-start.19) | collective-permute-done | bytes 589856 | tf_op jit(solution)/shard_map/ppermute | solution.py:56
  129.0 1.7 collective-permute-done.22.refs_1_
  130.7 6.7 %shard_map.326 = (bf16[512,3072]{1,0:T(8,128)(2,1)S(1)}, bf16[512,3072]{1,0:T(8,128)(2,1)S(1)}) custom-call(s32[3]{0:T(128)S(1)} %pad_add_fusion.2.info_ref, f32[8,3072]{1,0:T(8,128)S(1)} %get-tuple-element.268.shift_ref, bf16[512,768]{1,0:T(8,128)(2,1)S(1)} %get-tuple-element.289.low_ref, bf16[4,2,2,96,768]{4,3,2,1,0:T(8,128)(2,1)S(1)} %shard_map.325.refs_0_, ...), custom_call_target="tpu_custom_call" | custom-call | flops 2415919104 | bytes 11796480 | tf_op jit(solution)/shard_map/pallas_call | solution.py:73
  137.4 1.7 copy-done.28
  140.5 2.4 collective-permute-done.26.refs_5_
  142.9 4.5 %shard_map.328 = (f32[512,768]{1,0:T(8,128)S(1)}, f32[256,768]{1,0:T(8,128)S(1)}, bf16[256,768]{1,0:T(8,128)(2,1)S(1)}) custom-call(s32[3]{0:T(128)S(1)} %pad_add_fusion.2.info_ref, f32[16,768]{1,0:T(8,128)S(1)} %get-tuple-element.267.vec_ref.shift_ref.gain_ref, bf16[512,3072]{1,0:T(8,128)(2,1)S(1)} %get-tuple-element.299.active_ref, ...), custom_call_target="tpu_custom_call" | custom-call | flops 2415919104 | bytes 12582912 | tf_op jit(solution)/shard_map/pallas_call | solution.py:73
  147.4 2.3 collective-permute-start.27
  149.7 9.4 %collective-permute-done.27.far_ref = bf16[256,768]{1,0:T(8,128)(2,1)S(1)} collective-permute-done((bf16[256,768]{1,0:T(8,128)(2,1)S(1)}, bf16[256,768]{1,0:T(8,128)(2,1)S(1)}, u32[]{:S(2)}, u32[]{:S(2)}) %collective-permute-start.27) | collective-permute-done | bytes 393248 | tf_op jit(solution)/shard_map/ppermute | solution.py:42
  159.1 4.6 %shard_map.329 = (bf16[256,768]{1,0:T(8,128)(2,1)}, f32[256,768]{1,0:T(8,128)S(1)}, bf16[256,768]{1,0:T(8,128)(2,1)S(1)}, f32[8,768]{1,0:T(8,128)S(1)}, bf16[1,7...) custom-call(s32[3]{0:T(128)S(1)} %pad_add_fusion.2.info_ref, ...), custom_call_target="tpu_custom_call" | custom-call | flops 1811939328 | bytes 7471104 | tf_op jit(solution)/shard_map/pallas_call | solution.py:73
  163.9 1.8 collective-permute-start.29
  169.1 6.3 %collective-permute-done.29.grad_far_ref = bf16[256,768]{1,0:T(8,128)(2,1)S(1)} collective-permute-done((bf16[256,768]{1,0:T(8,128)(2,1)S(1)}, bf16[256,768]{1,0:T(8,128)(2,1)S(1)}, u32[]{:S(2)}, u32[]{:S(2)}) %collective-permute-start.29) | collective-permute-done | bytes 393248 | tf_op jit(solution)/shard_map/ppermute | solution.py:42
  175.4 5.9 %shard_map.331 = (f32[512,768]{1,0:T(8,128)S(1)}, bf16[512,768]{1,0:T(8,128)(2,1)S(1)}, f32[8,768]{1,0:T(8,128)S(1)}, bf16[2,16,48,768]{3,2,1,0:T(8,128)(2,1)S(1)}, bf16[2,16,48,768]{3,2,1,0:T(8,128)(2,1)}) custom-call(s32[3]{0:T(128)S(1)} %pad_add_fusion.2.info_ref, f32[16,768]{1,0:T(8,128)S(1)} %get-tuple-element.267.vec_ref.shift_ref.gain_ref, ...), custom_call_target="tpu_custom_call" | custom-call | flops 2415919104 | bytes 14155776 | tf_op jit(solution)/shard_map/pallas_call | solution.py:73
  182.2 7.5 %shard_map.332 = (bf16[512,3072]{1,0:T(8,128)(2,1)S(1)}, f32[8,3072]{1,0:T(8,128)S(1)}, bf16[2,768,768]{2,1,0:T(8,128)(2,1)S(1)}, bf16[2,768,768]{2,1,0:T(8,128)(2,1)S(1)}) custom-call(s32[3]{0:T(128)S(1)} %pad_add_fusion.2.info_ref, bf16[512,768]{1,0:T(8,128)(2,1)S(1)} %get-tuple-element.323.grad_low_ref, bf16[512,3072]{1,0:T(8,128)(2,1)S(1)} %copy-done.29, ...), custom_call_target="tpu_custom_call" | custom-call | flops 4831838208 | bytes 21233664 | tf_op jit(solution)/shard_map/pallas_call | solution.py:73
  194.4 4.3 %shard_map.334 = (f32[512,768]{1,0:T(8,128)S(1)}, f32[8,768]{1,0:T(8,128)S(1)}) custom-call(s32[3]{0:T(128)S(1)} %pad_add_fusion.2.info_ref, f32[16,768]{1,0:T(8,128)S(1)} %get-tuple-element.267.vec_ref.shift_ref.gain_ref, f32[512,768]{1,0:T(8,128)S(1)} %copy-done.9, f32[512,768]{1,0:T(8,128)S(1)} %copy-done.11, ...), custom_call_target="tpu_custom_call" | custom-call | flops 2415919104 | bytes 12582912 | tf_op jit(solution)/shard_map/pallas_call | solution.py:73
  198.7 9.0 %collective-permute-done.32.refs_1_ = bf16[4,2,96,768]{3,2,1,0:T(8,128)(2,1)S(1)} collective-permute-done((bf16[4,2,96,768]{3,2,1,0:T(8,128)(2,1)S(1)}, bf16[4,2,96,768]{3,2,1,0:T(8,128)(2,1)S(1)}, u32[]{:S(2)}, u32[]{:S(2)}) %collective-permute-start.32) | collective-permute-done | bytes 1179680 | tf_op jit(solution)/shard_map/ppermute | solution.py:56
  212.1 11.1 %shard_map.337 = (bf16[512,768]{1,0:T(8,128)(2,1)S(1)}, bf16[512,768]{1,0:T(8,128)(2,1)S(1)}, bf16[512,768]{1,0:T(8,128)(2,1)S(1)}, f32[8,768]{1,0:T(8,128)S(1)}...) custom-call(s32[3]{0:T(128)S(1)} %pad_add_fusion.2.info_ref, s32[4]{0:T(128)S(1)} %pad_add_fusion.3.counts_ref, ...), custom_call_target="tpu_custom_call" | custom-call | flops 4227858432 | bytes 14942208 | tf_op jit(solution)/shard_map/pallas_call | solution.py:73
  223.1 4.4 %collective-permute-done.34.received = bf16[4,96,768]{2,1,0:T(8,128)(2,1)S(1)} collective-permute-done((bf16[4,96,768]{2,1,0:T(8,128)(2,1)S(1)}, bf16[4,96,768]{2,1,0:T(8,128)(2,1)S(1)}, u32[]{:S(2)}, u32[]{:S(2)}) %collective-permute-start.34) | collective-permute-done | bytes 589856 | tf_op jit(solution)/shard_map/ppermute | solution.py:56
  227.5 3.4 collective-permute-done.35.refs_3_
  236.0 2.4 collective-permute-start.39
  238.3 3.7 %shard_map.340 = (f32[512,768]{1,0:T(8,128)S(1)}, f32[8,768]{1,0:T(8,128)S(1)}) custom-call(s32[3]{0:T(128)S(1)} %pad_add_fusion.2.info_ref, f32[16,768]{1,0:T(8,128)S(1)} %get-tuple-element.267.vec_ref.shift_ref.gain_ref, f32[512,768]{1,0:T(8,128)S(1)} %get-tuple-element.344.grad_ref, bf16[512,768]{1,0:T(8,128)(2,1)S(1)} %get-tuple-element.368.refs_0_, ...), custom_call_target="tpu_custom_call" | custom-call | flops 1811939328 | bytes 11796480 | tf_op jit(solution)/shard_map/pallas_call | solution.py:73
  242.4 1.9 collective-permute-done.38.far_a
  244.3 6.5 %collective-permute-done.39.far_b = bf16[96,768]{1,0:T(8,128)(2,1)S(1)} collective-permute-done((bf16[96,768]{1,0:T(8,128)(2,1)S(1)}, bf16[96,768]{1,0:T(8,128)(2,1)S(1)}, u32[]{:S(2)}, u32[]{:S(2)}) %collective-permute-start.39) | collective-permute-done | bytes 147488 | tf_op jit(solution)/shard_map/ppermute | solution.py:42
  254.7 3.2 collective-permute-start.44
  257.9 12.1 %shard_map.343 = (bf16[512,768]{1,0:T(8,128)(2,1)S(1)}, bf16[512,768]{1,0:T(8,128)(2,1)S(1)}, bf16[512,768]{1,0:T(8,128)(2,1)S(1)}, f32[8,768]{1,0:T(8,128)S(1)}...) custom-call(s32[3]{0:T(128)S(1)} %pad_add_fusion.2.info_ref, s32[4]{0:T(128)S(1)} %pad_add_fusion.4.counts_ref, ...), custom_call_target="tpu_custom_call" | custom-call | flops 4227858432 | bytes 14942208 | tf_op jit(solution)/shard_map/pallas_call | solution.py:73
  271.1 2.2 collective-permute-done.44.far_b
  275.1 3.9 %shard_map.344 = (f32[256,768]{1,0:T(8,128)S(1)}, f32[256,768]{1,0:T(8,128)S(1)}, bf16[512,768]{1,0:T(8,128)(2,1)}) custom-call(s32[3]{0:T(128)S(1)} %pad_add_fusion.2.info_ref, f32[16,768]{1,0:T(8,128)S(1)} %get-tuple-element.267.vec_ref.shift_ref.gain_ref, f32[512,768]{1,0:T(8,128)S(1)} %get-tuple-element.382.grad_ref, ...), custom_call_target="tpu_custom_call" | custom-call | flops 1811939328 | bytes 11796480 | tf_op jit(solution)/shard_map/pallas_call | solution.py:73
  279.0 5.0 %collective-permute-done.46.received = bf16[4,96,768]{2,1,0:T(8,128)(2,1)S(1)} collective-permute-done((bf16[4,96,768]{2,1,0:T(8,128)(2,1)S(1)}, bf16[4,96,768]{2,1,0:T(8,128)(2,1)S(1)}, u32[]{:S(2)}, u32[]{:S(2)}) %collective-permute-start.46) | collective-permute-done | bytes 589856 | tf_op jit(solution)/shard_map/ppermute | solution.py:56
  286.0 2.7 collective-permute-start.48
  288.7 1.7 collective-permute-start.50
  290.8 3.8 %collective-permute-done.48.near_b = bf16[96,768]{1,0:T(8,128)(2,1)S(1)} collective-permute-done((bf16[96,768]{1,0:T(8,128)(2,1)S(1)}, bf16[96,768]{1,0:T(8,128)(2,1)S(1)}, u32[]{:S(2)}, u32[]{:S(2)}) %collective-permute-start.48) | collective-permute-done | bytes 147488 | tf_op jit(solution)/shard_map/ppermute | solution.py:42
  294.6 5.2 %collective-permute-done.49.far_a = bf16[96,768]{1,0:T(8,128)(2,1)S(1)} collective-permute-done((bf16[96,768]{1,0:T(8,128)(2,1)S(1)}, bf16[96,768]{1,0:T(8,128)(2,1)S(1)}, u32[]{:S(2)}, u32[]{:S(2)}) %collective-permute-start.49) | collective-permute-done | bytes 147488 | tf_op jit(solution)/shard_map/ppermute | solution.py:42
  300.2 3.4 collective-permute-done.47.refs_1_
  312.0 1.8 shard_map.351
  313.7 3.6 %collective-permute-done.51.received = bf16[4,112,768]{2,1,0:T(8,128)(2,1)} collective-permute-done((bf16[4,112,768]{2,1,0:T(8,128)(2,1)}, bf16[4,112,768]{2,1,0:T(8,128)(2,1)}, u32[]{:S(2)}, u32[]{:S(2)}) %collective-permute-start.51) | collective-permute-done | bytes 688160 | tf_op jit(solution)/shard_map/ppermute | solution.py:56
  318.6 2.7 collective-permute-start.55
  321.4 1.7 collective-permute-start.57
  327.9 2.6 collective-permute-done.56.far_a
  330.4 3.7 %collective-permute-done.57.far_b = bf16[112,768]{1,0:T(8,128)(2,1)S(1)} collective-permute-done((bf16[112,768]{1,0:T(8,128)(2,1)S(1)}, bf16[112,768]{1,0:T(8,128)(2,1)S(1)}, u32[]{:S(2)}, u32[]{:S(2)}) %collective-permute-start.57) | collective-permute-done | bytes 172064 | tf_op jit(solution)/shard_map/ppermute | solution.py:42
  (272 shorter events, 85.1 us)
Async XLA Ops:
  4.5 19.3 %collective-permute-start.1 = (bf16[112,768]{1,0:T(8,128)(2,1)S(1)}, bf16[112,768]{1,0:T(8,128)(2,1)S(1)}, u32[]{:S(2)}, u32[]{:S(2)}) collective-permute-start(bf16[112,768]{1,0:T(8,128)(2,1)S(1)} %get-tuple-element.500), channel_id=1, source_target_pairs={{0,16},{1,17},{2,18},{3,19},{4,20},{5,21},{6,22},{7,23},{8,24},{9,... | collective-permute-start | bytes 516104 | tf_op jit(solution)/shard_map/ppermute | solution.py:42
  8.6 15.2 %collective-permute-start = (bf16[112,768]{1,0:T(8,128)(2,1)S(1)}, bf16[112,768]{1,0:T(8,128)(2,1)S(1)}, u32[]{:S(2)}, u32[]{:S(2)}) collective-permute-start(bf16[112,768]{1,0:T(8,128)(2,1)S(1)} %get-tuple-element.500), channel_id=1, source_target_pairs={{0,8},{1,9},{2,10},{3,11},{4,12},{5,13},{6,14},{7,15},{8,0},{9,1},... | collective-permute-start | bytes 516104 | tf_op jit(solution)/shard_map/ppermute | solution.py:42
  10.2 13.6 %collective-permute-start.2 = (bf16[112,768]{1,0:T(8,128)(2,1)S(1)}, bf16[112,768]{1,0:T(8,128)(2,1)S(1)}, u32[]{:S(2)}, u32[]{:S(2)}) collective-permute-start(bf16[112,768]{1,0:T(8,128)(2,1)S(1)} %get-tuple-element.248.refs_0_), channel_id=1, source_target_pairs={{0,24},{1,25},{2,26},{3,27},{4,28},{5,29},{6,30},{7,31},{8,16},{9,... | collective-permute-start | bytes 516104 | tf_op jit(solution)/shard_map/ppermute | solution.py:42
  10.5 13.4 %collective-permute-start.3 = (bf16[96,768]{1,0:T(8,128)(2,1)S(1)}, bf16[96,768]{1,0:T(8,128)(2,1)S(1)}, u32[]{:S(2)}, u32[]{:S(2)}) collective-permute-start(bf16[96,768]{1,0:T(8,128)(2,1)S(1)} %get-tuple-element.503), channel_id=1, source_target_pairs={{0,8},{1,9},{2,10},{3,11},{4,12},{5,13},{6,14},{7,15},{8,0},{9,1},... | collective-permute-start | bytes 442376 | tf_op jit(solution)/shard_map/ppermute | solution.py:42
  24.4 21.7 %collective-permute-start.5 = (bf16[4,112,768]{2,1,0:T(8,128)(2,1)S(1)}, bf16[4,112,768]{2,1,0:T(8,128)(2,1)S(1)}, u32[]{:S(2)}, u32[]{:S(2)}) collective-permute-start(bf16[4,112,768]{2,1,0:T(8,128)(2,1)S(1)} %shard_map.314.mine), channel_id=1, source_target_pairs={{0,4},{1,3},{2,6},{3,1},{4,0},{5,7},{6,2},{7,5},{8,12},{9,11},{10,... | collective-permute-start | bytes 2064392 | tf_op jit(solution)/shard_map/ppermute | solution.py:56
  26.1 20.1 %collective-permute-start.4 = (bf16[4,112,768]{2,1,0:T(8,128)(2,1)S(1)}, bf16[4,112,768]{2,1,0:T(8,128)(2,1)S(1)}, u32[]{:S(2)}, u32[]{:S(2)}) collective-permute-start(bf16[4,112,768]{2,1,0:T(8,128)(2,1)S(1)} %shard_map.314.mine), channel_id=1, source_target_pairs={{0,2},{1,5},{2,0},{3,7},{4,6},{5,1},{6,4},{7,3},{8,10},{9,13},{10,... | collective-permute-start | bytes 2064392 | tf_op jit(solution)/shard_map/ppermute | solution.py:56
  27.6 18.6 %collective-permute-start.7 = (bf16[240,768]{1,0:T(8,128)(2,1)S(1)}, bf16[240,768]{1,0:T(8,128)(2,1)S(1)}, u32[]{:S(2)}, u32[]{:S(2)}) collective-permute-start(bf16[240,768]{1,0:T(8,128)(2,1)S(1)} %pad_maximum_fusion.3), channel_id=1, source_target_pairs={{0,8},{1,9},{2,10},{3,11},{4,12},{5,13},{6,14},{7,15},{8,0},{9,1},... | collective-permute-start | bytes 1105928 | tf_op jit(solution)/shard_map/ppermute | solution.py:42
  29.6 16.5 %collective-permute-start.6 = (bf16[2,96,768]{2,1,0:T(8,128)(2,1)S(1)}, bf16[2,96,768]{2,1,0:T(8,128)(2,1)S(1)}, u32[]{:S(2)}, u32[]{:S(2)}) collective-permute-start(bf16[2,96,768]{2,1,0:T(8,128)(2,1)S(1)} %shard_map.315.refs_0_), channel_id=1, source_target_pairs={{0,24},{1,25},{2,26},{3,27},{4,28},{5,29},{6,30},{7,31},{8,16},{9,... | collective-permute-start | bytes 884744 | tf_op jit(solution)/shard_map/ppermute | solution.py:42
  46.1 25.2 %collective-permute-start.12 = (bf16[528,768]{1,0:T(8,128)(2,1)S(1)}, bf16[528,768]{1,0:T(8,128)(2,1)S(1)}, u32[]{:S(2)}, u32[]{:S(2)}) collective-permute-start(bf16[528,768]{1,0:T(8,128)(2,1)S(1)} %fusion.1), channel_id=1, source_target_pairs={{0,8},{1,9},{2,10},{3,11},{4,12},{5,13},{6,14},{7,15},{8,0},{9,1},... | collective-permute-start | bytes 2433032 | tf_op jit(solution)/shard_map/ppermute | solution.py:42
  46.2 25.1 %collective-permute-start.8 = (bf16[4,112,768]{2,1,0:T(8,128)(2,1)S(1)}, bf16[4,112,768]{2,1,0:T(8,128)(2,1)S(1)}, u32[]{:S(2)}, u32[]{:S(2)}) collective-permute-start(bf16[4,112,768]{2,1,0:T(8,128)(2,1)S(1)} %collective-permute-done.4.first_away), channel_id=1, source_target_pairs={{0,4},{1,3},{2,6},{3,1},{4,0},{5,7},{6,2},{7,5},{8,12},{9,11},{10,... | collective-permute-start | bytes 2064392 | tf_op jit(solution)/shard_map/ppermute | solution.py:56
  47.4 23.9 %collective-permute-start.10 = (bf16[4,96,768]{2,1,0:T(8,128)(2,1)S(1)}, bf16[4,96,768]{2,1,0:T(8,128)(2,1)S(1)}, u32[]{:S(2)}, u32[]{:S(2)}) collective-permute-start(bf16[4,96,768]{2,1,0:T(8,128)(2,1)S(1)} %bitcast.98), channel_id=1, source_target_pairs={{0,4},{1,3},{2,6},{3,1},{4,0},{5,7},{6,2},{7,5},{8,12},{9,11},{10,... | collective-permute-start | bytes 1769480 | tf_op jit(solution)/shard_map/ppermute | solution.py:56
  49.0 22.3 %collective-permute-start.9 = (bf16[4,96,768]{2,1,0:T(8,128)(2,1)S(1)}, bf16[4,96,768]{2,1,0:T(8,128)(2,1)S(1)}, u32[]{:S(2)}, u32[]{:S(2)}) collective-permute-start(bf16[4,96,768]{2,1,0:T(8,128)(2,1)S(1)} %bitcast.99), channel_id=1, source_target_pairs={{0,2},{1,5},{2,0},{3,7},{4,6},{5,1},{6,4},{7,3},{8,10},{9,13},{10,... | collective-permute-start | bytes 1769480 | tf_op jit(solution)/shard_map/ppermute | solution.py:56
  50.1 21.2 %collective-permute-start.11 = (bf16[2,96,768]{2,1,0:T(8,128)(2,1)S(1)}, bf16[2,96,768]{2,1,0:T(8,128)(2,1)S(1)}, u32[]{:S(2)}, u32[]{:S(2)}) collective-permute-start(bf16[2,96,768]{2,1,0:T(8,128)(2,1)S(1)} %get-tuple-element.260.refs_0_), channel_id=1, source_target_pairs={{0,24},{1,25},{2,26},{3,27},{4,28},{5,29},{6,30},{7,31},{8,16},{9,... | collective-permute-start | bytes 884744 | tf_op jit(solution)/shard_map/ppermute | solution.py:42
  72.8 18.2 %collective-permute-start.16 = (bf16[4,96,768]{2,1,0:T(8,128)(2,1)S(1)}, bf16[4,96,768]{2,1,0:T(8,128)(2,1)S(1)}, u32[]{:S(2)}, u32[]{:S(2)}) collective-permute-start(bf16[4,96,768]{2,1,0:T(8,128)(2,1)S(1)} %bitcast.101), channel_id=1, source_target_pairs={{0,4},{1,3},{2,6},{3,1},{4,0},{5,7},{6,2},{7,5},{8,12},{9,11},{10,... | collective-permute-start | bytes 1769480 | tf_op jit(solution)/shard_map/ppermute | solution.py:56
  74.3 16.6 %collective-permute-start.15 = (bf16[4,96,768]{2,1,0:T(8,128)(2,1)S(1)}, bf16[4,96,768]{2,1,0:T(8,128)(2,1)S(1)}, u32[]{:S(2)}, u32[]{:S(2)}) collective-permute-start(bf16[4,96,768]{2,1,0:T(8,128)(2,1)S(1)} %bitcast.102), channel_id=1, source_target_pairs={{0,2},{1,5},{2,0},{3,7},{4,6},{5,1},{6,4},{7,3},{8,10},{9,13},{10,... | collective-permute-start | bytes 1769480 | tf_op jit(solution)/shard_map/ppermute | solution.py:56
  74.7 20.2 %collective-permute-start.14 = (bf16[4,96,768]{2,1,0:T(8,128)(2,1)S(1)}, bf16[4,96,768]{2,1,0:T(8,128)(2,1)S(1)}, u32[]{:S(2)}, u32[]{:S(2)}) collective-permute-start(bf16[4,96,768]{2,1,0:T(8,128)(2,1)S(1)} %collective-permute-done.9.first_away), channel_id=1, source_target_pairs={{0,4},{1,3},{2,6},{3,1},{4,0},{5,7},{6,2},{7,5},{8,12},{9,11},{10,... | collective-permute-start | bytes 1769480 | tf_op jit(solution)/shard_map/ppermute | solution.py:56
  76.2 14.8 %collective-permute-start.17 = (bf16[2,144,768]{2,1,0:T(8,128)(2,1)S(1)}, bf16[2,144,768]{2,1,0:T(8,128)(2,1)S(1)}, u32[]{:S(2)}, u32[]{:S(2)}) collective-permute-start(bf16[2,144,768]{2,1,0:T(8,128)(2,1)S(1)} %get-tuple-element.276.refs_0_), channel_id=1, source_target_pairs={{0,24},{1,25},{2,26},{3,27},{4,28},{5,29},{6,30},{7,31},{8,16},{9,... | collective-permute-start | bytes 1327112 | tf_op jit(solution)/shard_map/ppermute | solution.py:42
  96.4 28.9 %collective-permute-start.21 = (bf16[4,144,768]{2,1,0:T(8,128)(2,1)S(1)}, bf16[4,144,768]{2,1,0:T(8,128)(2,1)S(1)}, u32[]{:S(2)}, u32[]{:S(2)}) collective-permute-start(bf16[4,144,768]{2,1,0:T(8,128)(2,1)S(1)} %bitcast.95), channel_id=1, source_target_pairs={{0,4},{1,3},{2,6},{3,1},{4,0},{5,7},{6,2},{7,5},{8,12},{9,11},{10,... | collective-permute-start | bytes 2654216 | tf_op jit(solution)/shard_map/ppermute | solution.py:56
  98.0 27.3 %collective-permute-start.20 = (bf16[4,144,768]{2,1,0:T(8,128)(2,1)S(1)}, bf16[4,144,768]{2,1,0:T(8,128)(2,1)S(1)}, u32[]{:S(2)}, u32[]{:S(2)}) collective-permute-start(bf16[4,144,768]{2,1,0:T(8,128)(2,1)S(1)} %bitcast.96), channel_id=1, source_target_pairs={{0,2},{1,5},{2,0},{3,7},{4,6},{5,1},{6,4},{7,3},{8,10},{9,13},{10,... | collective-permute-start | bytes 2654216 | tf_op jit(solution)/shard_map/ppermute | solution.py:56
  98.8 26.6 %collective-permute-start.19 = (bf16[4,96,768]{2,1,0:T(8,128)(2,1)S(1)}, bf16[4,96,768]{2,1,0:T(8,128)(2,1)S(1)}, u32[]{:S(2)}, u32[]{:S(2)}) collective-permute-start(bf16[4,96,768]{2,1,0:T(8,128)(2,1)S(1)} %collective-permute-done.15.first_away), channel_id=1, source_target_pairs={{0,4},{1,3},{2,6},{3,1},{4,0},{5,7},{6,2},{7,5},{8,12},{9,11},{10,... | collective-permute-start | bytes 1769480 | tf_op jit(solution)/shard_map/ppermute | solution.py:56
  126.8 13.7 %collective-permute-start.24 = (bf16[4,2,144,768]{3,2,1,0:T(8,128)(2,1)S(1)}, bf16[4,2,144,768]{3,2,1,0:T(8,128)(2,1)S(1)}, u32[]{:S(2)}, u32[]{:S(2)}) collective-permute-start(bf16[4,2,144,768]{3,2,1,0:T(8,128)(2,1)S(1)} %shard_map.327.refs_0_), channel_id=1, source_target_pairs={{0,1},{1,0},{2,3},{3,2},{4,5},{5,4},{6,7},{7,6},{8,9},{9,8},{10,11... | collective-permute-start | bytes 5308424 | tf_op jit(solution)/shard_map/ppermute | solution.py:48
  127.4 11.7 %collective-permute-start.25 = (bf16[4,144,768]{2,1,0:T(8,128)(2,1)S(1)}, bf16[4,144,768]{2,1,0:T(8,128)(2,1)S(1)}, u32[]{:S(2)}, u32[]{:S(2)}) collective-permute-start(bf16[4,144,768]{2,1,0:T(8,128)(2,1)S(1)} %collective-permute-done.21.refs_1_), channel_id=1, source_target_pairs={{0,1},{1,0},{2,3},{3,2},{4,5},{5,4},{6,7},{7,6},{8,9},{9,8},{10,11... | collective-permute-start | bytes 2654216 | tf_op jit(solution)/shard_map/ppermute | solution.py:48
  127.5 13.0 %collective-permute-start.23 = (bf16[4,144,768]{2,1,0:T(8,128)(2,1)S(1)}, bf16[4,144,768]{2,1,0:T(8,128)(2,1)S(1)}, u32[]{:S(2)}, u32[]{:S(2)}) collective-permute-start(bf16[4,144,768]{2,1,0:T(8,128)(2,1)S(1)} %collective-permute-done.20.other), channel_id=1, source_target_pairs={{0,4},{1,3},{2,6},{3,1},{4,0},{5,7},{6,2},{7,5},{8,12},{9,11},{10,... | collective-permute-start | bytes 2654216 | tf_op jit(solution)/shard_map/ppermute | solution.py:56
  147.4 11.7 %collective-permute-start.27 = (bf16[256,768]{1,0:T(8,128)(2,1)S(1)}, bf16[256,768]{1,0:T(8,128)(2,1)S(1)}, u32[]{:S(2)}, u32[]{:S(2)}) collective-permute-start(bf16[256,768]{1,0:T(8,128)(2,1)S(1)} %get-tuple-element.307), channel_id=1, source_target_pairs={{0,8},{1,9},{2,10},{3,11},{4,12},{5,13},{6,14},{7,15},{8,0},{9,1},... | collective-permute-start | bytes 1179656 | tf_op jit(solution)/shard_map/ppermute | solution.py:42
  163.9 11.5 %collective-permute-start.29 = (bf16[256,768]{1,0:T(8,128)(2,1)S(1)}, bf16[256,768]{1,0:T(8,128)(2,1)S(1)}, u32[]{:S(2)}, u32[]{:S(2)}) collective-permute-start(bf16[256,768]{1,0:T(8,128)(2,1)S(1)} %get-tuple-element.312), channel_id=1, source_target_pairs={{0,8},{1,9},{2,10},{3,11},{4,12},{5,13},{6,14},{7,15},{8,0},{9,1},... | collective-permute-start | bytes 1179656 | tf_op jit(solution)/shard_map/ppermute | solution.py:42
  167.5 13.8 %collective-permute-start.30 = (bf16[4,2,48,768]{3,2,1,0:T(8,128)(2,1)S(1)}, bf16[4,2,48,768]{3,2,1,0:T(8,128)(2,1)S(1)}, u32[]{:S(2)}, u32[]{:S(2)}) collective-permute-start(bf16[4,2,48,768]{3,2,1,0:T(8,128)(2,1)S(1)} %get-tuple-element.314), channel_id=1, source_target_pairs={{0,4},{1,3},{2,6},{3,1},{4,0},{5,7},{6,2},{7,5},{8,12},{9,11},{10,... | collective-permute-start | bytes 1769480 | tf_op jit(solution)/shard_map/ppermute | solution.py:56
  189.7 17.9 %collective-permute-start.33 = (bf16[2,16,48,768]{3,2,1,0:T(8,128)(2,1)S(1)}, bf16[2,16,48,768]{3,2,1,0:T(8,128)(2,1)S(1)}, u32[]{:S(2)}, u32[]{:S(2)}) collective-permute-start(bf16[2,16,48,768]{3,2,1,0:T(8,128)(2,1)S(1)} %bitcast.117), channel_id=1, source_target_pairs={{0,1},{1,0},{2,3},{3,2},{4,5},{5,4},{6,7},{7,6},{8,9},{9,8},{10,11... | collective-permute-start | bytes 7077896 | tf_op jit(solution)/shard_map/ppermute | solution.py:48
  191.4 16.3 %collective-permute-start.32 = (bf16[4,2,96,768]{3,2,1,0:T(8,128)(2,1)S(1)}, bf16[4,2,96,768]{3,2,1,0:T(8,128)(2,1)S(1)}, u32[]{:S(2)}, u32[]{:S(2)}) collective-permute-start(bf16[4,2,96,768]{3,2,1,0:T(8,128)(2,1)S(1)} %get-tuple-element.330), channel_id=1, source_target_pairs={{0,4},{1,3},{2,6},{3,1},{4,0},{5,7},{6,2},{7,5},{8,12},{9,11},{10,... | collective-permute-start | bytes 3538952 | tf_op jit(solution)/shard_map/ppermute | solution.py:56
  208.8 22.1 %collective-permute-start.35 = (bf16[4,2,96,768]{3,2,1,0:T(8,128)(2,1)S(1)}, bf16[4,2,96,768]{3,2,1,0:T(8,128)(2,1)S(1)}, u32[]{:S(2)}, u32[]{:S(2)}) collective-permute-start(bf16[4,2,96,768]{3,2,1,0:T(8,128)(2,1)S(1)} %get-tuple-element.343), channel_id=1, source_target_pairs={{0,4},{1,3},{2,6},{3,1},{4,0},{5,7},{6,2},{7,5},{8,12},{9,11},{10,... | collective-permute-start | bytes 3538952 | tf_op jit(solution)/shard_map/ppermute | solution.py:56
  211.2 16.3 %collective-permute-start.34 = (bf16[4,96,768]{2,1,0:T(8,128)(2,1)S(1)}, bf16[4,96,768]{2,1,0:T(8,128)(2,1)S(1)}, u32[]{:S(2)}, u32[]{:S(2)}) collective-permute-start(bf16[4,96,768]{2,1,0:T(8,128)(2,1)S(1)} %get-tuple-element.339), channel_id=1, source_target_pairs={{0,2},{1,5},{2,0},{3,7},{4,6},{5,1},{6,4},{7,3},{8,10},{9,13},{10,... | collective-permute-start | bytes 1769480 | tf_op jit(solution)/shard_map/ppermute | solution.py:56
  230.9 19.9 %collective-permute-start.40 = (bf16[2,16,48,768]{3,2,1,0:T(8,128)(2,1)S(1)}, bf16[2,16,48,768]{3,2,1,0:T(8,128)(2,1)S(1)}, u32[]{:S(2)}, u32[]{:S(2)}) collective-permute-start(bf16[2,16,48,768]{3,2,1,0:T(8,128)(2,1)S(1)} %bitcast.115), channel_id=1, source_target_pairs={{0,1},{1,0},{2,3},{3,2},{4,5},{5,4},{6,7},{7,6},{8,9},{9,8},{10,11... | collective-permute-start | bytes 7077896 | tf_op jit(solution)/shard_map/ppermute | solution.py:48
  231.9 19.0 %collective-permute-start.36 = (bf16[4,144,768]{2,1,0:T(8,128)(2,1)S(1)}, bf16[4,144,768]{2,1,0:T(8,128)(2,1)S(1)}, u32[]{:S(2)}, u32[]{:S(2)}) collective-permute-start(bf16[4,144,768]{2,1,0:T(8,128)(2,1)S(1)} %get-tuple-element.360), channel_id=1, source_target_pairs={{0,2},{1,5},{2,0},{3,7},{4,6},{5,1},{6,4},{7,3},{8,10},{9,13},{10,... | collective-permute-start | bytes 2654216 | tf_op jit(solution)/shard_map/ppermute | solution.py:56
  235.4 9.0 %collective-permute-start.38 = (bf16[96,768]{1,0:T(8,128)(2,1)S(1)}, bf16[96,768]{1,0:T(8,128)(2,1)S(1)}, u32[]{:S(2)}, u32[]{:S(2)}) collective-permute-start(bf16[96,768]{1,0:T(8,128)(2,1)S(1)} %get-tuple-element.365), channel_id=1, source_target_pairs={{0,8},{1,9},{2,10},{3,11},{4,12},{5,13},{6,14},{7,15},{8,0},{9,1},... | collective-permute-start | bytes 442376 | tf_op jit(solution)/shard_map/ppermute | solution.py:42
  236.0 14.9 %collective-permute-start.39 = (bf16[96,768]{1,0:T(8,128)(2,1)S(1)}, bf16[96,768]{1,0:T(8,128)(2,1)S(1)}, u32[]{:S(2)}, u32[]{:S(2)}) collective-permute-start(bf16[96,768]{1,0:T(8,128)(2,1)S(1)} %get-tuple-element.366), channel_id=1, source_target_pairs={{0,16},{1,17},{2,18},{3,19},{4,20},{5,21},{6,22},{7,23},{8,24},{9,... | collective-permute-start | bytes 442376 | tf_op jit(solution)/shard_map/ppermute | solution.py:42
  252.1 21.2 %collective-permute-start.41 = (bf16[4,2,96,768]{3,2,1,0:T(8,128)(2,1)S(1)}, bf16[4,2,96,768]{3,2,1,0:T(8,128)(2,1)S(1)}, u32[]{:S(2)}, u32[]{:S(2)}) collective-permute-start(bf16[4,2,96,768]{3,2,1,0:T(8,128)(2,1)S(1)} %get-tuple-element.375), channel_id=1, source_target_pairs={{0,4},{1,3},{2,6},{3,1},{4,0},{5,7},{6,2},{7,5},{8,12},{9,11},{10,... | collective-permute-start | bytes 3538952 | tf_op jit(solution)/shard_map/ppermute | solution.py:56
  253.4 16.6 %collective-permute-start.42 = (bf16[144,768]{1,0:T(8,128)(2,1)S(1)}, bf16[144,768]{1,0:T(8,128)(2,1)S(1)}, u32[]{:S(2)}, u32[]{:S(2)}) collective-permute-start(bf16[144,768]{1,0:T(8,128)(2,1)S(1)} %get-tuple-element.379), channel_id=1, source_target_pairs={{0,24},{1,25},{2,26},{3,27},{4,28},{5,29},{6,30},{7,31},{8,16},{9,... | collective-permute-start | bytes 663560 | tf_op jit(solution)/shard_map/ppermute | solution.py:42
  254.7 16.4 %collective-permute-start.43 = (bf16[144,768]{1,0:T(8,128)(2,1)S(1)}, bf16[144,768]{1,0:T(8,128)(2,1)S(1)}, u32[]{:S(2)}, u32[]{:S(2)}) collective-permute-start(bf16[144,768]{1,0:T(8,128)(2,1)S(1)} %get-tuple-element.380), channel_id=1, source_target_pairs={{0,8},{1,9},{2,10},{3,11},{4,12},{5,13},{6,14},{7,15},{8,0},{9,1},... | collective-permute-start | bytes 663560 | tf_op jit(solution)/shard_map/ppermute | solution.py:42
  254.7 18.6 %collective-permute-start.44 = (bf16[144,768]{1,0:T(8,128)(2,1)S(1)}, bf16[144,768]{1,0:T(8,128)(2,1)S(1)}, u32[]{:S(2)}, u32[]{:S(2)}) collective-permute-start(bf16[144,768]{1,0:T(8,128)(2,1)S(1)} %get-tuple-element.381), channel_id=1, source_target_pairs={{0,16},{1,17},{2,18},{3,19},{4,20},{5,21},{6,22},{7,23},{8,24},{9,... | collective-permute-start | bytes 663560 | tf_op jit(solution)/shard_map/ppermute | solution.py:42
  273.3 10.8 %collective-permute-start.45 = (bf16[2,16,48,768]{3,2,1,0:T(8,128)(2,1)S(1)}, bf16[2,16,48,768]{3,2,1,0:T(8,128)(2,1)S(1)}, u32[]{:S(2)}, u32[]{:S(2)}) collective-permute-start(bf16[2,16,48,768]{3,2,1,0:T(8,128)(2,1)S(1)} %bitcast.116), channel_id=1, source_target_pairs={{0,1},{1,0},{2,3},{3,2},{4,5},{5,4},{6,7},{7,6},{8,9},{9,8},{10,11... | collective-permute-start | bytes 7077896 | tf_op jit(solution)/shard_map/ppermute | solution.py:48
  274.1 9.9 %collective-permute-start.46 = (bf16[4,96,768]{2,1,0:T(8,128)(2,1)S(1)}, bf16[4,96,768]{2,1,0:T(8,128)(2,1)S(1)}, u32[]{:S(2)}, u32[]{:S(2)}) collective-permute-start(bf16[4,96,768]{2,1,0:T(8,128)(2,1)S(1)} %get-tuple-element.401), channel_id=1, source_target_pairs={{0,2},{1,5},{2,0},{3,7},{4,6},{5,1},{6,4},{7,3},{8,10},{9,13},{10,... | collective-permute-start | bytes 1769480 | tf_op jit(solution)/shard_map/ppermute | solution.py:56
  285.2 18.4 %collective-permute-start.47 = (bf16[4,2,112,768]{3,2,1,0:T(8,128)(2,1)S(1)}, bf16[4,2,112,768]{3,2,1,0:T(8,128)(2,1)S(1)}, u32[]{:S(2)}, u32[]{:S(2)}) collective-permute-start(bf16[4,2,112,768]{3,2,1,0:T(8,128)(2,1)S(1)} %get-tuple-element.416), channel_id=1, source_target_pairs={{0,4},{1,3},{2,6},{3,1},{4,0},{5,7},{6,2},{7,5},{8,12},{9,11},{10,... | collective-permute-start | bytes 4128776 | tf_op jit(solution)/shard_map/ppermute | solution.py:56
  288.7 11.1 %collective-permute-start.49 = (bf16[96,768]{1,0:T(8,128)(2,1)S(1)}, bf16[96,768]{1,0:T(8,128)(2,1)S(1)}, u32[]{:S(2)}, u32[]{:S(2)}) collective-permute-start(bf16[96,768]{1,0:T(8,128)(2,1)S(1)} %get-tuple-element.421), channel_id=1, source_target_pairs={{0,8},{1,9},{2,10},{3,11},{4,12},{5,13},{6,14},{7,15},{8,0},{9,1},... | collective-permute-start | bytes 442376 | tf_op jit(solution)/shard_map/ppermute | solution.py:42
  288.7 11.4 %collective-permute-start.50 = (bf16[96,768]{1,0:T(8,128)(2,1)S(1)}, bf16[96,768]{1,0:T(8,128)(2,1)S(1)}, u32[]{:S(2)}, u32[]{:S(2)}) collective-permute-start(bf16[96,768]{1,0:T(8,128)(2,1)S(1)} %get-tuple-element.422), channel_id=1, source_target_pairs={{0,16},{1,17},{2,18},{3,19},{4,20},{5,21},{6,22},{7,23},{8,24},{9,... | collective-permute-start | bytes 442376 | tf_op jit(solution)/shard_map/ppermute | solution.py:42
  290.4 28.2 %collective-permute-start.54 = (bf16[512,768]{1,0:T(8,128)(2,1)}, bf16[512,768]{1,0:T(8,128)(2,1)}, u32[]{:S(2)}, u32[]{:S(2)}) collective-permute-start(bf16[512,768]{1,0:T(8,128)(2,1)} %get-tuple-element.452), channel_id=1, source_target_pairs={{0,8},{1,9},{2,10},{3,11},{4,12},{5,13},{6,14},{7,15},{8,0},{9,1},... | collective-permute-start | bytes 2359304 | tf_op jit(solution)/shard_map/ppermute | solution.py:42
  306.1 11.3 %collective-permute-start.51 = (bf16[4,112,768]{2,1,0:T(8,128)(2,1)}, bf16[4,112,768]{2,1,0:T(8,128)(2,1)}, u32[]{:S(2)}, u32[]{:S(2)}) collective-permute-start(bf16[4,112,768]{2,1,0:T(8,128)(2,1)} %get-tuple-element.439), channel_id=1, source_target_pairs={{0,2},{1,5},{2,0},{3,7},{4,6},{5,1},{6,4},{7,3},{8,10},{9,13},{10,... | collective-permute-start | bytes 2064392 | tf_op jit(solution)/shard_map/ppermute | solution.py:56
  318.6 9.3 %collective-permute-start.55 = (bf16[112,768]{1,0:T(8,128)(2,1)S(1)}, bf16[112,768]{1,0:T(8,128)(2,1)S(1)}, u32[]{:S(2)}, u32[]{:S(2)}) collective-permute-start(bf16[112,768]{1,0:T(8,128)(2,1)S(1)} %get-tuple-element.454), channel_id=1, source_target_pairs={{0,24},{1,25},{2,26},{3,27},{4,28},{5,29},{6,30},{7,31},{8,16},{9,... | collective-permute-start | bytes 516104 | tf_op jit(solution)/shard_map/ppermute | solution.py:42
  321.4 9.1 %collective-permute-start.56 = (bf16[112,768]{1,0:T(8,128)(2,1)S(1)}, bf16[112,768]{1,0:T(8,128)(2,1)S(1)}, u32[]{:S(2)}, u32[]{:S(2)}) collective-permute-start(bf16[112,768]{1,0:T(8,128)(2,1)S(1)} %get-tuple-element.455), channel_id=1, source_target_pairs={{0,8},{1,9},{2,10},{3,11},{4,12},{5,13},{6,14},{7,15},{8,0},{9,1},... | collective-permute-start | bytes 516104 | tf_op jit(solution)/shard_map/ppermute | solution.py:42
  321.4 12.8 %collective-permute-start.57 = (bf16[112,768]{1,0:T(8,128)(2,1)S(1)}, bf16[112,768]{1,0:T(8,128)(2,1)S(1)}, u32[]{:S(2)}, u32[]{:S(2)}) collective-permute-start(bf16[112,768]{1,0:T(8,128)(2,1)S(1)} %get-tuple-element.456), channel_id=1, source_target_pairs={{0,16},{1,17},{2,18},{3,19},{4,20},{5,21},{6,22},{7,23},{8,24},{9,... | collective-permute-start | bytes 516104 | tf_op jit(solution)/shard_map/ppermute | solution.py:42
  (69 other events, 569.6 us)

commit v2 on v1

--- a/solution.py
+++ b/solution.py
@@ -1278,32 +1278,32 @@
     grad_second_sum, vec_second = second_back(
         grid, info, table, second_sum, grad_third_sum, grad_hidden, in_w
     )
-    outs, in_got, grad_second_sum = tie(outs, in_got, grad_second_sum)
+    in_got, grad_second_sum = tie(in_got, grad_second_sum)
     ins = first_returns(grid, info, in_keep, in_got)
-    outs = second_returns(grid, info, outs)
     *self_parts, vec_self, self_keep, self_send = scores_back(
         grid, False, slots, info, counts, grad_second_sum, [sq, sk, sv, so], [first_low], self_w
     )
-    outs, ins, self_parts, self_keep, self_send = tie(outs, ins, self_parts, self_keep, self_send)
+    outs, self_parts, self_keep, self_send = tie(outs, self_parts, self_keep, self_send)
     self_keep, self_send = by_piece(self_keep), by_piece(self_send)
     self_got = grid.swap_cores(self_send)
-    ins = second_returns(grid, info, gate, ins)
-    outs = third_returns(grid, info, outs)
+    outs = second_returns(grid, info, gate, outs)
     grad_first_sum, vec_first = project_back(
         grid, False, info, table, grad_second_sum, self_parts, [first_sum], self_w
     )
     ins, outs, self_got, grad_first_sum = tie(ins, outs, self_got, grad_first_sum)
+    ins = second_returns(grid, info, ins)
     selfs = first_returns(grid, info, self_keep, self_got)
-    ins = third_returns(grid, info, ins)
+    outs = third_returns(grid, info, outs)
     *cross_parts, vec_cross, cross_keep, cross_send = scores_back(
         grid, True, slots, info, other_counts, grad_first_sum, [cq, ck, cv, co], inputs, cross_w
     )
-    selfs, ins, cross_parts, cross_keep, cross_send = tie(
-        selfs, ins, cross_parts, cross_keep, cross_send
+    selfs, ins, outs, cross_parts, cross_keep, cross_send = tie(
+        selfs, ins, outs, cross_parts, cross_keep, cross_send
     )
     cross_keep, cross_send = by_piece(cross_keep), by_piece(cross_send)
     cross_got = grid.swap_cores(cross_send)
     selfs = second_returns(grid, info, selfs)
+    ins = third_returns(grid, info, ins)
     tables = [vec_cross, vec_self, vec_first, vec_second, vec_third, grad_gate_shift, vec_hidden]
     where = [(0, 0), (0, 1), (0, 2), (1, 0), (1, 1), (1, 2)]
     where += [(2, 0), (3, 0), (4, 0), (2, 1), (3, 1), (4, 1), (4, 2), (5, 0), (6, 0)]
@@ -1311,7 +1311,7 @@
     grad_mine, grad_theirs, outgoing = project_back(
         grid, True, info, table, grad_first_sum, cross_parts, [], cross_w
     )
-    cross_got, outgoing, selfs, outs, grad_vec = tie(cross_got, outgoing, selfs, outs, grad_vec)
+    cross_got, outgoing, selfs, ins, grad_vec = tie(cross_got, outgoing, selfs, ins, grad_vec)
     crosses = first_returns(grid, info, cross_keep, cross_got, grad_vec)
     incoming = grid.across(outgoing, grid.partner)
     selfs = third_returns(grid, info, selfs)
@@ -1341,26 +1341,26 @@
         return finish(info, done, layout, rows, [(2, 3, rows, width), (2, rows, width)])
 
     if rows % 16:
-        in_all = by_side(finished(in_done, 2, 1)).transpose(0, 2, 1, 3).reshape(2, rows, 4 * width)
-        gate_all = finished(in_done, 1)
+        in_all = by_side(finished(in_done, 2)).transpose(0, 2, 1, 3).reshape(2, rows, 4 * width)
+        gate_all = finished(out_done, 1)
         gate_both = sides(gate_all[0, 0] + gate_all[1, 1], gate_all[0, 1] + gate_all[1, 0])
-        out_all = by_side(finished(out_done, 2)).reshape(2, 4 * rows, width)
+        out_all = by_side(finished(out_done, 2, 1)).reshape(2, 4 * rows, width)
     else:
         every = slice(None)
         cuts = [(0, (every, slice(i * width, (i + 1) * width))) for i in range(4)]
-        layout = [[(1, ())] + cuts[:2], [(1, ())] + cuts[2:]]
-        in_all = finish(info, in_done, layout, rows, [(2, rows, 4 * width), (2, rows, width)])[0]
+        in_all = finish(info, in_done, (cuts[:2], cuts[2:]), rows, [(2, rows, 4 * width)])[0]
         gate_both = call(
             finish_gate_kernel,
             [((2, rows, width), f32)],
-            [info] + list(in_done),
+            [info] + list(out_done),
             [SMEM, VMEM, VMEM],
             [VMEM],
             room=GLUE_LIMIT,
         )[0]
-        places = [(0, (slice(i * rows, (i + 1) * rows),)) for i in range(4)]
-        layout = (places[:2], places[2:])
-        out_all = finish(info, out_done, layout, rows, [(2, 4 * rows, width)])[0]
+        places = [(1, ())] + [(0, (slice(i * rows, (i + 1) * rows),)) for i in range(4)]
+        layout = ((places[0], places[1], places[2]), (places[0], places[3], places[4]))
+        shapes = [(2, 4 * rows, width), (2, rows, width)]
+        out_all = finish(info, out_done, layout, rows, shapes)[0]
     crosses, in_all, out_all, gate_both = tie(crosses, in_all, out_all, gate_both)
     crosses = third_returns(grid, info, crosses)
     selfs, crosses[0], incoming = tie(selfs, crosses[0], incoming)

time: 349 us -> 345 us (0.989)
  waiting for transfers between devices: 154 us -> 146 us
    ppermute x21, waiting for transfers between devices: 50.2 us -> 43.6 us  [hop(): return lax.ppermute(values, AXES, pairs)]
    unnamed x119 -> x129, local copies, waits for them, and re-layouts: 9.69 us -> 8.35 us
  transfers between devices with their start and end apart: 60 -> 60, of which waited for: 32 -> 28; matrix products, arithmetic and copies ran while one was open for 1% -> 1% of each run, Pallas kernels for 27% -> 28%
where the time goes in v2:
time: 345 us; the launch traced here: 338 us
  waiting for transfers between devices  146 us (42%)
  Pallas kernels  109 us (32%)
  starting transfers between devices  62.8 us (18%)
  local copies, waits for them, and re-layouts  10.9 us (3%)
  other arithmetic  5.87 us (2%)
    pallas_call x46, Pallas kernels, call(): pl.pallas_call(kernel, out_shape=[jax.ShapeDtypeStruct(shape, dtype) for...  109 us
    ppermute x24, waiting for transfers between devices, across(): return lax.ppermute(values, AXES, pairs)  93.4 us
    ppermute x21, waiting for transfers between devices, hop(): return lax.ppermute(values, AXES, pairs)  43.6 us
    ppermute x24, starting transfers between devices, across(): return lax.ppermute(values, AXES, pairs)  36.9 us
    ppermute x21, starting transfers between devices, hop(): return lax.ppermute(values, AXES, pairs)  23.6 us
    ppermute x15, waiting for transfers between devices, swap_cores(): return lax.ppermute(values, AXES, pairs)  9.35 us
    unnamed x129, local copies, waits for them, and re-layouts  8.35 us
  transfers between devices with their start and end apart: 60, of which 28 were waited for; matrix products, arithmetic and copies ran while one was open for 1% of the time, Pallas kernels for 28%

profile of v2, /device:TPU:0, one launch (start us, length us, event | category | flops | bytes accessed | tf_op | source)
XLA Modules:
  0.0 337.7 jit_solution(3192739199442874995)
XLA Ops:
  4.5 4.1 %collective-permute-start.1 = (bf16[112,768]{1,0:T(8,128)(2,1)S(1)}, bf16[112,768]{1,0:T(8,128)(2,1)S(1)}, u32[]{:S(2)}, u32[]{:S(2)}) collective-permute-start(bf16[112,768]{1,0:T(8,128)(2,1)S(1)} %get-tuple-element.492), channel_id=1, source_target_pairs={{0,16},{1,17},{2,18},{3,19},{4,20},{5,21},{6,22},{7,23},{8,24},{9,... | collective-permute-start | bytes 516104 | tf_op jit(solution)/shard_map/ppermute | solution.py:42
  12.2 11.6 %collective-permute-done.3.refs_1_ = bf16[96,768]{1,0:T(8,128)(2,1)S(1)} collective-permute-done((bf16[96,768]{1,0:T(8,128)(2,1)S(1)}, bf16[96,768]{1,0:T(8,128)(2,1)S(1)}, u32[]{:S(2)}, u32[]{:S(2)}) %collective-permute-start.3) | collective-permute-done | bytes 147488 | tf_op jit(solution)/shard_map/ppermute | solution.py:42
  29.6 2.9 collective-permute-start.6
  32.6 13.5 %collective-permute-done.6.refs_1_ = bf16[2,96,768]{2,1,0:T(8,128)(2,1)S(1)} collective-permute-done((bf16[2,96,768]{2,1,0:T(8,128)(2,1)S(1)}, bf16[2,96,768]{2,1,0:T(8,128)(2,1)S(1)}, u32[]{:S(2)}, u32[]{:S(2)}) %collective-permute-start.6) | collective-permute-done | bytes 294944 | tf_op jit(solution)/shard_map/ppermute | solution.py:42
  51.3 20.0 %collective-permute-done.11.refs_1_ = bf16[2,96,768]{2,1,0:T(8,128)(2,1)S(1)} collective-permute-done((bf16[2,96,768]{2,1,0:T(8,128)(2,1)S(1)}, bf16[2,96,768]{2,1,0:T(8,128)(2,1)S(1)}, u32[]{:S(2)}, u32[]{:S(2)}) %collective-permute-start.11) | collective-permute-done | bytes 294944 | tf_op jit(solution)/shard_map/ppermute | solution.py:42
  76.2 2.0 collective-permute-start.17
  78.3 7.8 %shard_map.320 = (bf16[512,768]{1,0:T(8,128)(2,1)S(1)}, bf16[512,768]{1,0:T(8,128)(2,1)S(1)}, bf16[512,768]{1,0:T(8,128)(2,1)S(1)}, bf16[512,768]{1,0:T(8,128)(2...) custom-call(s32[3]{0:T(128)S(1)} %pad_add_fusion.2.info_ref, ...), custom_call_target="tpu_custom_call" | custom-call | flops 2818572288 | bytes 12582912 | tf_op jit(solution)/shard_map/pallas_call | solution.py:73
  87.0 4.0 %collective-permute-done.17.refs_1_ = bf16[2,144,768]{2,1,0:T(8,128)(2,1)S(1)} collective-permute-done((bf16[2,144,768]{2,1,0:T(8,128)(2,1)S(1)}, bf16[2,144,768]{2,1,0:T(8,128)(2,1)S(1)}, u32[]{:S(2)}, u32[]{:S(2)}) %collective-permute-start.17) | collective-permute-done | bytes 442400 | tf_op jit(solution)/shard_map/ppermute | solution.py:42
  91.0 4.0 %collective-permute-done.14.both_away = bf16[4,96,768]{2,1,0:T(8,128)(2,1)S(1)} collective-permute-done((bf16[4,96,768]{2,1,0:T(8,128)(2,1)S(1)}, bf16[4,96,768]{2,1,0:T(8,128)(2,1)S(1)}, u32[]{:S(2)}, u32[]{:S(2)}) %collective-permute-start.14) | collective-permute-done | bytes 589856 | tf_op jit(solution)/shard_map/ppermute | solution.py:56
  100.3 7.2 %shard_map.323 = (bf16[512,768]{1,0:T(8,128)(2,1)S(1)}, bf16[512,768]{1,0:T(8,128)(2,1)S(1)}, bf16[512,768]{1,0:T(8,128)(2,1)S(1)}, bf16[512,768]{1,0:T(8,128)(2...) custom-call(s32[3]{0:T(128)S(1)} %pad_add_fusion.2.info_ref, ...), custom_call_target="tpu_custom_call" | custom-call | flops 2818572288 | bytes 12582912 | tf_op jit(solution)/shard_map/pallas_call | solution.py:73
  109.3 16.0 %collective-permute-done.19.both_away = bf16[4,96,768]{2,1,0:T(8,128)(2,1)S(1)} collective-permute-done((bf16[4,96,768]{2,1,0:T(8,128)(2,1)S(1)}, bf16[4,96,768]{2,1,0:T(8,128)(2,1)S(1)}, u32[]{:S(2)}, u32[]{:S(2)}) %collective-permute-start.19) | collective-permute-done | bytes 589856 | tf_op jit(solution)/shard_map/ppermute | solution.py:56
  129.0 1.7 collective-permute-done.22.refs_1_
  130.7 6.7 %shard_map.326 = (bf16[512,3072]{1,0:T(8,128)(2,1)S(1)}, bf16[512,3072]{1,0:T(8,128)(2,1)S(1)}) custom-call(s32[3]{0:T(128)S(1)} %pad_add_fusion.2.info_ref, f32[8,3072]{1,0:T(8,128)S(1)} %get-tuple-element.264.shift_ref, bf16[512,768]{1,0:T(8,128)(2,1)S(1)} %get-tuple-element.285.low_ref, bf16[4,2,2,96,768]{4,3,2,1,0:T(8,128)(2,1)S(1)} %shard_map.325.refs_0_, ...), custom_call_target="tpu_custom_call" | custom-call | flops 2415919104 | bytes 11796480 | tf_op jit(solution)/shard_map/pallas_call | solution.py:73
  137.4 1.7 copy-done.35
  140.5 2.4 collective-permute-done.26.refs_5_
  142.9 4.4 %shard_map.328 = (f32[512,768]{1,0:T(8,128)S(1)}, f32[256,768]{1,0:T(8,128)S(1)}, bf16[256,768]{1,0:T(8,128)(2,1)S(1)}) custom-call(s32[3]{0:T(128)S(1)} %pad_add_fusion.2.info_ref, f32[16,768]{1,0:T(8,128)S(1)} %get-tuple-element.263.vec_ref.shift_ref.gain_ref, bf16[512,3072]{1,0:T(8,128)(2,1)S(1)} %get-tuple-element.295.active_ref, ...), custom_call_target="tpu_custom_call" | custom-call | flops 2415919104 | bytes 12582912 | tf_op jit(solution)/shard_map/pallas_call | solution.py:73
  147.4 2.3 collective-permute-start.27
  149.7 9.4 %collective-permute-done.27.far_ref = bf16[256,768]{1,0:T(8,128)(2,1)S(1)} collective-permute-done((bf16[256,768]{1,0:T(8,128)(2,1)S(1)}, bf16[256,768]{1,0:T(8,128)(2,1)S(1)}, u32[]{:S(2)}, u32[]{:S(2)}) %collective-permute-start.27) | collective-permute-done | bytes 393248 | tf_op jit(solution)/shard_map/ppermute | solution.py:42
  159.1 4.6 %shard_map.329 = (bf16[256,768]{1,0:T(8,128)(2,1)}, f32[256,768]{1,0:T(8,128)S(1)}, bf16[256,768]{1,0:T(8,128)(2,1)S(1)}, f32[8,768]{1,0:T(8,128)S(1)}, bf16[1,7...) custom-call(s32[3]{0:T(128)S(1)} %pad_add_fusion.2.info_ref, ...), custom_call_target="tpu_custom_call" | custom-call | flops 1811939328 | bytes 7471104 | tf_op jit(solution)/shard_map/pallas_call | solution.py:73
  163.8 1.8 collective-permute-start.29
  169.1 6.3 %collective-permute-done.29.grad_far_ref = bf16[256,768]{1,0:T(8,128)(2,1)S(1)} collective-permute-done((bf16[256,768]{1,0:T(8,128)(2,1)S(1)}, bf16[256,768]{1,0:T(8,128)(2,1)S(1)}, u32[]{:S(2)}, u32[]{:S(2)}) %collective-permute-start.29) | collective-permute-done | bytes 393248 | tf_op jit(solution)/shard_map/ppermute | solution.py:42
  175.4 5.9 %shard_map.331 = (f32[512,768]{1,0:T(8,128)S(1)}, bf16[512,768]{1,0:T(8,128)(2,1)S(1)}, f32[8,768]{1,0:T(8,128)S(1)}, bf16[2,16,48,768]{3,2,1,0:T(8,128)(2,1)S(1)}, bf16[2,16,48,768]{3,2,1,0:T(8,128)(2,1)}) custom-call(s32[3]{0:T(128)S(1)} %pad_add_fusion.2.info_ref, f32[16,768]{1,0:T(8,128)S(1)} %get-tuple-element.263.vec_ref.shift_ref.gain_ref, ...), custom_call_target="tpu_custom_call" | custom-call | flops 2415919104 | bytes 14155776 | tf_op jit(solution)/shard_map/pallas_call | solution.py:73
  181.4 8.1 %shard_map.332 = (bf16[512,3072]{1,0:T(8,128)(2,1)S(1)}, f32[8,3072]{1,0:T(8,128)S(1)}, bf16[2,768,768]{2,1,0:T(8,128)(2,1)S(1)}, bf16[2,768,768]{2,1,0:T(8,128)(2,1)}) custom-call(s32[3]{0:T(128)S(1)} %pad_add_fusion.2.info_ref, bf16[512,768]{1,0:T(8,128)(2,1)S(1)} %get-tuple-element.319.grad_low_ref, bf16[512,3072]{1,0:T(8,128)(2,1)S(1)} %copy-done.36, ...), custom_call_target="tpu_custom_call" | custom-call | flops 4831838208 | bytes 21233664 | tf_op jit(solution)/shard_map/pallas_call | solution.py:73
  190.1 2.0 shard_map.333
  193.7 4.3 %shard_map.334 = (f32[512,768]{1,0:T(8,128)S(1)}, f32[8,768]{1,0:T(8,128)S(1)}) custom-call(s32[3]{0:T(128)S(1)} %pad_add_fusion.2.info_ref, f32[16,768]{1,0:T(8,128)S(1)} %get-tuple-element.263.vec_ref.shift_ref.gain_ref, f32[512,768]{1,0:T(8,128)S(1)} %copy-done.11, f32[512,768]{1,0:T(8,128)S(1)} %get-tuple-element.329.grad_ref, ...), custom_call_target="tpu_custom_call" | custom-call | flops 2415919104 | bytes 12582912 | tf_op jit(solution)/shard_map/pallas_call | solution.py:73
  198.1 11.1 %shard_map.335 = (bf16[512,768]{1,0:T(8,128)(2,1)S(1)}, bf16[512,768]{1,0:T(8,128)(2,1)S(1)}, bf16[512,768]{1,0:T(8,128)(2,1)S(1)}, f32[8,768]{1,0:T(8,128)S(1)}...) custom-call(s32[3]{0:T(128)S(1)} %pad_add_fusion.2.info_ref, s32[4]{0:T(128)S(1)} %pad_add_fusion.3.counts_ref, ...), custom_call_target="tpu_custom_call" | custom-call | flops 4227858432 | bytes 14942208 | tf_op jit(solution)/shard_map/pallas_call | solution.py:73
  213.5 3.7 %shard_map.338 = (f32[512,768]{1,0:T(8,128)S(1)}, f32[8,768]{1,0:T(8,128)S(1)}) custom-call(s32[3]{0:T(128)S(1)} %pad_add_fusion.2.info_ref, f32[16,768]{1,0:T(8,128)S(1)} %get-tuple-element.263.vec_ref.shift_ref.gain_ref, f32[512,768]{1,0:T(8,128)S(1)} %get-tuple-element.332.grad_ref, bf16[512,768]{1,0:T(8,128)(2,1)S(1)} %get-tuple-element.354.refs_0_, ...), custom_call_target="tpu_custom_call" | custom-call | flops 1811939328 | bytes 11796480 | tf_op jit(solution)/shard_map/pallas_call | solution.py:73
  217.2 18.2 %collective-permute-done.35.received = bf16[4,144,768]{2,1,0:T(8,128)(2,1)S(1)} collective-permute-done((bf16[4,144,768]{2,1,0:T(8,128)(2,1)S(1)}, bf16[4,144,768]{2,1,0:T(8,128)(2,1)S(1)}, u32[]{:S(2)}, u32[]{:S(2)}) %collective-permute-start.35) | collective-permute-done | bytes 884768 | tf_op jit(solution)/shard_map/ppermute | solution.py:56
  243.1 2.4 collective-permute-start.41
  245.5 12.0 %shard_map.342 = (bf16[512,768]{1,0:T(8,128)(2,1)S(1)}, bf16[512,768]{1,0:T(8,128)(2,1)S(1)}, bf16[512,768]{1,0:T(8,128)(2,1)S(1)}, f32[8,768]{1,0:T(8,128)S(1)}...) custom-call(s32[3]{0:T(128)S(1)} %pad_add_fusion.2.info_ref, s32[4]{0:T(128)S(1)} %pad_add_fusion.4.counts_ref, ...), custom_call_target="tpu_custom_call" | custom-call | flops 4227858432 | bytes 14942208 | tf_op jit(solution)/shard_map/pallas_call | solution.py:73
  257.6 4.8 %collective-permute-done.41.far_b = bf16[144,768]{1,0:T(8,128)(2,1)S(1)} collective-permute-done((bf16[144,768]{1,0:T(8,128)(2,1)S(1)}, bf16[144,768]{1,0:T(8,128)(2,1)S(1)}, u32[]{:S(2)}, u32[]{:S(2)}) %collective-permute-start.41) | collective-permute-done | bytes 221216 | tf_op jit(solution)/shard_map/ppermute | solution.py:42
  267.0 3.2 collective-permute-start.46
  270.2 3.9 %shard_map.343 = (f32[256,768]{1,0:T(8,128)S(1)}, f32[256,768]{1,0:T(8,128)S(1)}, bf16[512,768]{1,0:T(8,128)(2,1)}) custom-call(s32[3]{0:T(128)S(1)} %pad_add_fusion.2.info_ref, f32[16,768]{1,0:T(8,128)S(1)} %get-tuple-element.263.vec_ref.shift_ref.gain_ref, f32[512,768]{1,0:T(8,128)S(1)} %get-tuple-element.372.grad_ref, ...), custom_call_target="tpu_custom_call" | custom-call | flops 1811939328 | bytes 11796480 | tf_op jit(solution)/shard_map/pallas_call | solution.py:73
  274.4 4.5 %collective-permute-done.45.far_a = bf16[96,768]{1,0:T(8,128)(2,1)S(1)} collective-permute-done((bf16[96,768]{1,0:T(8,128)(2,1)S(1)}, bf16[96,768]{1,0:T(8,128)(2,1)S(1)}, u32[]{:S(2)}, u32[]{:S(2)}) %collective-permute-start.45) | collective-permute-done | bytes 147488 | tf_op jit(solution)/shard_map/ppermute | solution.py:42
  281.6 2.8 collective-permute-start.48
  284.4 1.7 collective-permute-start.50
  286.7 3.6 %collective-permute-done.48.near_b = bf16[96,768]{1,0:T(8,128)(2,1)S(1)} collective-permute-done((bf16[96,768]{1,0:T(8,128)(2,1)S(1)}, bf16[96,768]{1,0:T(8,128)(2,1)S(1)}, u32[]{:S(2)}, u32[]{:S(2)}) %collective-permute-start.48) | collective-permute-done | bytes 147488 | tf_op jit(solution)/shard_map/ppermute | solution.py:42
  290.2 2.6 collective-permute-done.49.far_a
  292.8 5.1 %collective-permute-done.50.far_b = bf16[96,768]{1,0:T(8,128)(2,1)S(1)} collective-permute-done((bf16[96,768]{1,0:T(8,128)(2,1)S(1)}, bf16[96,768]{1,0:T(8,128)(2,1)S(1)}, u32[]{:S(2)}, u32[]{:S(2)}) %collective-permute-start.50) | collective-permute-done | bytes 147488 | tf_op jit(solution)/shard_map/ppermute | solution.py:42
  304.6 1.6 shard_map.351
  307.5 1.8 shard_map.353
  309.3 2.8 collective-permute-done.51.received
  313.4 2.8 collective-permute-start.55
  316.2 1.7 collective-permute-start.57
  320.4 1.6 shard_map.357
  322.6 3.0 collective-permute-done.56.far_a
  325.6 4.1 %collective-permute-done.57.far_b = bf16[112,768]{1,0:T(8,128)(2,1)S(1)} collective-permute-done((bf16[112,768]{1,0:T(8,128)(2,1)S(1)}, bf16[112,768]{1,0:T(8,128)(2,1)S(1)}, u32[]{:S(2)}, u32[]{:S(2)}) %collective-permute-start.57) | collective-permute-done | bytes 172064 | tf_op jit(solution)/shard_map/ppermute | solution.py:42
  335.6 1.6 shard_map.359
  (282 shorter events, 80.1 us)
Async XLA Ops:
  4.5 19.3 %collective-permute-start.1 = (bf16[112,768]{1,0:T(8,128)(2,1)S(1)}, bf16[112,768]{1,0:T(8,128)(2,1)S(1)}, u32[]{:S(2)}, u32[]{:S(2)}) collective-permute-start(bf16[112,768]{1,0:T(8,128)(2,1)S(1)} %get-tuple-element.492), channel_id=1, source_target_pairs={{0,16},{1,17},{2,18},{3,19},{4,20},{5,21},{6,22},{7,23},{8,24},{9,... | collective-permute-start | bytes 516104 | tf_op jit(solution)/shard_map/ppermute | solution.py:42
  8.6 15.2 %collective-permute-start = (bf16[112,768]{1,0:T(8,128)(2,1)S(1)}, bf16[112,768]{1,0:T(8,128)(2,1)S(1)}, u32[]{:S(2)}, u32[]{:S(2)}) collective-permute-start(bf16[112,768]{1,0:T(8,128)(2,1)S(1)} %get-tuple-element.492), channel_id=1, source_target_pairs={{0,8},{1,9},{2,10},{3,11},{4,12},{5,13},{6,14},{7,15},{8,0},{9,1},... | collective-permute-start | bytes 516104 | tf_op jit(solution)/shard_map/ppermute | solution.py:42
  10.2 13.6 %collective-permute-start.2 = (bf16[112,768]{1,0:T(8,128)(2,1)S(1)}, bf16[112,768]{1,0:T(8,128)(2,1)S(1)}, u32[]{:S(2)}, u32[]{:S(2)}) collective-permute-start(bf16[112,768]{1,0:T(8,128)(2,1)S(1)} %get-tuple-element.244.refs_0_), channel_id=1, source_target_pairs={{0,24},{1,25},{2,26},{3,27},{4,28},{5,29},{6,30},{7,31},{8,16},{9,... | collective-permute-start | bytes 516104 | tf_op jit(solution)/shard_map/ppermute | solution.py:42
  10.5 13.4 %collective-permute-start.3 = (bf16[96,768]{1,0:T(8,128)(2,1)S(1)}, bf16[96,768]{1,0:T(8,128)(2,1)S(1)}, u32[]{:S(2)}, u32[]{:S(2)}) collective-permute-start(bf16[96,768]{1,0:T(8,128)(2,1)S(1)} %get-tuple-element.495), channel_id=1, source_target_pairs={{0,8},{1,9},{2,10},{3,11},{4,12},{5,13},{6,14},{7,15},{8,0},{9,1},... | collective-permute-start | bytes 442376 | tf_op jit(solution)/shard_map/ppermute | solution.py:42
  24.4 21.7 %collective-permute-start.5 = (bf16[4,112,768]{2,1,0:T(8,128)(2,1)S(1)}, bf16[4,112,768]{2,1,0:T(8,128)(2,1)S(1)}, u32[]{:S(2)}, u32[]{:S(2)}) collective-permute-start(bf16[4,112,768]{2,1,0:T(8,128)(2,1)S(1)} %shard_map.314.mine), channel_id=1, source_target_pairs={{0,4},{1,3},{2,6},{3,1},{4,0},{5,7},{6,2},{7,5},{8,12},{9,11},{10,... | collective-permute-start | bytes 2064392 | tf_op jit(solution)/shard_map/ppermute | solution.py:56
  26.1 20.1 %collective-permute-start.4 = (bf16[4,112,768]{2,1,0:T(8,128)(2,1)S(1)}, bf16[4,112,768]{2,1,0:T(8,128)(2,1)S(1)}, u32[]{:S(2)}, u32[]{:S(2)}) collective-permute-start(bf16[4,112,768]{2,1,0:T(8,128)(2,1)S(1)} %shard_map.314.mine), channel_id=1, source_target_pairs={{0,2},{1,5},{2,0},{3,7},{4,6},{5,1},{6,4},{7,3},{8,10},{9,13},{10,... | collective-permute-start | bytes 2064392 | tf_op jit(solution)/shard_map/ppermute | solution.py:56
  27.6 18.6 %collective-permute-start.7 = (bf16[240,768]{1,0:T(8,128)(2,1)S(1)}, bf16[240,768]{1,0:T(8,128)(2,1)S(1)}, u32[]{:S(2)}, u32[]{:S(2)}) collective-permute-start(bf16[240,768]{1,0:T(8,128)(2,1)S(1)} %pad_maximum_fusion.3), channel_id=1, source_target_pairs={{0,8},{1,9},{2,10},{3,11},{4,12},{5,13},{6,14},{7,15},{8,0},{9,1},... | collective-permute-start | bytes 1105928 | tf_op jit(solution)/shard_map/ppermute | solution.py:42
  29.6 16.5 %collective-permute-start.6 = (bf16[2,96,768]{2,1,0:T(8,128)(2,1)S(1)}, bf16[2,96,768]{2,1,0:T(8,128)(2,1)S(1)}, u32[]{:S(2)}, u32[]{:S(2)}) collective-permute-start(bf16[2,96,768]{2,1,0:T(8,128)(2,1)S(1)} %shard_map.315.refs_0_), channel_id=1, source_target_pairs={{0,24},{1,25},{2,26},{3,27},{4,28},{5,29},{6,30},{7,31},{8,16},{9,... | collective-permute-start | bytes 884744 | tf_op jit(solution)/shard_map/ppermute | solution.py:42
  46.1 25.2 %collective-permute-start.12 = (bf16[528,768]{1,0:T(8,128)(2,1)S(1)}, bf16[528,768]{1,0:T(8,128)(2,1)S(1)}, u32[]{:S(2)}, u32[]{:S(2)}) collective-permute-start(bf16[528,768]{1,0:T(8,128)(2,1)S(1)} %fusion.1), channel_id=1, source_target_pairs={{0,8},{1,9},{2,10},{3,11},{4,12},{5,13},{6,14},{7,15},{8,0},{9,1},... | collective-permute-start | bytes 2433032 | tf_op jit(solution)/shard_map/ppermute | solution.py:42
  46.2 25.1 %collective-permute-start.8 = (bf16[4,112,768]{2,1,0:T(8,128)(2,1)S(1)}, bf16[4,112,768]{2,1,0:T(8,128)(2,1)S(1)}, u32[]{:S(2)}, u32[]{:S(2)}) collective-permute-start(bf16[4,112,768]{2,1,0:T(8,128)(2,1)S(1)} %collective-permute-done.4.first_away), channel_id=1, source_target_pairs={{0,4},{1,3},{2,6},{3,1},{4,0},{5,7},{6,2},{7,5},{8,12},{9,11},{10,... | collective-permute-start | bytes 2064392 | tf_op jit(solution)/shard_map/ppermute | solution.py:56
  47.4 23.9 %collective-permute-start.10 = (bf16[4,96,768]{2,1,0:T(8,128)(2,1)S(1)}, bf16[4,96,768]{2,1,0:T(8,128)(2,1)S(1)}, u32[]{:S(2)}, u32[]{:S(2)}) collective-permute-start(bf16[4,96,768]{2,1,0:T(8,128)(2,1)S(1)} %bitcast.98), channel_id=1, source_target_pairs={{0,4},{1,3},{2,6},{3,1},{4,0},{5,7},{6,2},{7,5},{8,12},{9,11},{10,... | collective-permute-start | bytes 1769480 | tf_op jit(solution)/shard_map/ppermute | solution.py:56
  49.0 22.3 %collective-permute-start.9 = (bf16[4,96,768]{2,1,0:T(8,128)(2,1)S(1)}, bf16[4,96,768]{2,1,0:T(8,128)(2,1)S(1)}, u32[]{:S(2)}, u32[]{:S(2)}) collective-permute-start(bf16[4,96,768]{2,1,0:T(8,128)(2,1)S(1)} %bitcast.99), channel_id=1, source_target_pairs={{0,2},{1,5},{2,0},{3,7},{4,6},{5,1},{6,4},{7,3},{8,10},{9,13},{10,... | collective-permute-start | bytes 1769480 | tf_op jit(solution)/shard_map/ppermute | solution.py:56
  50.1 21.2 %collective-permute-start.11 = (bf16[2,96,768]{2,1,0:T(8,128)(2,1)S(1)}, bf16[2,96,768]{2,1,0:T(8,128)(2,1)S(1)}, u32[]{:S(2)}, u32[]{:S(2)}) collective-permute-start(bf16[2,96,768]{2,1,0:T(8,128)(2,1)S(1)} %get-tuple-element.256.refs_0_), channel_id=1, source_target_pairs={{0,24},{1,25},{2,26},{3,27},{4,28},{5,29},{6,30},{7,31},{8,16},{9,... | collective-permute-start | bytes 884744 | tf_op jit(solution)/shard_map/ppermute | solution.py:42
  72.8 18.2 %collective-permute-start.16 = (bf16[4,96,768]{2,1,0:T(8,128)(2,1)S(1)}, bf16[4,96,768]{2,1,0:T(8,128)(2,1)S(1)}, u32[]{:S(2)}, u32[]{:S(2)}) collective-permute-start(bf16[4,96,768]{2,1,0:T(8,128)(2,1)S(1)} %bitcast.101), channel_id=1, source_target_pairs={{0,4},{1,3},{2,6},{3,1},{4,0},{5,7},{6,2},{7,5},{8,12},{9,11},{10,... | collective-permute-start | bytes 1769480 | tf_op jit(solution)/shard_map/ppermute | solution.py:56
  74.3 16.6 %collective-permute-start.15 = (bf16[4,96,768]{2,1,0:T(8,128)(2,1)S(1)}, bf16[4,96,768]{2,1,0:T(8,128)(2,1)S(1)}, u32[]{:S(2)}, u32[]{:S(2)}) collective-permute-start(bf16[4,96,768]{2,1,0:T(8,128)(2,1)S(1)} %bitcast.102), channel_id=1, source_target_pairs={{0,2},{1,5},{2,0},{3,7},{4,6},{5,1},{6,4},{7,3},{8,10},{9,13},{10,... | collective-permute-start | bytes 1769480 | tf_op jit(solution)/shard_map/ppermute | solution.py:56
  74.7 20.2 %collective-permute-start.14 = (bf16[4,96,768]{2,1,0:T(8,128)(2,1)S(1)}, bf16[4,96,768]{2,1,0:T(8,128)(2,1)S(1)}, u32[]{:S(2)}, u32[]{:S(2)}) collective-permute-start(bf16[4,96,768]{2,1,0:T(8,128)(2,1)S(1)} %collective-permute-done.9.first_away), channel_id=1, source_target_pairs={{0,4},{1,3},{2,6},{3,1},{4,0},{5,7},{6,2},{7,5},{8,12},{9,11},{10,... | collective-permute-start | bytes 1769480 | tf_op jit(solution)/shard_map/ppermute | solution.py:56
  76.2 14.8 %collective-permute-start.17 = (bf16[2,144,768]{2,1,0:T(8,128)(2,1)S(1)}, bf16[2,144,768]{2,1,0:T(8,128)(2,1)S(1)}, u32[]{:S(2)}, u32[]{:S(2)}) collective-permute-start(bf16[2,144,768]{2,1,0:T(8,128)(2,1)S(1)} %get-tuple-element.272.refs_0_), channel_id=1, source_target_pairs={{0,24},{1,25},{2,26},{3,27},{4,28},{5,29},{6,30},{7,31},{8,16},{9,... | collective-permute-start | bytes 1327112 | tf_op jit(solution)/shard_map/ppermute | solution.py:42
  96.4 28.9 %collective-permute-start.21 = (bf16[4,144,768]{2,1,0:T(8,128)(2,1)S(1)}, bf16[4,144,768]{2,1,0:T(8,128)(2,1)S(1)}, u32[]{:S(2)}, u32[]{:S(2)}) collective-permute-start(bf16[4,144,768]{2,1,0:T(8,128)(2,1)S(1)} %bitcast.95), channel_id=1, source_target_pairs={{0,4},{1,3},{2,6},{3,1},{4,0},{5,7},{6,2},{7,5},{8,12},{9,11},{10,... | collective-permute-start | bytes 2654216 | tf_op jit(solution)/shard_map/ppermute | solution.py:56
  98.0 27.3 %collective-permute-start.20 = (bf16[4,144,768]{2,1,0:T(8,128)(2,1)S(1)}, bf16[4,144,768]{2,1,0:T(8,128)(2,1)S(1)}, u32[]{:S(2)}, u32[]{:S(2)}) collective-permute-start(bf16[4,144,768]{2,1,0:T(8,128)(2,1)S(1)} %bitcast.96), channel_id=1, source_target_pairs={{0,2},{1,5},{2,0},{3,7},{4,6},{5,1},{6,4},{7,3},{8,10},{9,13},{10,... | collective-permute-start | bytes 2654216 | tf_op jit(solution)/shard_map/ppermute | solution.py:56
  98.8 26.6 %collective-permute-start.19 = (bf16[4,96,768]{2,1,0:T(8,128)(2,1)S(1)}, bf16[4,96,768]{2,1,0:T(8,128)(2,1)S(1)}, u32[]{:S(2)}, u32[]{:S(2)}) collective-permute-start(bf16[4,96,768]{2,1,0:T(8,128)(2,1)S(1)} %collective-permute-done.15.first_away), channel_id=1, source_target_pairs={{0,4},{1,3},{2,6},{3,1},{4,0},{5,7},{6,2},{7,5},{8,12},{9,11},{10,... | collective-permute-start | bytes 1769480 | tf_op jit(solution)/shard_map/ppermute | solution.py:56
  126.8 13.7 %collective-permute-start.24 = (bf16[4,2,144,768]{3,2,1,0:T(8,128)(2,1)S(1)}, bf16[4,2,144,768]{3,2,1,0:T(8,128)(2,1)S(1)}, u32[]{:S(2)}, u32[]{:S(2)}) collective-permute-start(bf16[4,2,144,768]{3,2,1,0:T(8,128)(2,1)S(1)} %shard_map.327.refs_0_), channel_id=1, source_target_pairs={{0,1},{1,0},{2,3},{3,2},{4,5},{5,4},{6,7},{7,6},{8,9},{9,8},{10,11... | collective-permute-start | bytes 5308424 | tf_op jit(solution)/shard_map/ppermute | solution.py:48
  127.4 11.7 %collective-permute-start.25 = (bf16[4,144,768]{2,1,0:T(8,128)(2,1)S(1)}, bf16[4,144,768]{2,1,0:T(8,128)(2,1)S(1)}, u32[]{:S(2)}, u32[]{:S(2)}) collective-permute-start(bf16[4,144,768]{2,1,0:T(8,128)(2,1)S(1)} %collective-permute-done.21.refs_1_), channel_id=1, source_target_pairs={{0,1},{1,0},{2,3},{3,2},{4,5},{5,4},{6,7},{7,6},{8,9},{9,8},{10,11... | collective-permute-start | bytes 2654216 | tf_op jit(solution)/shard_map/ppermute | solution.py:48
  127.5 13.0 %collective-permute-start.23 = (bf16[4,144,768]{2,1,0:T(8,128)(2,1)S(1)}, bf16[4,144,768]{2,1,0:T(8,128)(2,1)S(1)}, u32[]{:S(2)}, u32[]{:S(2)}) collective-permute-start(bf16[4,144,768]{2,1,0:T(8,128)(2,1)S(1)} %collective-permute-done.20.other), channel_id=1, source_target_pairs={{0,4},{1,3},{2,6},{3,1},{4,0},{5,7},{6,2},{7,5},{8,12},{9,11},{10,... | collective-permute-start | bytes 2654216 | tf_op jit(solution)/shard_map/ppermute | solution.py:56
  147.4 11.7 %collective-permute-start.27 = (bf16[256,768]{1,0:T(8,128)(2,1)S(1)}, bf16[256,768]{1,0:T(8,128)(2,1)S(1)}, u32[]{:S(2)}, u32[]{:S(2)}) collective-permute-start(bf16[256,768]{1,0:T(8,128)(2,1)S(1)} %get-tuple-element.303), channel_id=1, source_target_pairs={{0,8},{1,9},{2,10},{3,11},{4,12},{5,13},{6,14},{7,15},{8,0},{9,1},... | collective-permute-start | bytes 1179656 | tf_op jit(solution)/shard_map/ppermute | solution.py:42
  163.8 11.5 %collective-permute-start.29 = (bf16[256,768]{1,0:T(8,128)(2,1)S(1)}, bf16[256,768]{1,0:T(8,128)(2,1)S(1)}, u32[]{:S(2)}, u32[]{:S(2)}) collective-permute-start(bf16[256,768]{1,0:T(8,128)(2,1)S(1)} %get-tuple-element.308), channel_id=1, source_target_pairs={{0,8},{1,9},{2,10},{3,11},{4,12},{5,13},{6,14},{7,15},{8,0},{9,1},... | collective-permute-start | bytes 1179656 | tf_op jit(solution)/shard_map/ppermute | solution.py:42
  167.5 13.8 %collective-permute-start.30 = (bf16[4,2,48,768]{3,2,1,0:T(8,128)(2,1)S(1)}, bf16[4,2,48,768]{3,2,1,0:T(8,128)(2,1)S(1)}, u32[]{:S(2)}, u32[]{:S(2)}) collective-permute-start(bf16[4,2,48,768]{3,2,1,0:T(8,128)(2,1)S(1)} %get-tuple-element.310), channel_id=1, source_target_pairs={{0,4},{1,3},{2,6},{3,1},{4,0},{5,7},{6,2},{7,5},{8,12},{9,11},{10,... | collective-permute-start | bytes 1769480 | tf_op jit(solution)/shard_map/ppermute | solution.py:56
  192.1 17.0 %collective-permute-start.32 = (bf16[4,2,96,768]{3,2,1,0:T(8,128)(2,1)}, bf16[4,2,96,768]{3,2,1,0:T(8,128)(2,1)S(1)}, u32[]{:S(2)}, u32[]{:S(2)}) collective-permute-start(bf16[4,2,96,768]{3,2,1,0:T(8,128)(2,1)} %get-tuple-element.326), channel_id=1, source_target_pairs={{0,4},{1,3},{2,6},{3,1},{4,0},{5,7},{6,2},{7,5},{8,12},{9,11},{10,... | collective-permute-start | bytes 3538952 | tf_op jit(solution)/shard_map/ppermute | solution.py:56
  209.2 27.0 %collective-permute-start.36 = (bf16[2,16,48,768]{3,2,1,0:T(8,128)(2,1)S(1)}, bf16[2,16,48,768]{3,2,1,0:T(8,128)(2,1)S(1)}, u32[]{:S(2)}, u32[]{:S(2)}) collective-permute-start(bf16[2,16,48,768]{3,2,1,0:T(8,128)(2,1)S(1)} %bitcast.116), channel_id=1, source_target_pairs={{0,1},{1,0},{2,3},{3,2},{4,5},{5,4},{6,7},{7,6},{8,9},{9,8},{10,11... | collective-permute-start | bytes 7077896 | tf_op jit(solution)/shard_map/ppermute | solution.py:48
  210.4 25.7 %collective-permute-start.34 = (bf16[4,2,96,768]{3,2,1,0:T(8,128)(2,1)S(1)}, bf16[4,2,96,768]{3,2,1,0:T(8,128)(2,1)S(1)}, u32[]{:S(2)}, u32[]{:S(2)}) collective-permute-start(bf16[4,2,96,768]{3,2,1,0:T(8,128)(2,1)S(1)} %get-tuple-element.346), channel_id=1, source_target_pairs={{0,4},{1,3},{2,6},{3,1},{4,0},{5,7},{6,2},{7,5},{8,12},{9,11},{10,... | collective-permute-start | bytes 3538952 | tf_op jit(solution)/shard_map/ppermute | solution.py:56
  212.7 22.7 %collective-permute-start.35 = (bf16[4,144,768]{2,1,0:T(8,128)(2,1)S(1)}, bf16[4,144,768]{2,1,0:T(8,128)(2,1)S(1)}, u32[]{:S(2)}, u32[]{:S(2)}) collective-permute-start(bf16[4,144,768]{2,1,0:T(8,128)(2,1)S(1)} %get-tuple-element.352), channel_id=1, source_target_pairs={{0,2},{1,5},{2,0},{3,7},{4,6},{5,1},{6,4},{7,3},{8,10},{9,13},{10,... | collective-permute-start | bytes 2654216 | tf_op jit(solution)/shard_map/ppermute | solution.py:56
  237.3 25.1 %collective-permute-start.37 = (bf16[4,2,96,768]{3,2,1,0:T(8,128)(2,1)S(1)}, bf16[4,2,96,768]{3,2,1,0:T(8,128)(2,1)S(1)}, u32[]{:S(2)}, u32[]{:S(2)}) collective-permute-start(bf16[4,2,96,768]{3,2,1,0:T(8,128)(2,1)S(1)} %get-tuple-element.361), channel_id=1, source_target_pairs={{0,4},{1,3},{2,6},{3,1},{4,0},{5,7},{6,2},{7,5},{8,12},{9,11},{10,... | collective-permute-start | bytes 3538952 | tf_op jit(solution)/shard_map/ppermute | solution.py:56
  239.4 23.0 %collective-permute-start.38 = (bf16[4,96,768]{2,1,0:T(8,128)(2,1)S(1)}, bf16[4,96,768]{2,1,0:T(8,128)(2,1)S(1)}, u32[]{:S(2)}, u32[]{:S(2)}) collective-permute-start(bf16[4,96,768]{2,1,0:T(8,128)(2,1)S(1)} %get-tuple-element.365), channel_id=1, source_target_pairs={{0,2},{1,5},{2,0},{3,7},{4,6},{5,1},{6,4},{7,3},{8,10},{9,13},{10,... | collective-permute-start | bytes 1769480 | tf_op jit(solution)/shard_map/ppermute | solution.py:56
  241.0 16.6 %collective-permute-start.39 = (bf16[144,768]{1,0:T(8,128)(2,1)S(1)}, bf16[144,768]{1,0:T(8,128)(2,1)S(1)}, u32[]{:S(2)}, u32[]{:S(2)}) collective-permute-start(bf16[144,768]{1,0:T(8,128)(2,1)S(1)} %get-tuple-element.369), channel_id=1, source_target_pairs={{0,24},{1,25},{2,26},{3,27},{4,28},{5,29},{6,30},{7,31},{8,16},{9,... | collective-permute-start | bytes 663560 | tf_op jit(solution)/shard_map/ppermute | solution.py:42
  242.3 15.3 %collective-permute-start.40 = (bf16[144,768]{1,0:T(8,128)(2,1)S(1)}, bf16[144,768]{1,0:T(8,128)(2,1)S(1)}, u32[]{:S(2)}, u32[]{:S(2)}) collective-permute-start(bf16[144,768]{1,0:T(8,128)(2,1)S(1)} %get-tuple-element.370), channel_id=1, source_target_pairs={{0,8},{1,9},{2,10},{3,11},{4,12},{5,13},{6,14},{7,15},{8,0},{9,1},... | collective-permute-start | bytes 663560 | tf_op jit(solution)/shard_map/ppermute | solution.py:42
  243.1 19.3 %collective-permute-start.41 = (bf16[144,768]{1,0:T(8,128)(2,1)S(1)}, bf16[144,768]{1,0:T(8,128)(2,1)S(1)}, u32[]{:S(2)}, u32[]{:S(2)}) collective-permute-start(bf16[144,768]{1,0:T(8,128)(2,1)S(1)} %get-tuple-element.371), channel_id=1, source_target_pairs={{0,16},{1,17},{2,18},{3,19},{4,20},{5,21},{6,22},{7,23},{8,24},{9,... | collective-permute-start | bytes 663560 | tf_op jit(solution)/shard_map/ppermute | solution.py:42
  262.4 16.5 %collective-permute-start.42 = (bf16[2,16,48,768]{3,2,1,0:T(8,128)(2,1)S(1)}, bf16[2,16,48,768]{3,2,1,0:T(8,128)(2,1)S(1)}, u32[]{:S(2)}, u32[]{:S(2)}) collective-permute-start(bf16[2,16,48,768]{3,2,1,0:T(8,128)(2,1)S(1)} %bitcast.115), channel_id=1, source_target_pairs={{0,1},{1,0},{2,3},{3,2},{4,5},{5,4},{6,7},{7,6},{8,9},{9,8},{10,11... | collective-permute-start | bytes 7077896 | tf_op jit(solution)/shard_map/ppermute | solution.py:48
  263.3 15.6 %collective-permute-start.43 = (bf16[4,96,768]{2,1,0:T(8,128)(2,1)S(1)}, bf16[4,96,768]{2,1,0:T(8,128)(2,1)S(1)}, u32[]{:S(2)}, u32[]{:S(2)}) collective-permute-start(bf16[4,96,768]{2,1,0:T(8,128)(2,1)S(1)} %get-tuple-element.391), channel_id=1, source_target_pairs={{0,2},{1,5},{2,0},{3,7},{4,6},{5,1},{6,4},{7,3},{8,10},{9,13},{10,... | collective-permute-start | bytes 1769480 | tf_op jit(solution)/shard_map/ppermute | solution.py:56
  265.7 8.7 %collective-permute-start.44 = (bf16[96,768]{1,0:T(8,128)(2,1)S(1)}, bf16[96,768]{1,0:T(8,128)(2,1)S(1)}, u32[]{:S(2)}, u32[]{:S(2)}) collective-permute-start(bf16[96,768]{1,0:T(8,128)(2,1)S(1)} %get-tuple-element.395), channel_id=1, source_target_pairs={{0,24},{1,25},{2,26},{3,27},{4,28},{5,29},{6,30},{7,31},{8,16},{9,... | collective-permute-start | bytes 442376 | tf_op jit(solution)/shard_map/ppermute | solution.py:42
  267.0 11.9 %collective-permute-start.45 = (bf16[96,768]{1,0:T(8,128)(2,1)S(1)}, bf16[96,768]{1,0:T(8,128)(2,1)S(1)}, u32[]{:S(2)}, u32[]{:S(2)}) collective-permute-start(bf16[96,768]{1,0:T(8,128)(2,1)S(1)} %get-tuple-element.396), channel_id=1, source_target_pairs={{0,8},{1,9},{2,10},{3,11},{4,12},{5,13},{6,14},{7,15},{8,0},{9,1},... | collective-permute-start | bytes 442376 | tf_op jit(solution)/shard_map/ppermute | solution.py:42
  267.0 11.9 %collective-permute-start.46 = (bf16[96,768]{1,0:T(8,128)(2,1)S(1)}, bf16[96,768]{1,0:T(8,128)(2,1)S(1)}, u32[]{:S(2)}, u32[]{:S(2)}) collective-permute-start(bf16[96,768]{1,0:T(8,128)(2,1)S(1)} %get-tuple-element.397), channel_id=1, source_target_pairs={{0,16},{1,17},{2,18},{3,19},{4,20},{5,21},{6,22},{7,23},{8,24},{9,... | collective-permute-start | bytes 442376 | tf_op jit(solution)/shard_map/ppermute | solution.py:42
  280.0 18.4 %collective-permute-start.47 = (bf16[4,2,112,768]{3,2,1,0:T(8,128)(2,1)S(1)}, bf16[4,2,112,768]{3,2,1,0:T(8,128)(2,1)S(1)}, u32[]{:S(2)}, u32[]{:S(2)}) collective-permute-start(bf16[4,2,112,768]{3,2,1,0:T(8,128)(2,1)S(1)} %get-tuple-element.408), channel_id=1, source_target_pairs={{0,4},{1,3},{2,6},{3,1},{4,0},{5,7},{6,2},{7,5},{8,12},{9,11},{10,... | collective-permute-start | bytes 4128776 | tf_op jit(solution)/shard_map/ppermute | solution.py:56
  281.6 8.6 %collective-permute-start.48 = (bf16[96,768]{1,0:T(8,128)(2,1)S(1)}, bf16[96,768]{1,0:T(8,128)(2,1)S(1)}, u32[]{:S(2)}, u32[]{:S(2)}) collective-permute-start(bf16[96,768]{1,0:T(8,128)(2,1)S(1)} %get-tuple-element.412), channel_id=1, source_target_pairs={{0,24},{1,25},{2,26},{3,27},{4,28},{5,29},{6,30},{7,31},{8,16},{9,... | collective-permute-start | bytes 442376 | tf_op jit(solution)/shard_map/ppermute | solution.py:42
  284.4 13.6 %collective-permute-start.50 = (bf16[96,768]{1,0:T(8,128)(2,1)S(1)}, bf16[96,768]{1,0:T(8,128)(2,1)S(1)}, u32[]{:S(2)}, u32[]{:S(2)}) collective-permute-start(bf16[96,768]{1,0:T(8,128)(2,1)S(1)} %get-tuple-element.414), channel_id=1, source_target_pairs={{0,16},{1,17},{2,18},{3,19},{4,20},{5,21},{6,22},{7,23},{8,24},{9,... | collective-permute-start | bytes 442376 | tf_op jit(solution)/shard_map/ppermute | solution.py:42
  286.1 27.3 %collective-permute-start.54 = (bf16[512,768]{1,0:T(8,128)(2,1)}, bf16[512,768]{1,0:T(8,128)(2,1)}, u32[]{:S(2)}, u32[]{:S(2)}) collective-permute-start(bf16[512,768]{1,0:T(8,128)(2,1)} %get-tuple-element.444), channel_id=1, source_target_pairs={{0,8},{1,9},{2,10},{3,11},{4,12},{5,13},{6,14},{7,15},{8,0},{9,1},... | collective-permute-start | bytes 2359304 | tf_op jit(solution)/shard_map/ppermute | solution.py:42
  300.9 11.3 %collective-permute-start.51 = (bf16[4,112,768]{2,1,0:T(8,128)(2,1)}, bf16[4,112,768]{2,1,0:T(8,128)(2,1)}, u32[]{:S(2)}, u32[]{:S(2)}) collective-permute-start(bf16[4,112,768]{2,1,0:T(8,128)(2,1)} %get-tuple-element.431), channel_id=1, source_target_pairs={{0,2},{1,5},{2,0},{3,7},{4,6},{5,1},{6,4},{7,3},{8,10},{9,13},{10,... | collective-permute-start | bytes 2064392 | tf_op jit(solution)/shard_map/ppermute | solution.py:56
  313.4 9.2 %collective-permute-start.55 = (bf16[112,768]{1,0:T(8,128)(2,1)S(1)}, bf16[112,768]{1,0:T(8,128)(2,1)S(1)}, u32[]{:S(2)}, u32[]{:S(2)}) collective-permute-start(bf16[112,768]{1,0:T(8,128)(2,1)S(1)} %get-tuple-element.446), channel_id=1, source_target_pairs={{0,24},{1,25},{2,26},{3,27},{4,28},{5,29},{6,30},{7,31},{8,16},{9,... | collective-permute-start | bytes 516104 | tf_op jit(solution)/shard_map/ppermute | solution.py:42
  316.2 9.4 %collective-permute-start.56 = (bf16[112,768]{1,0:T(8,128)(2,1)S(1)}, bf16[112,768]{1,0:T(8,128)(2,1)S(1)}, u32[]{:S(2)}, u32[]{:S(2)}) collective-permute-start(bf16[112,768]{1,0:T(8,128)(2,1)S(1)} %get-tuple-element.447), channel_id=1, source_target_pairs={{0,8},{1,9},{2,10},{3,11},{4,12},{5,13},{6,14},{7,15},{8,0},{9,1},... | collective-permute-start | bytes 516104 | tf_op jit(solution)/shard_map/ppermute | solution.py:42
  316.2 13.5 %collective-permute-start.57 = (bf16[112,768]{1,0:T(8,128)(2,1)S(1)}, bf16[112,768]{1,0:T(8,128)(2,1)S(1)}, u32[]{:S(2)}, u32[]{:S(2)}) collective-permute-start(bf16[112,768]{1,0:T(8,128)(2,1)S(1)} %get-tuple-element.448), channel_id=1, source_target_pairs={{0,16},{1,17},{2,18},{3,19},{4,20},{5,21},{6,22},{7,23},{8,24},{9,... | collective-permute-start | bytes 516104 | tf_op jit(solution)/shard_map/ppermute | solution.py:42
  (74 other events, 563.9 us)
